TPU v7x, 512 devices: a whole 4x8x8 slice. The times are simulated.
512 devices in a mesh: dp: 64 (over x, y, core), tensor: 8 (over z).
Axes of the slice: x: 4, y: 8, z: 8, core: 2. Of those that a mesh axis runs over, the one named last changes fastest.
Arguments:
- tokens: bfloat16 [8192, 16384], P('dp', 'tensor'), may hold values from -60 to 60
- cotangent: bfloat16 [8192, 16384], P('dp', 'tensor'), may hold values from -16 to 16
- prompt_len: int32 [64], P('dp'), may hold values from 1 to 64
- resp_len: int32 [64], P('dp'), may hold values from 1 to 64
- ranks: int32 [64], P('dp'), may hold values from 0 to 7, as said below
- factors: float32 [8, 2048, 128], P('tensor', 'dp'), may hold values from -6 to 6
- first_moment: float32 [8, 2048, 128], P('tensor', 'dp'), may hold values from -8.286408e-05 to 8.286408e-05
- second_moment: float32 [8, 2048, 128], P('tensor', 'dp'), may hold values from 4.7683715e-12 to 9.536744e-10
- base_weight: bfloat16 [16384, 16384], P('dp', 'tensor'), may hold values from -0.046875 to 0.046875
- gain: float32 [16384], P('tensor'), may hold values from 0.5 to 1.5
- state: bfloat16 [16, 16384], P(None, 'tensor'), may hold values from -6 to 6
Outputs:
- new_factors: float32 [8, 2048, 128], P('tensor', 'dp')
- decoded: bfloat16 [16, 16384], P(None, 'tensor')
Inputs may be any that keep to these rules, and one draw needn't show every extreme that they name: `ranks`: each aligned group of 8 consecutive sequences holds every rank once.
All inputs are finite; a program needn't handle non-finite values.
Results may differ from a plain program's by a relative error of at most 0.0065.
Values may be sent and summed in bfloat16 or wider, within the bound.
No kernel may reach another device: no remote copies, remote signals or barrier semaphores. Data moves between devices by JAX's collectives and lax.ppermute only.
A program may use at most 64 MiB of HBM per device.

v0:
```python
import math

import jax
import jax.numpy as jnp
from jax import lax
from jax.sharding import PartitionSpec as P

MODEL_WIDTH = 16384
SEQLEN = 128
GROUP = 8
DECODE_STEPS = 4


adapter_alpha = 2.0
beta_one = 0.9
beta_two = 0.999
rate = 0.1
clip_norm = 1.0
adam_count = 200.0


def body(
    tokens,
    cotangent,
    prompt_len,
    resp_len,
    ranks,
    factors,
    first_moment,
    second_moment,
    base_weight,
    gain,
    state,
):
    rank_number = factors.shape[2] // 2
    share_count = factors.shape[1]
    adapter_scale = adapter_alpha / (rank_number * math.sqrt(MODEL_WIDTH))
    positions = jnp.arange(SEQLEN, dtype=jnp.int32)
    lower = prompt_len[:, None]
    upper = lower + resp_len[:, None]
    inside = (positions[None, :] >= lower) & (positions[None, :] < upper)
    advantage = (2 * ranks - (GROUP - 1)).astype(jnp.float32) / (GROUP - 1)
    per_seq = advantage / resp_len.astype(jnp.float32)
    weight = jnp.where(inside, per_seq[:, None], jnp.float32(0.0)).reshape(-1)
    weighted = (cotangent.astype(jnp.float32) * weight[:, None]).astype(jnp.bfloat16)
    local_low = lax.all_gather(factors.astype(jnp.bfloat16), "dp", axis=1, tiled=True)[0]
    hidden_part = jnp.dot(tokens, local_low[:, :rank_number], preferred_element_type=jnp.float32)
    proj_part = jnp.dot(weighted, local_low[:, rank_number:], preferred_element_type=jnp.float32)
    hidden_sum, proj_sum = lax.psum((hidden_part, proj_part), "tensor")
    hidden_low = hidden_sum.astype(jnp.bfloat16)
    proj_low = proj_sum.astype(jnp.bfloat16)
    dims = (((0,), (0,)), ((), ()))
    grad_down = lax.dot_general(tokens, proj_low, dims, preferred_element_type=jnp.float32)
    grad_up = lax.dot_general(weighted, hidden_low, dims, preferred_element_type=jnp.float32)
    share_pieces = lax.psum_scatter(
        adapter_scale * jnp.concatenate([grad_down, grad_up], axis=1),
        "dp",
        scatter_dimension=0,
        tiled=True,
    )
    squared = lax.psum(jnp.sum(share_pieces * share_pieces), ("dp", "tensor"))
    clip = jnp.minimum(jnp.float32(1.0), clip_norm / (jnp.sqrt(squared) + 1e-06))
    grads = clip * share_pieces
    moment_one = beta_one * first_moment[0] + (1.0 - beta_one) * grads
    moment_two = beta_two * second_moment[0] + (1.0 - beta_two) * grads * grads
    step_size = (
        moment_one
        / (1.0 - beta_one**adam_count)
        / (jnp.sqrt(moment_two / (1.0 - beta_two**adam_count)) + 1e-08)
    )
    updated = factors[0] - rate * step_size
    new_factors = updated[None]
    block_rows = lax.all_gather(new_factors, "dp", axis=1, tiled=True)[0]
    dp_index = lax.axis_index("dp")
    tp_index = lax.axis_index("tensor")
    dp_count = lax.axis_size("dp")
    tp_count = lax.axis_size("tensor")
    tile_rows = base_weight.shape[0]
    tile_cols = base_weight.shape[1]
    down_all = lax.all_gather(updated[None, :, :rank_number], ("dp", "tensor"), axis=0, tiled=True)
    down_all = (
        down_all.reshape(dp_count, tp_count, share_count, rank_number)
        .transpose(1, 0, 2, 3)
        .reshape(-1, rank_number)
    )
    down_tile = lax.dynamic_slice_in_dim(down_all, dp_index * tile_rows, tile_rows, 0)
    merged = base_weight.astype(jnp.float32) + adapter_scale * jnp.dot(
        down_tile, block_rows[:, rank_number:].T, precision=lax.Precision.HIGHEST
    )
    full_state = lax.all_gather(state, "tensor", axis=1, tiled=True)
    result = state
    for step in range(DECODE_STEPS):
        rows_in = lax.dynamic_slice_in_dim(full_state, dp_index * tile_rows, tile_rows, 1)
        value_portion = jnp.dot(
            rows_in.astype(jnp.float32), merged, precision=lax.Precision.HIGHEST
        )
        summed = lax.psum(value_portion, "dp")
        before = lax.dynamic_slice_in_dim(full_state, tp_index * tile_cols, tile_cols, 1).astype(
            jnp.float32
        )
        resid = before + summed
        total = lax.psum(jnp.sum(resid * resid, axis=1), "tensor")
        result = (resid * lax.rsqrt(total / MODEL_WIDTH + 1e-05)[:, None] * gain[None, :]).astype(
            jnp.bfloat16
        )
        if step + 1 < DECODE_STEPS:
            full_state = lax.all_gather(result, "tensor", axis=1, tiled=True)
    return (new_factors, result)


def solution(mesh):
    return jax.shard_map(
        body,
        mesh=mesh,
        in_specs=(
            P("dp", "tensor"),
            P("dp", "tensor"),
            P("dp"),
            P("dp"),
            P("dp"),
            P("tensor", "dp", None),
            P("tensor", "dp", None),
            P("tensor", "dp", None),
            P("dp", "tensor"),
            P("tensor"),
            P(None, "tensor"),
        ),
        out_specs=(P("tensor", "dp", None), P(None, "tensor")),
        check_vma=False,
    )
```

profile of v0, /device:TPU:1, one launch (start us, length us, event | category | flops | bytes accessed | tf_op | source)
XLA Modules:
  0.0 1439.6 jit_solution(8001388234104789584)
XLA Ops:
  10.0 53.7 %all_gather.21 = bf16[1,2048,128]{2,1,0:T(8,128)(2,1)S(1)} all-gather(bf16[1,32,128]{2,1,0:T(8,128)(2,1)S(1)} %convert_element_type.56), channel_id=1, replica_groups=mesh['dp'=64,'tensor'=8] {'dp'}, dimensions={1}, use_global_device_ids=true | all-gather | bytes 532480 | tf_op jit(solution)/shard_map/all_gather | solution.py:46
  64.1 1.7 fusion.4
  65.8 28.2 %all-reduce = (bf16[128,64]{0,1:T(8,128)(2,1)S(1)}, bf16[128,64]{0,1:T(8,128)(2,1)S(1)}) all-reduce(f32[128,64]{0,1:T(8,128)S(1)} %fusion.2, f32[128,64]{0,1:T(8,128)S(1)} %fusion.4), channel_id=1, replica_groups=mesh['dp'=64,'tensor'=8] {'tensor'}, use_global_device_ids=true, to_apply=%region_1.2 | all-reduce | flops 16384 | bytes 98304 | tf_op jit(solution)/shard_map/psum | solution.py:49
  94.7 1.3 copy.30
  96.3 142.4 %reduce-scatter.4.cloned.1.call-done = f32[32,128]{1,0:T(8,128)} async-done(((f32[2048,128]{1,0:T(8,128)}), f32[32,128]{1,0:T(8,128)}) %reduce-scatter.4.cloned.1.call-update) | async-done | bytes 16400
  240.2 102.2 %psum.79 = f32[]{:T(128)} all-reduce(f32[]{:T(128)} %multiply_reduce_fusion.4), channel_id=1, replica_groups=mesh['dp'=64,'tensor'=8] {'dp','tensor'}, use_global_device_ids=true, to_apply=%region_4.5 | all-reduce | flops 1 | bytes 8 | tf_op jit(solution)/shard_map/psum | solution.py:61
  344.8 19.8 %all_gather.22 = bf16[16,16384]{1,0:T(8,128)(2,1)S(1)} all-gather(bf16[16,2048]{1,0:T(8,128)(2,1)S(1)} %copy-done.3), channel_id=1, replica_groups=mesh['dp'=64,'tensor'=8] {'tensor'}, dimensions={1}, use_global_device_ids=true | all-gather | bytes 589824 | tf_op jit(solution)/shard_map/all_gather | solution.py:90
  364.6 103.9 %all-gather.5.cloned.1.call-done = f32[16384,64]{1,0:T(8,128)} async-done(((f32[32,64]{1,0:T(8,128)}), f32[16384,64]{1,0:T(8,128)}) %all-gather.5.cloned.1.call-update) | async-done | bytes 4194320 | tf_op jit(solution)/shard_map/all_gather | solution.py:80
  468.4 8.0 copy.27
  476.4 73.3 %all-gather.7.cloned.1.call-done = f32[2048,128]{1,0:T(8,128)} async-done(((f32[32,128]{1,0:T(8,128)}), f32[2048,128]{1,0:T(8,128)}) %all-gather.7.cloned.1.call-update) | async-done | bytes 1048592 | tf_op jit(solution)/shard_map/all_gather | solution.py:73
  549.7 3.6 fusion
  553.4 1.5 fusion.23
  554.9 182.2 %all-reduce.6.cloned.1.call-done = f32[16,2048]{1,0:T(8,128)} async-done(((f32[16,2048]{1,0:T(8,128)}), f32[16,2048]{1,0:T(8,128)}) %all-reduce.6.cloned.1.call-update) | async-done | bytes 131088 | tf_op jit(solution)/shard_map/psum | solution.py:97
  737.1 1.0 multiply_reduce_fusion.3
  738.2 14.3 psum.81
  752.5 1.0 multiply_convert_fusion.6
  753.5 20.2 %all_gather.25 = bf16[16,16384]{1,0:T(8,128)(2,1)S(1)} all-gather(bf16[16,2048]{1,0:T(8,128)(2,1)S(1)} %multiply_convert_fusion.6), channel_id=1, replica_groups=mesh['dp'=64,'tensor'=8] {'tensor'}, dimensions={1}, use_global_device_ids=true | all-gather | bytes 589824 | tf_op jit(solution)/shard_map/all_gather | solution.py:107
  773.7 1.5 fusion.21
  775.3 188.0 %all-reduce.8.cloned.1.call-done = f32[16,2048]{1,0:T(8,128)} async-done(((f32[16,2048]{1,0:T(8,128)}), f32[16,2048]{1,0:T(8,128)}) %all-reduce.8.cloned.1.call-update) | async-done | bytes 131088 | tf_op jit(solution)/shard_map/psum | solution.py:97
  963.3 1.0 multiply_reduce_fusion.2
  964.3 14.3 psum.83
  979.7 20.4 %all_gather.26 = bf16[16,16384]{1,0:T(8,128)(2,1)S(1)} all-gather(bf16[16,2048]{1,0:T(8,128)(2,1)S(1)} %multiply_convert_fusion.5), channel_id=1, replica_groups=mesh['dp'=64,'tensor'=8] {'tensor'}, dimensions={1}, use_global_device_ids=true | all-gather | bytes 589824 | tf_op jit(solution)/shard_map/all_gather | solution.py:107
  1000.0 1.5 fusion.19
  1001.6 188.0 %all-reduce.10.cloned.1.call-done = f32[16,2048]{1,0:T(8,128)} async-done(((f32[16,2048]{1,0:T(8,128)}), f32[16,2048]{1,0:T(8,128)}) %all-reduce.10.cloned.1.call-update) | async-done | bytes 131088 | tf_op jit(solution)/shard_map/psum | solution.py:97
  1189.6 1.0 multiply_reduce_fusion.1
  1190.6 14.3 psum.85
  1206.0 20.2 %all_gather.27 = bf16[16,16384]{1,0:T(8,128)(2,1)S(1)} all-gather(bf16[16,2048]{1,0:T(8,128)(2,1)S(1)} %multiply_convert_fusion.4), channel_id=1, replica_groups=mesh['dp'=64,'tensor'=8] {'tensor'}, dimensions={1}, use_global_device_ids=true | all-gather | bytes 589824 | tf_op jit(solution)/shard_map/all_gather | solution.py:107
  1226.2 1.5 fusion.17
  1228.3 187.4 %all-reduce.12.cloned.1.call-done = f32[16,2048]{1,0:T(8,128)} async-done(((f32[16,2048]{1,0:T(8,128)}), f32[16,2048]{1,0:T(8,128)}) %all-reduce.12.cloned.1.call-update) | async-done | bytes 131088 | tf_op jit(solution)/shard_map/psum | solution.py:97
  1415.7 1.0 multiply_reduce_fusion
  1416.8 14.3 psum.87
  1431.1 1.6 multiply_convert_fusion.3
  (50 shorter events, 8.0 us)
Async XLA Ops:
  7.2 56.6 %copy-start = (bf16[128,2048]{1,0:T(8,128)(2,1)S(1)}, bf16[128,2048]{1,0:T(8,128)(2,1)}, u32[]{:S(2)}) copy-start(bf16[128,2048]{1,0:T(8,128)(2,1)} %param.11) | copy-start | bytes 1572868
  7.2 86.8 %copy-start.1 = (bf16[128,2048]{1,0:T(8,128)(2,1)S(1)}, bf16[128,2048]{1,0:T(8,128)(2,1)}, u32[]{:S(2)}) copy-start(bf16[128,2048]{1,0:T(8,128)(2,1)} %param.12) | copy-start | bytes 1572868
  7.2 231.5 %reduce-scatter.4.cloned.1.call-start = ((), (), s32[]{:S(2)}) async-start(), calls=%async_computation.7 | async-start | bytes 1064960
  94.6 1.5 copy-start.4
  94.6 1.5 copy-start.5
  94.7 145.4 %copy-start.6 = (f32[1,32,128]{2,1,0:T(8,128)S(1)}, f32[1,32,128]{2,1,0:T(8,128)}, u32[]{:S(2)}) copy-start(f32[1,32,128]{2,1,0:T(8,128)} %param.18) | copy-start | bytes 49156
  94.7 250.1 %copy-start.3 = (bf16[16,2048]{1,0:T(8,128)(2,1)S(1)}, bf16[16,2048]{1,0:T(8,128)(2,1)}, u32[]{:S(2)}) copy-start(bf16[16,2048]{1,0:T(8,128)(2,1)} %param.21) | copy-start | bytes 196612
  96.0 372.4 %all-gather.5.cloned.1.call-start = ((), (), s32[]{:S(2)}) async-start(), calls=%async_computation.5 | async-start | bytes 8404992 | tf_op jit(solution)/shard_map/all_gather | solution.py:80
  343.9 205.8 %all-gather.7.cloned.1.call-start = ((), (), s32[]{:S(2)}) async-start(), calls=%async_computation.6 | async-start | bytes 1064960 | tf_op jit(solution)/shard_map/all_gather | solution.py:73
  344.7 392.4 %all-reduce.6.cloned.1.call-start = ((), (), s32[]{:S(2)}) async-start(), calls=%async_computation.1 | async-start | bytes 262144 | tf_op jit(solution)/shard_map/psum | solution.py:97
  553.3 199.2 %copy-start.2 = (f32[2048]{0:T(1024)S(1)}, f32[2048]{0:T(1024)}, u32[]{:S(2)}) copy-start(f32[2048]{0:T(1024)} %param.20) | copy-start | bytes 24580
  554.8 408.4 %all-reduce.8.cloned.1.call-start = ((), (), s32[]{:S(2)}) async-start(), calls=%async_computation.2 | async-start | bytes 262144 | tf_op jit(solution)/shard_map/psum | solution.py:97
  775.2 414.4 %all-reduce.10.cloned.1.call-start = ((), (), s32[]{:S(2)}) async-start(), calls=%async_computation.3 | async-start | bytes 262144 | tf_op jit(solution)/shard_map/psum | solution.py:97
  1001.5 414.2 %all-reduce.12.cloned.1.call-start = ((), (), s32[]{:S(2)}) async-start(), calls=%async_computation.4 | async-start | bytes 262144 | tf_op jit(solution)/shard_map/psum | solution.py:97
Sparse Core Ops, SparseCore 0:
  96.2 142.4 reduce-scatter.3
  344.1 124.3 all-gather.4
  472.4 77.3 all-gather.6
  555.0 182.1 all-reduce.5
  775.3 187.9 all-reduce.7
  1001.6 187.9 all-reduce.9
  1227.8 187.9 all-reduce.11
where the time goes:
time: 1440 us
  waiting for transfers between devices  1070 us (74%)
  blocking collectives  322 us (22%)
  between operations  17.1 us (1%)
    psum x4, waiting for transfers between devices, body(): summed = lax.psum(value_portion, 'dp')  746 us
    unnamed x8, waiting for transfers between devices  142 us
    all_gather x1, waiting for transfers between devices, body(): lax.all_gather(updated[None, :, :rank_number], ('dp', 'tensor'), axis=0,...  104 us
    psum x1, blocking collectives, body(): squared = lax.psum(jnp.sum(share_pieces * share_pieces), ('dp', 'tensor'))  102 us
    all_gather x1, waiting for transfers between devices, body(): block_rows = lax.all_gather(new_factors, 'dp', axis=1, tiled=True)[0]  73.3 us
    all_gather x3, blocking collectives, body(): full_state = lax.all_gather(result, 'tensor', axis=1, tiled=True)  60.8 us
    psum x4, blocking collectives, body(): total = lax.psum(jnp.sum(resid * resid, axis=1), 'tensor')  57.4 us
    all_gather x1, blocking collectives, body(): lax.all_gather(factors.astype(jnp.bfloat16), 'dp', axis=1, tiled=True)[0]  53.7 us
  transfers between devices with their start and end apart: 7, of which 7 were waited for; matrix products, arithmetic and copies ran while one was open for 1% of the time, Pallas kernels for 0%

commit v1 on v0

v1 whole, which is shorter than its diff:
```python
import math

import jax
import jax.numpy as jnp
from jax import lax
from jax.sharding import Mesh
from jax.sharding import PartitionSpec as P

MODEL_WIDTH = 16384
SEQLEN = 128
GROUP = 8
RANK = 64
BATCH = 16
BLOCK = 2048
TILE = 256
OWN = 32

adapter_alpha = 2.0
beta_one = 0.9
beta_two = 0.999
rate = 0.1
adam_count = 200.0
scale = adapter_alpha / (RANK * math.sqrt(MODEL_WIDTH))

bf16 = jnp.bfloat16
f32 = jnp.float32
HIGHEST = lax.Precision.HIGHEST

AXES = ("x", "ya", "yb", "yc", "core", "z")
DP = ("x", "ya", "yb", "yc", "core")
MAJOR = ("x", "ya")
MINOR = ("yb", "yc", "core")


def swap(chunks, axes):
    return lax.all_to_all(chunks, axes, 0, 0, tiled=False)


def share(piece, axes, count):
    return swap(jnp.broadcast_to(piece[None], (count,) + piece.shape), axes)


def high_low(value):
    high = lax.reduce_precision(value, 8, 7)
    return high.astype(bf16), (value - high).astype(bf16)


def body(
    tokens,
    cotangent,
    prompt_len,
    resp_len,
    ranks,
    factors,
    first_moment,
    second_moment,
    base_weight,
    gain,
    state,
):
    major = lax.axis_index(MAJOR)
    minor = lax.axis_index(MINOR)
    z = lax.axis_index("z")
    dp = lax.axis_index(DP)
    at_home = (z == major).astype(f32)
    quarter = dp % 4

    crossed = lax.ppermute(
        base_weight, ("x", "ya", "z"), [(a * 8 + b, b * 8 + a) for a in range(8) for b in range(8)]
    )
    crossed = lax.all_gather(crossed, MINOR, axis=0, tiled=True)
    crossed = lax.dynamic_slice_in_dim(crossed, minor * TILE, TILE, 1)

    positions = jnp.arange(SEQLEN, dtype=jnp.int32)
    lower = prompt_len[:, None]
    upper = lower + resp_len[:, None]
    inside = (positions[None, :] >= lower) & (positions[None, :] < upper)
    advantage = (2 * ranks - (GROUP - 1)).astype(f32) / (GROUP - 1)
    per_seq = advantage / resp_len.astype(f32)
    weight = jnp.where(inside, per_seq[:, None], f32(0.0)).reshape(-1)
    weighted = (cotangent.astype(f32) * weight[:, None]).astype(bf16)

    low = share(factors[0].astype(bf16), DP, 64).reshape(BLOCK, 2 * RANK)
    hidden = jnp.dot(tokens, low[:, :RANK], preferred_element_type=f32)
    projected = jnp.dot(weighted, low[:, RANK:], preferred_element_type=f32)
    parts = share(jnp.concatenate([hidden, projected], axis=1).astype(bf16), "z", 8)
    both = jnp.sum(parts.astype(f32), axis=0).astype(bf16)
    dims = (((0,), (0,)), ((), ()))
    grad_down = lax.dot_general(tokens, both[:, RANK:], dims, preferred_element_type=f32)
    grad_up = lax.dot_general(weighted, both[:, :RANK], dims, preferred_element_type=f32)
    grads = jnp.concatenate([grad_down, grad_up], axis=1).astype(bf16)
    pieces = swap(grads.reshape(64, OWN, 2 * RANK), DP)
    grads = scale * jnp.sum(pieces.astype(f32), axis=0)

    squared = jnp.broadcast_to(jnp.sum(grads * grads), (1, 128))
    squared = jnp.sum(share(squared, ("x", "core"), 8), axis=0)
    squared = jnp.sum(share(squared, ("ya", "yb", "yc", "z"), 64), axis=0)
    clip = jnp.minimum(f32(1.0), f32(1.0) / (jnp.sqrt(squared) + 1e-06))
    grads = clip * grads
    moment_one = beta_one * first_moment[0] + (1.0 - beta_one) * grads
    moment_two = beta_two * second_moment[0] + (1.0 - beta_two) * grads * grads
    step_size = (
        moment_one
        / (1.0 - beta_one**adam_count)
        / (jnp.sqrt(moment_two / (1.0 - beta_two**adam_count)) + 1e-08)
    )
    updated = factors[0] - rate * step_size

    block = share(updated.astype(bf16), DP, 64).reshape(BLOCK, 2 * RANK)
    down_block = block[:, :RANK]
    up_block = block[:, RANK:].astype(f32)

    def crossed_product(current):
        tile = lax.dynamic_slice_in_dim(current, minor * TILE, TILE, 1).astype(f32)
        return jnp.dot(current, crossed, preferred_element_type=f32) + at_home * tile

    base = crossed_product(state)
    inner = jnp.dot(state, down_block, preferred_element_type=f32)
    gain_tile = lax.dynamic_slice_in_dim(gain, minor * TILE, TILE, 0)
    sent = jnp.concatenate(
        [lax.dynamic_slice_in_dim(block, minor * TILE, TILE, 0)]
        + [part.reshape(-1, 128) for value in (base, inner, gain_tile) for part in high_low(value)],
        axis=0,
    )
    got = share(sent, "z", 8)
    mine = lax.dynamic_index_in_dim(got, major, 0, keepdims=False)
    total = jnp.sum(got[:, TILE : TILE + 80].astype(f32), axis=0)
    base = (total[0:32] + total[32:64]).reshape(BATCH, TILE)
    inner = (total[64:72] + total[72:80]).reshape(BATCH, RANK)
    gain_tile = mine[TILE + 80 :].astype(f32)
    gain_tile = (gain_tile[0:2] + gain_tile[2:4]).reshape(TILE)
    down_tile = mine[:TILE, :RANK]
    up_tile = mine[:TILE, RANK:].astype(f32)
    resid = base + scale * jnp.dot(inner, up_tile.T, precision=HIGHEST)

    own_gain = lax.dynamic_slice_in_dim(gain.reshape(4, 4, 128), quarter, 1, 0)[0]

    def tile_to_own(resid):
        sums = jnp.sum(resid * resid, axis=1)
        current = (resid * gain_tile[None, :]).astype(bf16)
        part = jnp.dot(current, base_weight, preferred_element_type=f32)
        thin = jnp.dot(current, down_tile, preferred_element_type=f32)
        part = part + scale * jnp.dot(thin, up_block.T, precision=HIGHEST)
        home = lax.dynamic_update_slice(
            jnp.zeros((BATCH, BLOCK), f32), at_home * current.astype(f32), (0, minor * TILE)
        )
        part = (part + home).reshape(64, 4, 128)
        sums = jnp.broadcast_to(sums[:, None, None, None], (BATCH, 4, 4, 128)).reshape(64, 4, 128)
        got = jnp.sum(swap(jnp.concatenate([part, sums], axis=1), DP), axis=0)
        return got[:4] * lax.rsqrt(got[4:] / MODEL_WIDTH + 1e-05)

    own = tile_to_own(resid)
    current = share((own * own_gain).astype(bf16), DP, 64).reshape(BATCH, BLOCK)

    before = current.astype(f32) / gain[None, :]
    sums = jnp.sum(before * before, axis=1)
    inner = jnp.dot(current, down_block, preferred_element_type=f32)
    part = crossed_product(current) + scale * jnp.dot(inner, up_tile.T, precision=HIGHEST)
    sent = jnp.concatenate([part, jnp.broadcast_to(sums[:, None], (BATCH, 128))], axis=1)
    got = jnp.sum(share(sent, "z", 8), axis=0)
    resid = got[:, :TILE] * lax.rsqrt(got[:, TILE : TILE + 1] / MODEL_WIDTH + 1e-05)

    own = tile_to_own(resid)
    sums = jnp.broadcast_to(jnp.sum(own * own), (1, 128))
    sums = jnp.sum(share(sums, ("yc", "core", "z"), 32), axis=0)
    own = (own * lax.rsqrt(sums / MODEL_WIDTH + 1e-05) * own_gain).astype(bf16)
    result = share(own, DP, 64).reshape(BATCH, BLOCK)
    return (updated[None], result)


def solution(mesh):
    fine = Mesh(mesh.devices.reshape(4, 2, 2, 2, 2, 8), AXES)
    return jax.shard_map(
        body,
        mesh=fine,
        in_specs=(
            P(DP, "z"),
            P(DP, "z"),
            P(DP),
            P(DP),
            P(DP),
            P("z", DP, None),
            P("z", DP, None),
            P("z", DP, None),
            P(DP, "z"),
            P("z"),
            P(None, "z"),
        ),
        out_specs=(P("z", DP, None), P(None, "z")),
        check_vma=False,
    )
```

time: 1440 us -> 387 us (0.27)
  waiting for transfers between devices: 1070 us -> 68.5 us
  blocking collectives: 322 us -> 151 us
  starting transfers between devices: 0.29 us -> 128 us
    psum x4 -> x0, waiting for transfers between devices: 746 us -> none  [body(): summed = lax.psum(value_portion, 'dp')]
    psum x6 -> x0, blocking collectives: 188 us -> none  [the longest x1 102 us: body(): squared = lax.psum(jnp.sum(share_pieces * share_pieces), ('dp', 'tensor'))]
    all_gather x2 -> x1, waiting for transfers between devices: 177 us -> 0.02 us  [body(): crossed = lax.all_gather(crossed, MINOR, axis=0, tiled=True)]
    all_to_all x0 -> x9, blocking collectives: none -> 151 us  [swap(): return lax.all_to_all(chunks, axes, 0, 0, tiled=False)]
    unnamed x8 -> x1, waiting for transfers between devices: 142 us -> 0.02 us
    all_gather x5 -> x0, blocking collectives: 134 us -> none  [the longest x3 60.8 us: body(): full_state = lax.all_gather(result, 'tensor', axis=1, tiled=True)]
    all_to_all x0 -> x4, starting transfers between devices: none -> 126 us  [swap(): return lax.all_to_all(chunks, axes, 0, 0, tiled=False)]
    all_to_all x0 -> x4, waiting for transfers between devices: none -> 68.5 us  [swap(): return lax.all_to_all(chunks, axes, 0, 0, tiled=False)]
  transfers between devices with their start and end apart: 7 -> 6, of which waited for: 7 -> 4; matrix products, arithmetic and copies ran while one was open for 1% -> 3% of each run, Pallas kernels for 0% -> 0%
where the time goes in v1:
time: 387 us; the launch traced here: 386 us
  blocking collectives  151 us (39%)
  starting transfers between devices  128 us (33%)
  waiting for transfers between devices  68.5 us (18%)
  between operations  16.6 us (4%)
  matrix products  9.59 us (2%)
  local copies, waits for them, and re-layouts  7.95 us (2%)
  other arithmetic  5.26 us (1%)
    all_to_all x9, blocking collectives, swap(): return lax.all_to_all(chunks, axes, 0, 0, tiled=False)  151 us
    all_to_all x4, starting transfers between devices, swap(): return lax.all_to_all(chunks, axes, 0, 0, tiled=False)  126 us
    all_to_all x4, waiting for transfers between devices, swap(): return lax.all_to_all(chunks, axes, 0, 0, tiled=False)  68.5 us
  transfers between devices with their start and end apart: 6, of which 4 were waited for; matrix products, arithmetic and copies ran while one was open for 3% of the time, Pallas kernels for 0%

profile of v1, /device:TPU:1, one launch (start us, length us, event | category | flops | bytes accessed | tf_op | source)
XLA Modules:
  0.0 386.3 jit_solution(2986191570395032863)
XLA Ops:
  7.3 2.0 collective-permute-start
  9.3 1.1 copy-done.2
  10.4 0.7 convert_bitcast_fusion.1
  11.1 0.9 broadcast_in_dim.49
  12.0 109.9 %all-to-all-start = ((bf16[64,32,128]{2,1,0:T(8,128)(2,1)}), bf16[64,32,128]{2,1,0:T(8,128)(2,1)S(1)}, u32[]{:S(2)}, u32[]{:S(2)}) async-start(bf16[64,32,128]{2,1,0:T(8,128)(2,1)} %broadcast_in_dim.49), calls=%async_computation | async-start | bytes 1048576 | tf_op jit(solution)/shard_map/all_to_all | solution.py:36
  124.0 17.5 %all-to-all-done = bf16[64,32,128]{2,1,0:T(8,128)(2,1)S(1)} async-done(((bf16[64,32,128]{2,1,0:T(8,128)(2,1)}), bf16[64,32,128]{2,1,0:T(8,128)(2,1)S(1)}, u32[]{:S(2)}, u32[]{:S(2)}) %all-to-all-start) | async-done | bytes 524320 | tf_op jit(solution)/shard_map/all_to_all | solution.py:36
  141.8 1.7 convolution_convert_fusion.2
  143.7 25.7 %all_to_all.65 = bf16[8,128,128]{2,1,0:T(8,128)(2,1)S(1)} all-to-all(bf16[8,128,128]{2,1,0:T(8,128)(2,1)S(1)} %broadcast_in_dim.53), channel_id=1, replica_groups=mesh['x'=4,'ya'=2,'yb'=2,'yc'=2,'core'=2,'z'=8] {'z'}, dimensions={0} | all-to-all | bytes 524288 | tf_op jit(solution)/shard_map/all_to_all | solution.py:36
  169.5 1.3 convolution_convert_fusion
  172.0 29.4 %all_to_all.66 = bf16[64,32,128]{2,1,0:T(8,128)(2,1)S(1)} all-to-all(bf16[64,32,128]{2,1,0:T(8,128)(2,1)S(1)} %pad_maximum_fusion), channel_id=1, replica_groups=mesh['x'=4,'ya'=2,'yb'=2,'yc'=2,'core'=2,'z'=8] {'x','ya','yb','yc','core'}, dimensions={0} | all-to-all | bytes 1048576 | tf_op jit(solution)/shard_map/all_to_all | solution.py:36
  202.1 0.6 broadcast_in_dim_broadcast_in_dim_broadcast_in_dim.6
  202.8 9.2 %all_to_all.67 = f32[8,1,128]{2,1,0:T(1,128)S(1)} all-to-all(f32[8,1,128]{2,1,0:T(1,128)S(1)} %broadcast_in_dim_broadcast_in_dim_broadcast_in_dim.6), channel_id=1, replica_groups=mesh['x'=4,'ya'=2,'yb'=2,'yc'=2,'core'=2,'z'=8] {'x','core'}, dimensions={0} | all-to-all | bytes 8192 | tf_op jit(solution)/shard_map/all_to_all | solution.py:36
  212.0 14.9 %all_to_all.68 = f32[64,1,128]{2,1,0:T(1,128)S(1)} all-to-all(f32[64,1,128]{2,1,0:T(1,128)S(1)} %broadcast_in_dim.54), channel_id=1, replica_groups=mesh['x'=4,'ya'=2,'yb'=2,'yc'=2,'core'=2,'z'=8] {'ya','yb','yc','z'}, dimensions={0} | all-to-all | bytes 65536 | tf_op jit(solution)/shard_map/all_to_all | solution.py:36
  226.9 0.6 convert_bitcast_fusion
  227.5 0.9 broadcast_in_dim.56
  228.4 6.0 %all-to-all-start.5 = ((bf16[64,32,128]{2,1,0:T(8,128)(2,1)}), bf16[64,32,128]{2,1,0:T(8,128)(2,1)S(1)}, u32[]{:S(2)}, u32[]{:S(2)}) async-start(bf16[64,32,128]{2,1,0:T(8,128)(2,1)} %broadcast_in_dim.56), calls=%async_computation.5 | async-start | bytes 1048576 | tf_op jit(solution)/shard_map/all_to_all | solution.py:36
  234.5 17.2 %all-to-all-done.5 = bf16[64,32,128]{2,1,0:T(8,128)(2,1)S(1)} async-done(((bf16[64,32,128]{2,1,0:T(8,128)(2,1)}), bf16[64,32,128]{2,1,0:T(8,128)(2,1)S(1)}, u32[]{:S(2)}, u32[]{:S(2)}) %all-to-all-start.5) | async-done | bytes 524320 | tf_op jit(solution)/shard_map/all_to_all | solution.py:36
  252.1 1.5 fusion.25
  253.8 1.0 broadcast_in_dim.57
  254.8 3.5 all-to-all-start.6
  258.3 21.7 %all-to-all-done.6 = bf16[8,340,128]{2,1,0:T(8,128)(2,1)S(1)} async-done(((bf16[8,340,128]{2,1,0:T(8,128)(2,1)}), bf16[8,340,128]{2,1,0:T(8,128)(2,1)S(1)}, u32[]{:S(2)}, u32[]{:S(2)}) %all-to-all-start.6) | async-done | bytes 696352 | tf_op jit(solution)/shard_map/all_to_all | solution.py:36
  282.0 0.8 pad_maximum_fusion.1
  282.8 6.2 %all-to-all-start.7 = ((f32[64,8,128]{2,1,0:T(8,128)}), f32[64,8,128]{2,1,0:T(8,128)S(1)}, u32[]{:S(2)}, u32[]{:S(2)}) async-start(f32[64,8,128]{2,1,0:T(8,128)} %pad_maximum_fusion.1), calls=%async_computation.7 | async-start | bytes 524288 | tf_op jit(solution)/shard_map/all_to_all | solution.py:36
  289.0 12.0 %all-to-all-done.7 = f32[64,8,128]{2,1,0:T(8,128)S(1)} async-done(((f32[64,8,128]{2,1,0:T(8,128)}), f32[64,8,128]{2,1,0:T(8,128)S(1)}, u32[]{:S(2)}, u32[]{:S(2)}) %all-to-all-start.7) | async-done | bytes 262176 | tf_op jit(solution)/shard_map/all_to_all | solution.py:36
  301.1 15.6 %all_to_all.69 = bf16[64,4,128]{2,1,0:T(4,128)(2,1)S(1)} all-to-all(bf16[64,4,128]{2,1,0:T(4,128)(2,1)S(1)} %broadcast_in_dim.112), channel_id=1, replica_groups=mesh['x'=4,'ya'=2,'yb'=2,'yc'=2,'core'=2,'z'=8] {'x','ya','yb','yc','core'}, dimensions={0} | all-to-all | bytes 131072 | tf_op jit(solution)/shard_map/all_to_all | solution.py:36
  317.9 1.5 fusion.4
  319.6 12.8 %all_to_all.70 = f32[8,16,384]{2,1,0:T(8,128)S(1)} all-to-all(f32[8,16,384]{2,1,0:T(8,128)S(1)} %broadcast_in_dim.114), channel_id=1, replica_groups=mesh['x'=4,'ya'=2,'yb'=2,'yc'=2,'core'=2,'z'=8] {'z'}, dimensions={0} | all-to-all | bytes 393216 | tf_op jit(solution)/shard_map/all_to_all | solution.py:36
  334.2 16.4 %all_to_all.71 = f32[64,8,128]{2,1,0:T(8,128)S(1)} all-to-all(f32[64,8,128]{2,1,0:T(8,128)S(1)} %pad_maximum_fusion.2), channel_id=1, replica_groups=mesh['x'=4,'ya'=2,'yb'=2,'yc'=2,'core'=2,'z'=8] {'x','ya','yb','yc','core'}, dimensions={0} | all-to-all | bytes 524288 | tf_op jit(solution)/shard_map/all_to_all | solution.py:36
  351.3 0.7 broadcast_in_dim_broadcast_in_dim_broadcast_in_dim.7
  351.9 11.0 %all_to_all.72 = f32[32,1,128]{2,1,0:T(1,128)S(1)} all-to-all(f32[32,1,128]{2,1,0:T(1,128)S(1)} %broadcast_in_dim_broadcast_in_dim_broadcast_in_dim.7), channel_id=1, replica_groups=mesh['x'=4,'ya'=2,'yb'=2,'yc'=2,'core'=2,'z'=8] {'yc','core','z'}, dimensions={0} | all-to-all | bytes 32768 | tf_op jit(solution)/shard_map/all_to_all | solution.py:36
  363.0 15.8 %all_to_all.73 = bf16[64,4,128]{2,1,0:T(4,128)(2,1)S(1)} all-to-all(bf16[64,4,128]{2,1,0:T(4,128)(2,1)S(1)} %broadcast_in_dim.118), channel_id=1, replica_groups=mesh['x'=4,'ya'=2,'yb'=2,'yc'=2,'core'=2,'z'=8] {'x','ya','yb','yc','core'}, dimensions={0} | all-to-all | bytes 131072 | tf_op jit(solution)/shard_map/all_to_all | solution.py:36
  378.8 0.7 reshape.215
  (90 shorter events, 8.9 us)
Async XLA Ops:
  7.2 134.3 %copy-start = (bf16[128,2048]{1,0:T(8,128)(2,1)S(1)}, bf16[128,2048]{1,0:T(8,128)(2,1)}, u32[]{:S(2)}) copy-start(bf16[128,2048]{1,0:T(8,128)(2,1)} %param.11) | copy-start | bytes 1572868
  7.2 219.7 %copy-start.4 = (f32[1,32,128]{2,1,0:T(8,128)S(1)}, f32[1,32,128]{2,1,0:T(8,128)}, u32[]{:S(2)}) copy-start(f32[1,32,128]{2,1,0:T(8,128)} %param.16) | copy-start | bytes 49156
  7.2 219.7 %copy-start.6 = (f32[1,32,128]{2,1,0:T(8,128)S(1)}, f32[1,32,128]{2,1,0:T(8,128)}, u32[]{:S(2)}) copy-start(f32[1,32,128]{2,1,0:T(8,128)} %param.18) | copy-start | bytes 49156
  7.2 219.7 %copy-start.7 = (f32[1,32,128]{2,1,0:T(8,128)S(1)}, f32[1,32,128]{2,1,0:T(8,128)}, u32[]{:S(2)}) copy-start(f32[1,32,128]{2,1,0:T(8,128)} %param.17) | copy-start | bytes 49156
  7.2 227.2 %copy-start.5 = (f32[2048]{0:T(1024)S(1)}, f32[2048]{0:T(1024)}, u32[]{:S(2)}) copy-start(f32[2048]{0:T(1024)} %param.20) | copy-start | bytes 24580
  7.2 244.5 %copy-start.3 = (bf16[16,2048]{1,0:T(8,128)(2,1)S(1)}, bf16[16,2048]{1,0:T(8,128)(2,1)}, u32[]{:S(2)}) copy-start(bf16[16,2048]{1,0:T(8,128)(2,1)} %param.21) | copy-start | bytes 196612
  7.2 244.9 %all-gather.2.cloned.1.call-start = ((), (), s32[]{:S(2)}) async-start(), calls=%async_computation.13 | async-start | bytes 9437184 | tf_op jit(solution)/shard_map/all_gather | solution.py:71
  7.3 2.0 collective-permute-start
  9.3 1.1 copy-start.2
  12.0 129.5 %all-to-all-start = ((bf16[64,32,128]{2,1,0:T(8,128)(2,1)}), bf16[64,32,128]{2,1,0:T(8,128)(2,1)S(1)}, u32[]{:S(2)}, u32[]{:S(2)}) async-start(bf16[64,32,128]{2,1,0:T(8,128)(2,1)} %broadcast_in_dim.49), calls=%async_computation | async-start | bytes 1048576 | tf_op jit(solution)/shard_map/all_to_all | solution.py:36
  121.9 158.7 %copy-start.1 = (bf16[256,2048]{1,0:T(8,128)(2,1)S(1)}, bf16[256,2048]{1,0:T(8,128)(2,1)}, u32[]{:S(2)}) copy-start(bf16[256,2048]{1,0:T(8,128)(2,1)} %param.19) | copy-start | bytes 3145732
  228.4 23.3 %all-to-all-start.5 = ((bf16[64,32,128]{2,1,0:T(8,128)(2,1)}), bf16[64,32,128]{2,1,0:T(8,128)(2,1)S(1)}, u32[]{:S(2)}, u32[]{:S(2)}) async-start(bf16[64,32,128]{2,1,0:T(8,128)(2,1)} %broadcast_in_dim.56), calls=%async_computation.5 | async-start | bytes 1048576 | tf_op jit(solution)/shard_map/all_to_all | solution.py:36
  254.8 25.3 %all-to-all-start.6 = ((bf16[8,340,128]{2,1,0:T(8,128)(2,1)}), bf16[8,340,128]{2,1,0:T(8,128)(2,1)S(1)}, u32[]{:S(2)}, u32[]{:S(2)}) async-start(bf16[8,340,128]{2,1,0:T(8,128)(2,1)} %broadcast_in_dim.57), calls=%async_computation.6 | async-start | bytes 1409024 | tf_op jit(solution)/shard_map/all_to_all | solution.py:36
  282.8 18.2 %all-to-all-start.7 = ((f32[64,8,128]{2,1,0:T(8,128)}), f32[64,8,128]{2,1,0:T(8,128)S(1)}, u32[]{:S(2)}, u32[]{:S(2)}) async-start(f32[64,8,128]{2,1,0:T(8,128)} %pad_maximum_fusion.1), calls=%async_computation.7 | async-start | bytes 524288 | tf_op jit(solution)/shard_map/all_to_all | solution.py:36
Sparse Core Ops, SparseCore 0:
  10.5 214.3 all-gather.1

commit v2 on v1

v2 whole, which is shorter than its diff:
```python
import math

import jax
import jax.numpy as jnp
from jax import lax
from jax.sharding import Mesh
from jax.sharding import PartitionSpec as P

MODEL_WIDTH = 16384
SEQLEN = 128
GROUP = 8
DECODE_STEPS = 4
RANK = 64
BATCH = 16
BLOCK = 2048
TILE = 256
OWN = 32

adapter_alpha = 2.0
beta_one = 0.9
beta_two = 0.999
rate = 0.1
adam_count = 200.0
scale = adapter_alpha / (RANK * math.sqrt(MODEL_WIDTH))

bf16 = jnp.bfloat16
f32 = jnp.float32
HIGHEST = lax.Precision.HIGHEST

AXES = ("x", "ya", "yb", "yc", "core", "z")
DP = ("x", "ya", "yb", "yc", "core")
MAJOR = ("x", "ya")
MINOR = ("yb", "yc", "core")
CROSS = ("x", "ya", "z")


def swap(chunks, axes):
    return lax.all_to_all(chunks, axes, 0, 0, tiled=False)


def share(piece, axes, count):
    return swap(jnp.broadcast_to(piece[None], (count,) + piece.shape), axes)


def high_low(value):
    high = lax.reduce_precision(value, 8, 7)
    return high.astype(bf16), (value - high).astype(bf16)


def chunks_of(value):
    return value.reshape(8, 2, 8, TILE).transpose(0, 2, 1, 3).reshape(64, 4, 128)


def body(
    tokens,
    cotangent,
    prompt_len,
    resp_len,
    ranks,
    factors,
    first_moment,
    second_moment,
    base_weight,
    gain,
    state,
):
    major = lax.axis_index(MAJOR)
    minor = lax.axis_index(MINOR)
    z = lax.axis_index("z")

    swapped = [(a * 8 + b, b * 8 + a) for a in range(8) for b in range(8)]
    old = lax.ppermute(
        jnp.concatenate([factors[0], first_moment[0], second_moment[0]], axis=0), DP, swapped
    )

    positions = jnp.arange(SEQLEN, dtype=jnp.int32)
    lower = prompt_len[:, None]
    upper = lower + resp_len[:, None]
    inside = (positions[None, :] >= lower) & (positions[None, :] < upper)
    advantage = (2 * ranks - (GROUP - 1)).astype(f32) / (GROUP - 1)
    per_seq = advantage / resp_len.astype(f32)
    weight = jnp.where(inside, per_seq[:, None], f32(0.0)).reshape(-1)
    weighted = (cotangent.astype(f32) * weight[:, None]).astype(bf16)

    low = share(factors[0].astype(bf16), DP, 64).reshape(BLOCK, 2 * RANK)
    hidden = jnp.dot(tokens, low[:, :RANK], preferred_element_type=f32)
    projected = jnp.dot(weighted, low[:, RANK:], preferred_element_type=f32)
    state_tile = lax.dynamic_slice_in_dim(state, minor * TILE, TILE, 1)
    sent = jnp.concatenate(
        [jnp.concatenate([hidden, projected], axis=1).astype(bf16), state_tile.reshape(32, 128)],
        axis=0,
    )
    got = share(sent, "z", 8)
    both = jnp.sum(got[:, :SEQLEN].astype(f32), axis=0).astype(bf16)
    states = got[:, SEQLEN:].reshape(8, BATCH, TILE)

    dims = (((0,), (0,)), ((), ()))
    grad_down = lax.dot_general(tokens, both[:, RANK:], dims, preferred_element_type=f32)
    grad_up = lax.dot_general(weighted, both[:, :RANK], dims, preferred_element_type=f32)
    grads = jnp.concatenate([grad_down, grad_up], axis=1).astype(bf16)
    grads = grads.reshape(8, 8, OWN, 2 * RANK).transpose(1, 0, 2, 3).reshape(64, OWN, 2 * RANK)
    first = lax.dynamic_index_in_dim(states, major, 0, keepdims=False)
    first = chunks_of(jnp.dot(first, base_weight, preferred_element_type=f32))
    pieces = swap(jnp.concatenate([grads, *high_low(first)], axis=1), DP).astype(f32)
    pieces = jnp.sum(pieces, axis=0)
    grads = scale * pieces[:OWN]
    own_state = lax.dynamic_slice(state, (2 * major, minor * TILE), (2, TILE)).astype(f32)
    own_base = (pieces[OWN : OWN + 4] + pieces[OWN + 4 :]).reshape(2, TILE) + own_state

    squared = jnp.broadcast_to(jnp.sum(grads * grads), (1, 128))
    squared = jnp.sum(share(squared, ("x", "core"), 8), axis=0)
    squared = jnp.sum(share(squared, ("ya", "yb", "yc", "z"), 64), axis=0)
    clip = jnp.minimum(f32(1.0), f32(1.0) / (jnp.sqrt(squared) + 1e-06))
    grads = clip * grads
    moment_one = beta_one * old[OWN : 2 * OWN] + (1.0 - beta_one) * grads
    moment_two = beta_two * old[2 * OWN :] + (1.0 - beta_two) * grads * grads
    step_size = (
        moment_one
        / (1.0 - beta_one**adam_count)
        / (jnp.sqrt(moment_two / (1.0 - beta_two**adam_count)) + 1e-08)
    )
    updated = old[:OWN] - rate * step_size
    new_factors = lax.ppermute(updated, DP, swapped)[None]

    own_gain = lax.dynamic_slice_in_dim(gain, minor * TILE, TILE, 0)
    sent = jnp.concatenate(
        [
            updated.astype(bf16),
            *[part.reshape(-1, 128) for value in (own_base, own_gain) for part in high_low(value)],
        ],
        axis=0,
    )
    got = share(sent, CROSS, 64).reshape(8, 8, OWN + 12, 128)
    home = lax.dynamic_index_in_dim(got, major, 1, keepdims=False)
    near = lax.dynamic_index_in_dim(got[:, :, :OWN, RANK:], z, 1, keepdims=False)
    down_tile = home[:, :OWN, :RANK].reshape(TILE, RANK)
    up_tile = home[:, :OWN, RANK:].reshape(TILE, RANK).astype(f32)
    up_near = near.reshape(TILE, RANK).astype(f32)
    rest = home[:, OWN:].astype(f32)
    base = (rest[:, 0:4] + rest[:, 4:8]).reshape(BATCH, TILE)
    tile_gain = (rest[0, 8:10] + rest[0, 10:12]).reshape(TILE)

    states = states.reshape(8, BATCH, 8, OWN).transpose(1, 2, 0, 3).reshape(BATCH, BLOCK)
    down_all = got[:, :, :OWN, :RANK].reshape(BLOCK, RANK)
    inner = jnp.dot(states, down_all, preferred_element_type=f32)
    inner = jnp.sum(share(inner.reshape(8, 128), MINOR, 8), axis=0).reshape(BATCH, RANK)
    resid = base + scale * jnp.dot(inner, up_tile.T, precision=HIGHEST)
    inner = lax.dynamic_slice_in_dim(inner, 2 * major, 2, 0)
    own = own_base + scale * jnp.dot(inner, up_near.T, precision=HIGHEST)
    own = (own * own_gain).astype(bf16)
    current = (resid * tile_gain).astype(bf16)

    for step in range(1, DECODE_STEPS):
        if step > 1:
            current = share(own.reshape(4, 128), CROSS, 64).reshape(8, 8, 4, 128)
            current = lax.dynamic_index_in_dim(current, major, 1, keepdims=False)
            current = current.reshape(BATCH, TILE)
            resid = current.astype(f32) / tile_gain
        sums = jnp.sum(resid * resid, axis=1)
        part = jnp.dot(current, base_weight, preferred_element_type=f32)
        thin = jnp.dot(current, down_tile, preferred_element_type=f32)
        pairs = jnp.stack(
            [thin.reshape(8, 128), jnp.broadcast_to(sums[:, None], (BATCH, 64)).reshape(8, 128)],
            axis=1,
        )
        pairs = jnp.broadcast_to(pairs[:, None], (8, 8, 2, 128)).reshape(64, 2, 128)
        got = jnp.sum(swap(jnp.concatenate([chunks_of(part), pairs], axis=1), DP), axis=0)
        thin = got[4].reshape(2, RANK)
        norm = lax.rsqrt(got[5].reshape(2, 64)[:, :1] / MODEL_WIDTH + 1e-05)
        total = own.astype(f32) + got[:4].reshape(2, TILE)
        resid = norm * (total + scale * jnp.dot(thin, up_near.T, precision=HIGHEST))
        own = (resid * own_gain).astype(bf16)

    sums = jnp.broadcast_to(jnp.sum(resid * resid, axis=1)[:, None], (2, 64)).reshape(1, 128)
    sums = jnp.sum(share(sums, ("yb", "yc", "core", "z"), 64), axis=0).reshape(2, 64)[:, :1]
    own = (resid * lax.rsqrt(sums / MODEL_WIDTH + 1e-05) * own_gain).astype(bf16)
    result = share(own.reshape(4, 128), DP, 64)
    result = result.reshape(8, 8, 2, TILE).transpose(0, 2, 1, 3).reshape(BATCH, BLOCK)
    return (new_factors, result)


def solution(mesh):
    fine = Mesh(mesh.devices.reshape(4, 2, 2, 2, 2, 8), AXES)
    return jax.shard_map(
        body,
        mesh=fine,
        in_specs=(
            P(DP, "z"),
            P(DP, "z"),
            P(DP),
            P(DP),
            P(DP),
            P("z", DP, None),
            P("z", DP, None),
            P("z", DP, None),
            P(DP, "z"),
            P("z"),
            P(None, "z"),
        ),
        out_specs=(P("z", DP, None), P(None, "z")),
        check_vma=False,
    )
```

time: 387 us -> 306 us (0.79)
  blocking collectives: 151 us -> 90 us
  starting transfers between devices: 128 us -> 82.9 us
  waiting for transfers between devices: 68.5 us -> 88.9 us
  between operations: 16.6 us -> 3.21 us
  local copies, waits for them, and re-layouts: 7.95 us -> 18 us
  other arithmetic: 5.26 us -> 12 us
    all_to_all x9 -> x5, blocking collectives: 151 us -> 90 us  [swap(): return lax.all_to_all(chunks, axes, 0, 0, tiled=False)]
    all_to_all x4 -> x9, starting transfers between devices: 126 us -> 68 us  [swap(): return lax.all_to_all(chunks, axes, 0, 0, tiled=False)]
    all_to_all x4 -> x9, waiting for transfers between devices: 68.5 us -> 87.1 us  [swap(): return lax.all_to_all(chunks, axes, 0, 0, tiled=False)]
    ppermute x1 -> x2, starting transfers between devices: 2.02 us -> 14.9 us  [the longest x1 7.45 us: body(): lax.ppermute(jnp.concatenate([factors[0], first_moment[0], second_moment[...]
  transfers between devices with their start and end apart: 6 -> 11, of which waited for: 4 -> 10; matrix products, arithmetic and copies ran while one was open for 3% -> 3% of each run, Pallas kernels for 0% -> 0%
where the time goes in v2:
time: 306 us; the launch traced here: 305 us
  blocking collectives  90 us (29%)
  waiting for transfers between devices  88.9 us (29%)
  starting transfers between devices  82.9 us (27%)
  local copies, waits for them, and re-layouts  18 us (6%)
  other arithmetic  12 us (4%)
  matrix products  9.97 us (3%)
  between operations  3.21 us (1%)
    all_to_all x5, blocking collectives, swap(): return lax.all_to_all(chunks, axes, 0, 0, tiled=False)  90 us
    all_to_all x9, waiting for transfers between devices, swap(): return lax.all_to_all(chunks, axes, 0, 0, tiled=False)  87.1 us
    all_to_all x9, starting transfers between devices, swap(): return lax.all_to_all(chunks, axes, 0, 0, tiled=False)  68 us
    ppermute x1, starting transfers between devices, body(): lax.ppermute(jnp.concatenate([factors[0], first_moment[0], second_moment[...  7.45 us
    ppermute x1, starting transfers between devices, body(): new_factors = lax.ppermute(updated, DP, swapped)[None]  7.45 us
  transfers between devices with their start and end apart: 11, of which 10 were waited for; matrix products, arithmetic and copies ran while one was open for 3% of the time, Pallas kernels for 0%

profile of v2, /device:TPU:1, one launch (start us, length us, event | category | flops | bytes accessed | tf_op | source)
XLA Modules:
  0.0 304.9 jit_solution(1224190633669211703)
XLA Ops:
  2.3 11.8 %all-to-all-start = ((bf16[64,32,128]{2,1,0:T(8,128)(2,1)}), bf16[64,32,128]{2,1,0:T(8,128)(2,1)S(1)}, u32[]{:S(2)}, u32[]{:S(2)}) async-start(bf16[64,32,128]{2,1,0:T(8,128)(2,1)} %broadcast_in_dim.73), calls=%async_computation | async-start | bytes 1048576 | tf_op jit(solution)/shard_map/all_to_all | solution.py:38
  16.9 14.5 %all-to-all-done = bf16[64,32,128]{2,1,0:T(8,128)(2,1)S(1)} async-done(((bf16[64,32,128]{2,1,0:T(8,128)(2,1)}), bf16[64,32,128]{2,1,0:T(8,128)(2,1)S(1)}, u32[]{:S(2)}, u32[]{:S(2)}) %all-to-all-start) | async-done | bytes 524320 | tf_op jit(solution)/shard_map/all_to_all | solution.py:38
  33.3 10.0 %all-to-all-start.1 = ((bf16[8,160,128]{2,1,0:T(8,128)(2,1)}), bf16[8,160,128]{2,1,0:T(8,128)(2,1)S(1)}, u32[]{:S(2)}, u32[]{:S(2)}) async-start(bf16[8,160,128]{2,1,0:T(8,128)(2,1)} %broadcast_in_dim.146), calls=%async_computation.1 | async-start | bytes 655360 | tf_op jit(solution)/shard_map/all_to_all | solution.py:38
  43.9 13.1 %all-to-all-done.1 = bf16[8,160,128]{2,1,0:T(8,128)(2,1)S(1)} async-done(((bf16[8,160,128]{2,1,0:T(8,128)(2,1)}), bf16[8,160,128]{2,1,0:T(8,128)(2,1)S(1)}, u32[]{:S(2)}, u32[]{:S(2)}) %all-to-all-start.1) | async-done | bytes 327712 | tf_op jit(solution)/shard_map/all_to_all | solution.py:38
  59.1 1.2 copy.144
  60.3 2.0 copy.143
  62.2 1.3 maximum_bitcast_fusion
  65.4 6.3 %all-to-all-start.2 = ((bf16[64,40,128]{2,1,0:T(8,128)(2,1)}), bf16[64,40,128]{2,1,0:T(8,128)(2,1)S(1)}, u32[]{:S(2)}, u32[]{:S(2)}) async-start(bf16[64,40,128]{2,1,0:T(8,128)(2,1)} %pad_maximum_fusion), calls=%async_computation.2 | async-start | bytes 1310720 | tf_op jit(solution)/shard_map/all_to_all | solution.py:38
  71.7 7.5 %collective-permute-start = (f32[96,128]{1,0:T(8,128)S(1)}, f32[96,128]{1,0:T(8,128)S(1)}, u32[]{:S(2)}, u32[]{:S(2)}) collective-permute-start(f32[96,128]{1,0:T(8,128)S(1)} %pad_maximum_fusion.5), channel_id=1, source_target_pairs={{0,0},{8,64},{16,128},{24,192},{32,256},{40,320},{48,384},{56,448}... | collective-permute-start | bytes 147464 | tf_op jit(solution)/shard_map/ppermute | solution.py:72
  80.0 11.4 %all-to-all-done.2 = bf16[64,40,128]{2,1,0:T(8,128)(2,1)S(1)} async-done(((bf16[64,40,128]{2,1,0:T(8,128)(2,1)}), bf16[64,40,128]{2,1,0:T(8,128)(2,1)S(1)}, u32[]{:S(2)}, u32[]{:S(2)}) %all-to-all-start.2) | async-done | bytes 655392 | tf_op jit(solution)/shard_map/all_to_all | solution.py:38
  92.0 1.2 broadcast_in_dim_broadcast_in_dim_broadcast_in_dim.3
  93.3 6.3 %all-to-all-start.3 = ((f32[8,1,128]{2,1,0:T(1,128)}), f32[8,1,128]{2,1,0:T(1,128)S(1)}, u32[]{:S(2)}, u32[]{:S(2)}) async-start(f32[8,1,128]{2,1,0:T(1,128)} %broadcast_in_dim_broadcast_in_dim_broadcast_in_dim.3), calls=%async_computation.3 | async-start | bytes 8192 | tf_op jit(solution)/shard_map/all_to_all | solution.py:38
  99.6 4.5 %all-to-all-done.3 = f32[8,1,128]{2,1,0:T(1,128)S(1)} async-done(((f32[8,1,128]{2,1,0:T(1,128)}), f32[8,1,128]{2,1,0:T(1,128)S(1)}, u32[]{:S(2)}, u32[]{:S(2)}) %all-to-all-start.3) | async-done | bytes 4128 | tf_op jit(solution)/shard_map/all_to_all | solution.py:38
  104.8 4.6 %all-to-all-start.4 = ((f32[64,1,128]{2,1,0:T(1,128)}), f32[64,1,128]{2,1,0:T(1,128)S(1)}, u32[]{:S(2)}, u32[]{:S(2)}) async-start(f32[64,1,128]{2,1,0:T(1,128)} %broadcast_in_dim.147), calls=%async_computation.4 | async-start | bytes 65536 | tf_op jit(solution)/shard_map/all_to_all | solution.py:38
  110.2 9.9 %all-to-all-done.4 = f32[64,1,128]{2,1,0:T(1,128)S(1)} async-done(((f32[64,1,128]{2,1,0:T(1,128)}), f32[64,1,128]{2,1,0:T(1,128)S(1)}, u32[]{:S(2)}, u32[]{:S(2)}) %all-to-all-start.4) | async-done | bytes 32800 | tf_op jit(solution)/shard_map/all_to_all | solution.py:38
  121.8 4.6 %all-to-all-start.5 = ((bf16[64,44,128]{2,1,0:T(8,128)(2,1)}), bf16[64,44,128]{2,1,0:T(8,128)(2,1)S(1)}, u32[]{:S(2)}, u32[]{:S(2)}) async-start(bf16[64,44,128]{2,1,0:T(8,128)(2,1)} %broadcast_in_dim.149), calls=%async_computation.5 | async-start | bytes 1572864 | tf_op jit(solution)/shard_map/all_to_all | solution.py:38
  127.4 19.2 %all-to-all-done.5 = bf16[64,44,128]{2,1,0:T(8,128)(2,1)S(1)} async-done(((bf16[64,44,128]{2,1,0:T(8,128)(2,1)}), bf16[64,44,128]{2,1,0:T(8,128)(2,1)S(1)}, u32[]{:S(2)}, u32[]{:S(2)}) %all-to-all-start.5) | async-done | bytes 720928 | tf_op jit(solution)/shard_map/all_to_all | solution.py:38
  147.3 1.4 convolution_bitcast_fusion.3
  149.4 12.0 %all-to-all-start.6 = ((f32[8,8,128]{2,1,0:T(8,128)}), f32[8,8,128]{2,1,0:T(8,128)}, u32[]{:S(2)}, u32[]{:S(2)}) async-start(f32[8,8,128]{2,1,0:T(8,128)} %broadcast_in_dim.151), calls=%async_computation.6 | async-start | bytes 65536 | tf_op jit(solution)/shard_map/all_to_all | solution.py:38
  162.2 1.3 fusion.45
  164.2 2.3 all-to-all-done.6
  167.9 1.6 multiply_reduce_fusion
  172.0 6.1 %all-to-all-start.7 = ((f32[64,6,128]{2,1,0:T(8,128)}), f32[64,6,128]{2,1,0:T(8,128)S(1)}, u32[]{:S(2)}, u32[]{:S(2)}) async-start(f32[64,6,128]{2,1,0:T(8,128)} %pad_maximum_fusion.1), calls=%async_computation.7 | async-start | bytes 524288 | tf_op jit(solution)/shard_map/all_to_all | solution.py:38
  178.4 11.8 %all-to-all-done.7 = f32[64,6,128]{2,1,0:T(8,128)S(1)} async-done(((f32[64,6,128]{2,1,0:T(8,128)}), f32[64,6,128]{2,1,0:T(8,128)S(1)}, u32[]{:S(2)}, u32[]{:S(2)}) %all-to-all-start.7) | async-done | bytes 196640 | tf_op jit(solution)/shard_map/all_to_all | solution.py:38
  191.7 18.9 %all_to_all.70 = bf16[64,4,128]{2,1,0:T(4,128)(2,1)S(1)} all-to-all(bf16[64,4,128]{2,1,0:T(4,128)(2,1)S(1)} %broadcast_in_dim.157), channel_id=1, replica_groups=mesh['x'=4,'ya'=2,'yb'=2,'yc'=2,'core'=2,'z'=8] {'x','ya','z'}, dimensions={0} | all-to-all | bytes 131072 | tf_op jit(solution)/shard_map/all_to_all | solution.py:38
  212.3 18.7 %all_to_all.71 = f32[64,6,128]{2,1,0:T(8,128)S(1)} all-to-all(f32[64,6,128]{2,1,0:T(8,128)S(1)} %pad_maximum_fusion.2), channel_id=1, replica_groups=mesh['x'=4,'ya'=2,'yb'=2,'yc'=2,'core'=2,'z'=8] {'x','ya','yb','yc','core'}, dimensions={0} | all-to-all | bytes 393216 | tf_op jit(solution)/shard_map/all_to_all | solution.py:38
  231.7 19.0 %all_to_all.72 = bf16[64,4,128]{2,1,0:T(4,128)(2,1)S(1)} all-to-all(bf16[64,4,128]{2,1,0:T(4,128)(2,1)S(1)} %broadcast_in_dim.163), channel_id=1, replica_groups=mesh['x'=4,'ya'=2,'yb'=2,'yc'=2,'core'=2,'z'=8] {'x','ya','z'}, dimensions={0} | all-to-all | bytes 131072 | tf_op jit(solution)/shard_map/all_to_all | solution.py:38
  252.4 18.8 %all_to_all.73 = f32[64,6,128]{2,1,0:T(8,128)S(1)} all-to-all(f32[64,6,128]{2,1,0:T(8,128)S(1)} %pad_maximum_fusion.3), channel_id=1, replica_groups=mesh['x'=4,'ya'=2,'yb'=2,'yc'=2,'core'=2,'z'=8] {'x','ya','yb','yc','core'}, dimensions={0} | all-to-all | bytes 393216 | tf_op jit(solution)/shard_map/all_to_all | solution.py:38
  272.0 14.5 %all_to_all.74 = f32[64,1,128]{2,1,0:T(1,128)S(1)} all-to-all(f32[64,1,128]{2,1,0:T(1,128)S(1)} %broadcast_in_dim.170), channel_id=1, replica_groups=mesh['x'=4,'ya'=2,'yb'=2,'yc'=2,'core'=2,'z'=8] {'yb','yc','core','z'}, dimensions={0} | all-to-all | bytes 65536 | tf_op jit(solution)/shard_map/all_to_all | solution.py:38
  287.6 6.2 %all-to-all-start.13 = ((bf16[64,4,128]{2,1,0:T(4,128)(2,1)}), bf16[64,4,128]{2,1,0:T(4,128)(2,1)S(1)}, u32[]{:S(2)}, u32[]{:S(2)}) async-start(bf16[64,4,128]{2,1,0:T(4,128)(2,1)} %broadcast_in_dim.172), calls=%async_computation.13 | async-start | bytes 131072 | tf_op jit(solution)/shard_map/all_to_all | solution.py:38
  293.8 7.5 %collective-permute-start.1 = (f32[32,128]{1,0:T(8,128)S(1)}, f32[32,128]{1,0:T(8,128)S(1)}, u32[]{:S(2)}, u32[]{:S(2)}) collective-permute-start(f32[32,128]{1,0:T(8,128)S(1)} %copy-done.8), channel_id=1, source_target_pairs={{0,0},{8,64},{16,128},{24,192},{32,256},{40,320},{48,384},{56,448}... | collective-permute-start | bytes 49160 | tf_op jit(solution)/shard_map/ppermute | solution.py:123
  301.2 1.8 collective-permute-done.1
  (180 shorter events, 30.3 us)
Async XLA Ops:
  0.6 30.7 %copy-start = (bf16[128,2048]{1,0:T(8,128)(2,1)S(1)}, bf16[128,2048]{1,0:T(8,128)(2,1)}, u32[]{:S(2)}) copy-start(bf16[128,2048]{1,0:T(8,128)(2,1)} %param.11) | copy-start | bytes 1572868
  2.3 29.4 %copy-start.2 = (bf16[128,2048]{1,0:T(8,128)(2,1)S(1)}, bf16[128,2048]{1,0:T(8,128)(2,1)}, u32[]{:S(2)}) copy-start(bf16[128,2048]{1,0:T(8,128)(2,1)} %param.12) | copy-start | bytes 1572868
  2.3 29.1 %all-to-all-start = ((bf16[64,32,128]{2,1,0:T(8,128)(2,1)}), bf16[64,32,128]{2,1,0:T(8,128)(2,1)S(1)}, u32[]{:S(2)}, u32[]{:S(2)}) async-start(bf16[64,32,128]{2,1,0:T(8,128)(2,1)} %broadcast_in_dim.73), calls=%async_computation | async-start | bytes 1048576 | tf_op jit(solution)/shard_map/all_to_all | solution.py:38
  31.7 11.6 %copy-start.1 = (bf16[256,2048]{1,0:T(8,128)(2,1)S(1)}, bf16[256,2048]{1,0:T(8,128)(2,1)}, u32[]{:S(2)}) copy-start(bf16[256,2048]{1,0:T(8,128)(2,1)} %param.19) | copy-start | bytes 3145732
  33.3 23.7 %all-to-all-start.1 = ((bf16[8,160,128]{2,1,0:T(8,128)(2,1)}), bf16[8,160,128]{2,1,0:T(8,128)(2,1)S(1)}, u32[]{:S(2)}, u32[]{:S(2)}) async-start(bf16[8,160,128]{2,1,0:T(8,128)(2,1)} %broadcast_in_dim.146), calls=%async_computation.1 | async-start | bytes 655360 | tf_op jit(solution)/shard_map/all_to_all | solution.py:38
  64.4 7.3 %copy-start.3 = (f32[1,32,128]{2,1,0:T(8,128)S(1)}, f32[1,32,128]{2,1,0:T(8,128)}, u32[]{:S(2)}) copy-start(f32[1,32,128]{2,1,0:T(8,128)} %param.16) | copy-start | bytes 49156
  65.4 6.3 %copy-start.6 = (f32[1,32,128]{2,1,0:T(8,128)S(1)}, f32[1,32,128]{2,1,0:T(8,128)}, u32[]{:S(2)}) copy-start(f32[1,32,128]{2,1,0:T(8,128)} %param.18) | copy-start | bytes 49156
  65.4 6.3 %copy-start.7 = (f32[1,32,128]{2,1,0:T(8,128)S(1)}, f32[1,32,128]{2,1,0:T(8,128)}, u32[]{:S(2)}) copy-start(f32[1,32,128]{2,1,0:T(8,128)} %param.17) | copy-start | bytes 49156
  65.4 26.0 %all-to-all-start.2 = ((bf16[64,40,128]{2,1,0:T(8,128)(2,1)}), bf16[64,40,128]{2,1,0:T(8,128)(2,1)S(1)}, u32[]{:S(2)}, u32[]{:S(2)}) async-start(bf16[64,40,128]{2,1,0:T(8,128)(2,1)} %pad_maximum_fusion), calls=%async_computation.2 | async-start | bytes 1310720 | tf_op jit(solution)/shard_map/all_to_all | solution.py:38
  71.7 48.4 %collective-permute-start = (f32[96,128]{1,0:T(8,128)S(1)}, f32[96,128]{1,0:T(8,128)S(1)}, u32[]{:S(2)}, u32[]{:S(2)}) collective-permute-start(f32[96,128]{1,0:T(8,128)S(1)} %pad_maximum_fusion.5), channel_id=1, source_target_pairs={{0,0},{8,64},{16,128},{24,192},{32,256},{40,320},{48,384},{56,448}... | collective-permute-start | bytes 147464 | tf_op jit(solution)/shard_map/ppermute | solution.py:72
  80.0 19.7 %copy-start.9 = (f32[256]{0:T(256)}, f32[256]{0:T(256)S(1)}, u32[]{:S(2)}) copy-start(f32[256]{0:T(256)S(1)} %get-tuple-element.13) | copy-start | bytes 3076
  93.3 10.8 %all-to-all-start.3 = ((f32[8,1,128]{2,1,0:T(1,128)}), f32[8,1,128]{2,1,0:T(1,128)S(1)}, u32[]{:S(2)}, u32[]{:S(2)}) async-start(f32[8,1,128]{2,1,0:T(1,128)} %broadcast_in_dim_broadcast_in_dim_broadcast_in_dim.3), calls=%async_computation.3 | async-start | bytes 8192 | tf_op jit(solution)/shard_map/all_to_all | solution.py:38
  99.6 22.2 %copy-start.4 = (f32[2,256]{1,0:T(2,128)}, f32[2,256]{1,0:T(2,128)S(1)}, u32[]{:S(2)}) copy-start(f32[2,256]{1,0:T(2,128)S(1)} %reshape.238) | copy-start | bytes 6148
  104.8 15.3 %all-to-all-start.4 = ((f32[64,1,128]{2,1,0:T(1,128)}), f32[64,1,128]{2,1,0:T(1,128)S(1)}, u32[]{:S(2)}, u32[]{:S(2)}) async-start(f32[64,1,128]{2,1,0:T(1,128)} %broadcast_in_dim.147), calls=%async_computation.4 | async-start | bytes 65536 | tf_op jit(solution)/shard_map/all_to_all | solution.py:38
  121.8 24.7 %all-to-all-start.5 = ((bf16[64,44,128]{2,1,0:T(8,128)(2,1)}), bf16[64,44,128]{2,1,0:T(8,128)(2,1)S(1)}, u32[]{:S(2)}, u32[]{:S(2)}) async-start(bf16[64,44,128]{2,1,0:T(8,128)(2,1)} %broadcast_in_dim.149), calls=%async_computation.5 | async-start | bytes 1572864 | tf_op jit(solution)/shard_map/all_to_all | solution.py:38
  149.4 17.1 %all-to-all-start.6 = ((f32[8,8,128]{2,1,0:T(8,128)}), f32[8,8,128]{2,1,0:T(8,128)}, u32[]{:S(2)}, u32[]{:S(2)}) async-start(f32[8,8,128]{2,1,0:T(8,128)} %broadcast_in_dim.151), calls=%async_computation.6 | async-start | bytes 65536 | tf_op jit(solution)/shard_map/all_to_all | solution.py:38
  169.5 1.2 copy-start.11
  169.5 1.4 copy-start.13
  172.0 18.5 %copy-start.5 = (f32[2,256]{1,0:T(2,128)S(1)}, f32[2,256]{1,0:T(2,128)}, u32[]{:S(2)}) copy-start(f32[2,256]{1,0:T(2,128)} %copy-done.4) | copy-start | bytes 6148
  172.0 18.5 %copy-start.10 = (f32[256]{0:T(256)S(1)}, f32[256]{0:T(256)}, u32[]{:S(2)}) copy-start(f32[256]{0:T(256)} %copy-done.9) | copy-start | bytes 3076
  172.0 18.1 %all-to-all-start.7 = ((f32[64,6,128]{2,1,0:T(8,128)}), f32[64,6,128]{2,1,0:T(8,128)S(1)}, u32[]{:S(2)}, u32[]{:S(2)}) async-start(f32[64,6,128]{2,1,0:T(8,128)} %pad_maximum_fusion.1), calls=%async_computation.7 | async-start | bytes 524288 | tf_op jit(solution)/shard_map/all_to_all | solution.py:38
  178.1 32.5 %copy-start.12 = (f32[2,128]{1,0:T(2,128)S(1)}, f32[2,128]{1,0:T(2,128)}, u32[]{:S(2)}) copy-start(f32[2,128]{1,0:T(2,128)} %get-tuple-element.23) | copy-start | bytes 3076
  251.6 42.2 %copy-start.8 = (f32[32,128]{1,0:T(8,128)S(1)}, f32[32,128]{1,0:T(8,128)}, u32[]{:S(2)}) copy-start(f32[32,128]{1,0:T(8,128)} %get-tuple-element.15) | copy-start | bytes 49156
  287.6 16.0 %all-to-all-start.13 = ((bf16[64,4,128]{2,1,0:T(4,128)(2,1)}), bf16[64,4,128]{2,1,0:T(4,128)(2,1)S(1)}, u32[]{:S(2)}, u32[]{:S(2)}) async-start(bf16[64,4,128]{2,1,0:T(4,128)(2,1)} %broadcast_in_dim.172), calls=%async_computation.13 | async-start | bytes 131072 | tf_op jit(solution)/shard_map/all_to_all | solution.py:38
  293.8 9.3 %collective-permute-start.1 = (f32[32,128]{1,0:T(8,128)S(1)}, f32[32,128]{1,0:T(8,128)S(1)}, u32[]{:S(2)}, u32[]{:S(2)}) collective-permute-start(f32[32,128]{1,0:T(8,128)S(1)} %copy-done.8), channel_id=1, source_target_pairs={{0,0},{8,64},{16,128},{24,192},{32,256},{40,320},{48,384},{56,448}... | collective-permute-start | bytes 49160 | tf_op jit(solution)/shard_map/ppermute | solution.py:123

commit v3 on v2

v3 whole, which is shorter than its diff:
```python
import math

import jax
import jax.numpy as jnp
from jax import lax
from jax.sharding import Mesh
from jax.sharding import PartitionSpec as P

MODEL_WIDTH = 16384
SEQLEN = 128
GROUP = 8
DECODE_STEPS = 4
RANK = 64
BATCH = 16
BLOCK = 2048
TILE = 256
OWN = 32

adapter_alpha = 2.0
beta_one = 0.9
beta_two = 0.999
rate = 0.1
adam_count = 200.0
scale = adapter_alpha / (RANK * math.sqrt(MODEL_WIDTH))

bf16 = jnp.bfloat16
f32 = jnp.float32
HIGHEST = lax.Precision.HIGHEST

AXES = ("x", "ya", "yb", "yc", "core", "z")
DP = ("x", "ya", "yb", "yc", "core")
Y = ("ya", "yb", "yc")
XY = ("x", "ya", "yb", "yc")


def swap(chunks, axes):
    return lax.all_to_all(chunks, axes, 0, 0, tiled=False)


def share(piece, axes, count):
    return swap(jnp.broadcast_to(piece[None], (count,) + piece.shape), axes)


def core_swap(value):
    return lax.ppermute(value, "core", [(0, 1), (1, 0)])


def high_low(value):
    high = lax.reduce_precision(value, 8, 7)
    return high.astype(bf16), (value - high).astype(bf16)


def pick(value, index, axis):
    return lax.dynamic_index_in_dim(value, index, axis, keepdims=False)


def body(
    tokens,
    cotangent,
    prompt_len,
    resp_len,
    ranks,
    factors,
    first_moment,
    second_moment,
    base_weight,
    gain,
    state,
):
    x = lax.axis_index("x")
    y = lax.axis_index(Y)
    core = lax.axis_index("core")
    z = lax.axis_index("z")
    major = lax.axis_index(("x", "ya"))
    minor = lax.axis_index(("yb", "yc", "core"))
    part = x * 2 + core

    rows = lax.all_gather(base_weight, Y, axis=0, tiled=True)

    there = [(c * 8 + r, r * 2 + c) for r in range(8) for c in range(2)]
    back = [(b, a) for a, b in there]
    old = lax.ppermute(
        jnp.concatenate([factors[0], first_moment[0], second_moment[0]], axis=0), Y + ("core",), there
    )

    positions = jnp.arange(SEQLEN, dtype=jnp.int32)
    lower = prompt_len[:, None]
    upper = lower + resp_len[:, None]
    inside = (positions[None, :] >= lower) & (positions[None, :] < upper)
    advantage = (2 * ranks - (GROUP - 1)).astype(f32) / (GROUP - 1)
    per_seq = advantage / resp_len.astype(f32)
    weight = jnp.where(inside, per_seq[:, None], f32(0.0)).reshape(-1)
    weighted = (cotangent.astype(f32) * weight[:, None]).astype(bf16)

    mine = share(factors[0].astype(bf16), XY, 32)
    other = core_swap(mine)
    low = jnp.where(core == 0, jnp.stack([mine, other], 1), jnp.stack([other, mine], 1))
    low = low.reshape(BLOCK, 2 * RANK)
    hidden = jnp.dot(tokens, low[:, :RANK], preferred_element_type=f32)
    projected = jnp.dot(weighted, low[:, RANK:], preferred_element_type=f32)
    state_tile = lax.dynamic_slice_in_dim(state, minor * TILE, TILE, 1)
    sent = jnp.concatenate(
        [jnp.concatenate([hidden, projected], axis=1).astype(bf16), state_tile.reshape(32, 128)],
        axis=0,
    )
    got = share(sent, "z", 8)
    both = jnp.sum(got[:, :SEQLEN].astype(f32), axis=0).astype(bf16)
    first = pick(got[:, SEQLEN:], major, 0).reshape(BATCH, TILE)

    dims = (((0,), (0,)), ((), ()))
    grad_down = lax.dot_general(tokens, both[:, RANK:], dims, preferred_element_type=f32)
    grad_up = lax.dot_general(weighted, both[:, :RANK], dims, preferred_element_type=f32)
    grads = jnp.concatenate([grad_down, grad_up], axis=1).astype(bf16).reshape(4, 2, 8, OWN, 128)
    first = jnp.dot(first, base_weight, preferred_element_type=f32)
    first = first.reshape(8, 2, 4, 2, TILE)

    def half(which):
        base = pick(first, which, 3).transpose(2, 0, 1, 3).reshape(32, 4, 128)
        return pick(grads, which, 1).reshape(32, OWN, 128), base

    give, give_base = half(1 - core)
    keep, keep_base = half(core)
    got = core_swap(jnp.concatenate([give, *high_low(give_base)], axis=1)).astype(f32)
    keep = (keep.astype(f32) + got[:, :OWN]).astype(bf16)
    keep_base = keep_base + got[:, OWN : OWN + 4] + got[:, OWN + 4 :]
    pieces = swap(jnp.concatenate([keep, *high_low(keep_base)], axis=1), XY).astype(f32)
    pieces = jnp.sum(pieces, axis=0)
    grads = scale * pieces[:OWN]
    own_state = lax.dynamic_slice(state, (2 * y, part * TILE), (2, TILE))
    own_base = (pieces[OWN : OWN + 4] + pieces[OWN + 4 :]).reshape(2, TILE)
    own_base = own_base + own_state.astype(f32)

    squared = jnp.broadcast_to(jnp.sum(grads * grads), (1, 128))
    squared = jnp.sum(share(squared, ("yb", "yc", "core", "z"), 64), axis=0)
    squared = jnp.sum(share(squared, ("x", "ya"), 8), axis=0)
    clip = jnp.minimum(f32(1.0), f32(1.0) / (jnp.sqrt(squared) + 1e-06))
    grads = clip * grads
    moment_one = beta_one * old[OWN : 2 * OWN] + (1.0 - beta_one) * grads
    moment_two = beta_two * old[2 * OWN :] + (1.0 - beta_two) * grads * grads
    step_size = (
        moment_one
        / (1.0 - beta_one**adam_count)
        / (jnp.sqrt(moment_two / (1.0 - beta_two**adam_count)) + 1e-08)
    )
    updated = old[:OWN] - rate * step_size
    new_factors = lax.ppermute(updated, Y + ("core",), back)[None]

    near = share(updated.astype(bf16), Y, 8).reshape(TILE, 2 * RANK)
    down = near[:, :RANK]
    up = near[:, RANK:].astype(f32).T
    own_gain = lax.dynamic_slice_in_dim(gain, part * TILE, TILE, 0)

    def spread(pair):
        return jnp.broadcast_to(pair[:, None], (2, 64)).reshape(1, 128)

    thin = jnp.dot(own_state, down, preferred_element_type=f32).reshape(1, 128)
    thin = jnp.sum(share(thin, ("x", "core", "z"), 64), axis=0).reshape(2, RANK)
    resid = own_base + scale * jnp.dot(thin, up, precision=HIGHEST)

    for step in range(1, DECODE_STEPS):
        own = (resid * own_gain).astype(bf16)
        thin = jnp.dot(own, down, preferred_element_type=f32).reshape(1, 128)
        pairs = jnp.concatenate([thin, spread(jnp.sum(resid * resid, axis=1))], axis=0)
        sent = jnp.concatenate([own.reshape(4, 128), *high_low(pairs)], axis=0)
        got = share(sent, ("x", "z"), 32).reshape(4, 8, 8, 128)
        current = pick(got[:, :, :4].reshape(4, 4, 2, 2, TILE), x, 1)
        current = current.transpose(2, 1, 0, 3).reshape(2, BLOCK)
        pairs = jnp.sum(got[:, :, 4:].astype(f32), axis=(0, 1))
        pairs = 0.25 * (pairs[:2] + pairs[2:])
        sums = jnp.dot(current, rows, preferred_element_type=f32)
        sums = sums.reshape(2, 8, TILE).transpose(1, 0, 2).reshape(8, 4, 128)
        sent = jnp.concatenate([sums, jnp.broadcast_to(pairs[None], (8, 2, 128))], axis=1)
        got = jnp.sum(swap(sent, ("x", "core")), axis=0)
        thin = got[4].reshape(2, RANK)
        norm = lax.rsqrt(got[5].reshape(2, 64)[:, :1] / MODEL_WIDTH + 1e-05)
        total = own.astype(f32) + got[:4].reshape(2, TILE)
        resid = norm * (total + scale * jnp.dot(thin, up, precision=HIGHEST))

    sums = jnp.sum(share(spread(jnp.sum(resid * resid, axis=1)), ("x", "core", "z"), 64), axis=0)
    norm = lax.rsqrt(sums.reshape(2, 64)[:, :1] / MODEL_WIDTH + 1e-05)
    own = (resid * norm * own_gain).astype(bf16)
    result = share(own.reshape(4, 128), DP, 64).reshape(4, 8, 2, 2, TILE)
    result = result.transpose(1, 3, 0, 2, 4).reshape(BATCH, BLOCK)
    return (new_factors, result)


def solution(mesh):
    fine = Mesh(mesh.devices.reshape(4, 2, 2, 2, 2, 8), AXES)
    return jax.shard_map(
        body,
        mesh=fine,
        in_specs=(
            P(DP, "z"),
            P(DP, "z"),
            P(DP),
            P(DP),
            P(DP),
            P("z", DP, None),
            P("z", DP, None),
            P("z", DP, None),
            P(DP, "z"),
            P("z"),
            P(None, "z"),
        ),
        out_specs=(P("z", DP, None), P(None, "z")),
        check_vma=False,
    )
```

time: 306 us -> 294 us (0.961)
  waiting for transfers between devices: 88.9 us -> 48 us
  blocking collectives: 90 us -> 120 us
  starting transfers between devices: 82.9 us -> 56.1 us
  between operations: 3.21 us -> 16.7 us
  matrix products: 9.97 us -> 23.4 us
  other arithmetic: 12 us -> 3.09 us
  local copies, waits for them, and re-layouts: 18 us -> 24.6 us
    all_to_all x9 -> x6, waiting for transfers between devices: 87.1 us -> 43.3 us  [swap(): return lax.all_to_all(chunks, axes, 0, 0, tiled=False)]
    all_to_all x9 -> x6, starting transfers between devices: 68 us -> 37 us  [swap(): return lax.all_to_all(chunks, axes, 0, 0, tiled=False)]
    all_to_all x5 -> x9, blocking collectives: 90 us -> 120 us  [swap(): return lax.all_to_all(chunks, axes, 0, 0, tiled=False)]
    dot_general x13 -> x12, matrix products: 6.97 us -> 20.7 us  [the longest x3 16.9 us: body(): sums = jnp.dot(current, rows, preferred_element_type=f32)]
    dot_general x4 -> x3, local copies, waits for them, and re-layouts: 0.57 us -> 13.9 us  [the longest x1 12.4 us: body(): sums = jnp.dot(current, rows, preferred_element_type=f32)]
    ppermute x1 -> x3, starting transfers between devices: 7.45 us -> 15.5 us  [the longest x2 7.99 us: core_swap(): return lax.ppermute(value, 'core', [(0, 1), (1, 0)])]
    ppermute x1, starting transfers between devices: 7.45 us -> 3.61 us  [body(): lax.ppermute(jnp.concatenate([factors[0], first_moment[0], second_moment[...]
  transfers between devices with their start and end apart: 11 -> 11, of which waited for: 10 -> 9; matrix products, arithmetic and copies ran while one was open for 3% -> 5% of each run, Pallas kernels for 0% -> 0%
where the time goes in v3:
time: 294 us; the launch traced here: 292 us
  blocking collectives  120 us (41%)
  starting transfers between devices  56.1 us (19%)
  waiting for transfers between devices  48 us (16%)
  local copies, waits for them, and re-layouts  24.6 us (8%)
  matrix products  23.4 us (8%)
  between operations  16.7 us (6%)
  other arithmetic  3.09 us (1%)
    all_to_all x9, blocking collectives, swap(): return lax.all_to_all(chunks, axes, 0, 0, tiled=False)  120 us
    all_to_all x6, waiting for transfers between devices, swap(): return lax.all_to_all(chunks, axes, 0, 0, tiled=False)  43.3 us
    all_to_all x6, starting transfers between devices, swap(): return lax.all_to_all(chunks, axes, 0, 0, tiled=False)  37 us
    dot_general x3, matrix products, body(): sums = jnp.dot(current, rows, preferred_element_type=f32)  16.9 us
    dot_general x1, local copies, waits for them, and re-layouts, body(): sums = jnp.dot(current, rows, preferred_element_type=f32)  12.4 us
    ppermute x2, starting transfers between devices, core_swap(): return lax.ppermute(value, 'core', [(0, 1), (1, 0)])  7.99 us
    ppermute x1, starting transfers between devices, body(): new_factors = lax.ppermute(updated, Y + ('core',), back)[None]  7.49 us
  transfers between devices with their start and end apart: 11, of which 9 were waited for; matrix products, arithmetic and copies ran while one was open for 5% of the time, Pallas kernels for 0%

profile of v3, /device:TPU:1, one launch (start us, length us, event | category | flops | bytes accessed | tf_op | source)
XLA Modules:
  0.0 292.0 jit_solution(2037372832107310179)
XLA Ops:
  8.7 20.0 %all_to_all.75 = bf16[32,32,128]{2,1,0:T(8,128)(2,1)S(1)} all-to-all(bf16[32,32,128]{2,1,0:T(8,128)(2,1)S(1)} %broadcast_in_dim.59), channel_id=1, replica_groups=mesh['x'=4,'ya'=2,'yb'=2,'yc'=2,'core'=2,'z'=8] {'x','ya','yb','yc'}, dimensions={0} | all-to-all | bytes 524288 | tf_op jit(solution)/shard_map/all_to_all | solution.py:37
  28.7 5.6 %collective-permute-start.1 = (bf16[32,32,128]{2,1,0:T(8,128)(2,1)S(1)}, bf16[32,32,128]{2,1,0:T(8,128)(2,1)S(1)}, u32[]{:S(2)}, u32[]{:S(2)}) collective-permute-start(bf16[32,32,128]{2,1,0:T(8,128)(2,1)S(1)} %all_to_all.75), channel_id=1, source_target_pairs={{0,8},{8,0},{1,9},{9,1},{2,10},{10,2},{3,11},{11,3},{4,12},{12,4},... | collective-permute-start | bytes 786440 | tf_op jit(solution)/shard_map/ppermute | solution.py:45
  37.6 1.7 convolution_convert_fusion.2
  40.3 10.1 %all-to-all-start.1 = ((bf16[8,160,128]{2,1,0:T(8,128)(2,1)}), bf16[8,160,128]{2,1,0:T(8,128)(2,1)S(1)}, u32[]{:S(2)}, u32[]{:S(2)}) async-start(bf16[8,160,128]{2,1,0:T(8,128)(2,1)} %broadcast_in_dim.63), calls=%async_computation.1 | async-start | bytes 655360 | tf_op jit(solution)/shard_map/all_to_all | solution.py:37
  50.3 1.5 copy.69
  51.8 12.3 %all-to-all-done.1 = bf16[8,160,128]{2,1,0:T(8,128)(2,1)S(1)} async-done(((bf16[8,160,128]{2,1,0:T(8,128)(2,1)}), bf16[8,160,128]{2,1,0:T(8,128)(2,1)S(1)}, u32[]{:S(2)}, u32[]{:S(2)}) %all-to-all-start.1) | async-done | bytes 327712 | tf_op jit(solution)/shard_map/all_to_all | solution.py:37
  66.3 2.4 collective-permute-start.2
  70.2 19.4 %all_to_all.76 = bf16[32,40,128]{2,1,0:T(8,128)(2,1)S(1)} all-to-all(bf16[32,40,128]{2,1,0:T(8,128)(2,1)S(1)} %pad_maximum_fusion.1), channel_id=1, replica_groups=mesh['x'=4,'ya'=2,'yb'=2,'yc'=2,'core'=2,'z'=8] {'x','ya','yb','yc'}, dimensions={0} | all-to-all | bytes 655360 | tf_op jit(solution)/shard_map/all_to_all | solution.py:37
  90.9 16.7 %all_to_all.77 = f32[64,1,128]{2,1,0:T(1,128)S(1)} all-to-all(f32[64,1,128]{2,1,0:T(1,128)S(1)} %broadcast_in_dim_broadcast_in_dim_broadcast_in_dim.3), channel_id=1, replica_groups=mesh['x'=4,'ya'=2,'yb'=2,'yc'=2,'core'=2,'z'=8] {'yb','yc','core','z'}, dimensions={0} | all-to-all | bytes 65536 | tf_op jit(solution)/shard_map/all_to_all | solution.py:37
  108.2 4.6 %all-to-all-start.4 = ((f32[8,1,128]{2,1,0:T(1,128)}), f32[8,1,128]{2,1,0:T(1,128)S(1)}, u32[]{:S(2)}, u32[]{:S(2)}) async-start(f32[8,1,128]{2,1,0:T(1,128)} %broadcast_in_dim.64), calls=%async_computation.4 | async-start | bytes 8192 | tf_op jit(solution)/shard_map/all_to_all | solution.py:37
  112.8 3.6 %collective-permute-start = (f32[96,128]{1,0:T(8,128)S(1)}, f32[96,128]{1,0:T(8,128)S(1)}, u32[]{:S(2)}, u32[]{:S(2)}) collective-permute-start(f32[96,128]{1,0:T(8,128)S(1)} %pad_maximum_fusion.3), channel_id=1, source_target_pairs={{0,0},{64,8},{8,16},{72,24},{16,32},{80,40},{24,48},{88,56},{32,64... | collective-permute-start | bytes 147464 | tf_op jit(solution)/shard_map/ppermute | solution.py:82
  116.4 5.2 %all-to-all-done.4 = f32[8,1,128]{2,1,0:T(1,128)S(1)} async-done(((f32[8,1,128]{2,1,0:T(1,128)}), f32[8,1,128]{2,1,0:T(1,128)S(1)}, u32[]{:S(2)}, u32[]{:S(2)}) %all-to-all-start.4) | async-done | bytes 4128 | tf_op jit(solution)/shard_map/all_to_all | solution.py:37
  121.6 2.0 collective-permute-done
  124.3 3.4 %all-to-all-start.5 = ((bf16[8,32,128]{2,1,0:T(8,128)(2,1)}), bf16[8,32,128]{2,1,0:T(8,128)(2,1)S(1)}, u32[]{:S(2)}, u32[]{:S(2)}) async-start(bf16[8,32,128]{2,1,0:T(8,128)(2,1)} %broadcast_in_dim.66), calls=%async_computation.5 | async-start | bytes 131072 | tf_op jit(solution)/shard_map/all_to_all | solution.py:37
  128.4 6.4 %all-to-all-done.5 = bf16[8,32,128]{2,1,0:T(8,128)(2,1)S(1)} async-done(((bf16[8,32,128]{2,1,0:T(8,128)(2,1)}), bf16[8,32,128]{2,1,0:T(8,128)(2,1)S(1)}, u32[]{:S(2)}, u32[]{:S(2)}) %all-to-all-start.5) | async-done | bytes 65568 | tf_op jit(solution)/shard_map/all_to_all | solution.py:37
  136.4 10.2 %all-to-all-start.6 = ((f32[64,1,128]{2,1,0:T(1,128)}), f32[64,1,128]{2,1,0:T(1,128)S(1)}, u32[]{:S(2)}, u32[]{:S(2)}) async-start(f32[64,1,128]{2,1,0:T(1,128)} %broadcast_in_dim.68), calls=%async_computation.6 | async-start | bytes 65536 | tf_op jit(solution)/shard_map/all_to_all | solution.py:37
  146.6 9.1 %all-to-all-done.6 = f32[64,1,128]{2,1,0:T(1,128)S(1)} async-done(((f32[64,1,128]{2,1,0:T(1,128)}), f32[64,1,128]{2,1,0:T(1,128)S(1)}, u32[]{:S(2)}, u32[]{:S(2)}) %all-to-all-start.6) | async-done | bytes 32800 | tf_op jit(solution)/shard_map/all_to_all | solution.py:37
  158.0 3.9 %all-to-all-start.7 = ((bf16[32,8,128]{2,1,0:T(8,128)(2,1)}), bf16[32,8,128]{2,1,0:T(8,128)(2,1)S(1)}, u32[]{:S(2)}, u32[]{:S(2)}) async-start(bf16[32,8,128]{2,1,0:T(8,128)(2,1)} %broadcast_in_dim.70), calls=%async_computation.7 | async-start | bytes 131072 | tf_op jit(solution)/shard_map/all_to_all | solution.py:37
  161.8 8.9 %all-to-all-done.7 = bf16[32,8,128]{2,1,0:T(8,128)(2,1)S(1)} async-done(((bf16[32,8,128]{2,1,0:T(8,128)(2,1)}), bf16[32,8,128]{2,1,0:T(8,128)(2,1)S(1)}, u32[]{:S(2)}, u32[]{:S(2)}) %all-to-all-start.7) | async-done | bytes 65568 | tf_op jit(solution)/shard_map/all_to_all | solution.py:37
  170.9 12.4 %copy.61 = bf16[2048,2048]{1,0:T(8,128)(2,1)} copy(bf16[2048,2048]{0,1:T(8,128)(2,1)} %bitcast.84) | data formatting | bytes 16777216 | tf_op jit(solution)/shard_map/dot_general | solution.py:170
  183.2 5.6 %convolution_bitcast_fusion.2 = f32[8,2,256]{2,1,0:T(2,128)S(1)} fusion(bf16[2,2048,1]{1,0,2:T(2,128)(2,1)S(1)} %reshape.234, bf16[8,256,2048]{2,1,0:T(8,128)(2,1)} %bitcast.81), kind=kOutput, calls=%fused_computation.8 | convolution fusion | flops 16777216 | bytes 8413184 | tf_op jit(solution)/shard_map/dot_general | solution.py:170
  188.9 9.1 %all_to_all.78 = f32[8,6,128]{2,1,0:T(8,128)S(1)} all-to-all(f32[8,6,128]{2,1,0:T(8,128)S(1)} %pad_maximum_fusion.4), channel_id=1, replica_groups=mesh['x'=4,'ya'=2,'yb'=2,'yc'=2,'core'=2,'z'=8] {'x','core'}, dimensions={0} | all-to-all | bytes 49152 | tf_op jit(solution)/shard_map/all_to_all | solution.py:37
  199.2 11.8 %all_to_all.79 = bf16[32,8,128]{2,1,0:T(8,128)(2,1)S(1)} all-to-all(bf16[32,8,128]{2,1,0:T(8,128)(2,1)S(1)} %broadcast_in_dim.73), channel_id=1, replica_groups=mesh['x'=4,'ya'=2,'yb'=2,'yc'=2,'core'=2,'z'=8] {'x','z'}, dimensions={0} | all-to-all | bytes 131072 | tf_op jit(solution)/shard_map/all_to_all | solution.py:37
  211.2 5.6 %convolution_bitcast_fusion.1 = f32[8,2,256]{2,1,0:T(2,128)S(1)} fusion(bf16[2,2048,1]{1,0,2:T(2,128)(2,1)S(1)} %reshape.235, bf16[8,256,2048]{2,1,0:T(8,128)(2,1)} %bitcast.82), kind=kOutput, calls=%fused_computation.7 | convolution fusion | flops 16777216 | bytes 8413184 | tf_op jit(solution)/shard_map/dot_general | solution.py:170
  216.9 9.1 %all_to_all.80 = f32[8,6,128]{2,1,0:T(8,128)S(1)} all-to-all(f32[8,6,128]{2,1,0:T(8,128)S(1)} %pad_maximum_fusion.5), channel_id=1, replica_groups=mesh['x'=4,'ya'=2,'yb'=2,'yc'=2,'core'=2,'z'=8] {'x','core'}, dimensions={0} | all-to-all | bytes 49152 | tf_op jit(solution)/shard_map/all_to_all | solution.py:37
  227.1 11.8 %all_to_all.81 = bf16[32,8,128]{2,1,0:T(8,128)(2,1)S(1)} all-to-all(bf16[32,8,128]{2,1,0:T(8,128)(2,1)S(1)} %broadcast_in_dim.76), channel_id=1, replica_groups=mesh['x'=4,'ya'=2,'yb'=2,'yc'=2,'core'=2,'z'=8] {'x','z'}, dimensions={0} | all-to-all | bytes 131072 | tf_op jit(solution)/shard_map/all_to_all | solution.py:37
  239.1 5.6 %convolution_bitcast_fusion = f32[8,2,256]{2,1,0:T(2,128)S(1)} fusion(bf16[2,2048,1]{1,0,2:T(2,128)(2,1)S(1)} %reshape.236, bf16[8,256,2048]{2,1,0:T(8,128)(2,1)} %bitcast.83), kind=kOutput, calls=%fused_computation.6 | convolution fusion | flops 16777216 | bytes 8413184 | tf_op jit(solution)/shard_map/dot_general | solution.py:170
  244.8 9.1 %all_to_all.82 = f32[8,6,128]{2,1,0:T(8,128)S(1)} all-to-all(f32[8,6,128]{2,1,0:T(8,128)S(1)} %pad_maximum_fusion.6), channel_id=1, replica_groups=mesh['x'=4,'ya'=2,'yb'=2,'yc'=2,'core'=2,'z'=8] {'x','core'}, dimensions={0} | all-to-all | bytes 49152 | tf_op jit(solution)/shard_map/all_to_all | solution.py:37
  254.8 13.3 %all_to_all.83 = f32[64,1,128]{2,1,0:T(1,128)S(1)} all-to-all(f32[64,1,128]{2,1,0:T(1,128)S(1)} %broadcast_in_dim.80), channel_id=1, replica_groups=mesh['x'=4,'ya'=2,'yb'=2,'yc'=2,'core'=2,'z'=8] {'x','core','z'}, dimensions={0} | all-to-all | bytes 65536 | tf_op jit(solution)/shard_map/all_to_all | solution.py:37
  269.0 4.9 %all-to-all-start.14 = ((bf16[64,4,128]{2,1,0:T(4,128)(2,1)}), bf16[64,4,128]{2,1,0:T(4,128)(2,1)S(1)}, u32[]{:S(2)}, u32[]{:S(2)}) async-start(bf16[64,4,128]{2,1,0:T(4,128)(2,1)} %broadcast_in_dim.82), calls=%async_computation.14 | async-start | bytes 131072 | tf_op jit(solution)/shard_map/all_to_all | solution.py:37
  273.9 7.5 %collective-permute-start.3 = (f32[32,128]{1,0:T(8,128)S(1)}, f32[32,128]{1,0:T(8,128)S(1)}, u32[]{:S(2)}, u32[]{:S(2)}) collective-permute-start(f32[32,128]{1,0:T(8,128)S(1)} %get-tuple-element.9), channel_id=1, source_target_pairs={{0,0},{8,64},{16,8},{24,72},{32,16},{40,80},{48,24},{56,88},{64,32... | collective-permute-start | bytes 49160 | tf_op jit(solution)/shard_map/ppermute | solution.py:146
  282.3 1.5 all-to-all-done.14
  (158 shorter events, 21.3 us)
Async XLA Ops:
  7.2 30.1 %copy-start = (bf16[128,2048]{1,0:T(8,128)(2,1)S(1)}, bf16[128,2048]{1,0:T(8,128)(2,1)}, u32[]{:S(2)}) copy-start(bf16[128,2048]{1,0:T(8,128)(2,1)} %param.11) | copy-start | bytes 1572868
  7.2 57.6 %copy-start.1 = (bf16[128,2048]{1,0:T(8,128)(2,1)S(1)}, bf16[128,2048]{1,0:T(8,128)(2,1)}, u32[]{:S(2)}) copy-start(bf16[128,2048]{1,0:T(8,128)(2,1)} %param.12) | copy-start | bytes 1572868
  7.2 163.7 %all-gather.2.cloned.1.call-start = ((), (), s32[]{:S(2)}) async-start(), calls=%async_computation.15 | async-start | bytes 9437184 | tf_op jit(solution)/shard_map/all_gather | solution.py:78
  28.7 8.5 %collective-permute-start.1 = (bf16[32,32,128]{2,1,0:T(8,128)(2,1)S(1)}, bf16[32,32,128]{2,1,0:T(8,128)(2,1)S(1)}, u32[]{:S(2)}, u32[]{:S(2)}) collective-permute-start(bf16[32,32,128]{2,1,0:T(8,128)(2,1)S(1)} %all_to_all.75), channel_id=1, source_target_pairs={{0,8},{8,0},{1,9},{9,1},{2,10},{10,2},{3,11},{11,3},{4,12},{12,4},... | collective-permute-start | bytes 786440 | tf_op jit(solution)/shard_map/ppermute | solution.py:45
  37.6 75.1 %copy-start.2 = (f32[1,32,128]{2,1,0:T(8,128)S(1)}, f32[1,32,128]{2,1,0:T(8,128)}, u32[]{:S(2)}) copy-start(f32[1,32,128]{2,1,0:T(8,128)} %param.16) | copy-start | bytes 49156
  37.6 75.1 %copy-start.3 = (f32[1,32,128]{2,1,0:T(8,128)S(1)}, f32[1,32,128]{2,1,0:T(8,128)}, u32[]{:S(2)}) copy-start(f32[1,32,128]{2,1,0:T(8,128)} %param.18) | copy-start | bytes 49156
  37.6 75.1 %copy-start.4 = (f32[1,32,128]{2,1,0:T(8,128)S(1)}, f32[1,32,128]{2,1,0:T(8,128)}, u32[]{:S(2)}) copy-start(f32[1,32,128]{2,1,0:T(8,128)} %param.17) | copy-start | bytes 49156
  40.3 23.8 %all-to-all-start.1 = ((bf16[8,160,128]{2,1,0:T(8,128)(2,1)}), bf16[8,160,128]{2,1,0:T(8,128)(2,1)S(1)}, u32[]{:S(2)}, u32[]{:S(2)}) async-start(bf16[8,160,128]{2,1,0:T(8,128)(2,1)} %broadcast_in_dim.63), calls=%async_computation.1 | async-start | bytes 655360 | tf_op jit(solution)/shard_map/all_to_all | solution.py:37
  66.3 3.6 %collective-permute-start.2 = (bf16[32,40,128]{2,1,0:T(8,128)(2,1)S(1)}, bf16[32,40,128]{2,1,0:T(8,128)(2,1)S(1)}, u32[]{:S(2)}, u32[]{:S(2)}) collective-permute-start(bf16[32,40,128]{2,1,0:T(8,128)(2,1)S(1)} %pad_maximum_fusion), channel_id=1, source_target_pairs={{0,8},{8,0},{1,9},{9,1},{2,10},{10,2},{3,11},{11,3},{4,12},{12,4},... | collective-permute-start | bytes 983048 | tf_op jit(solution)/shard_map/ppermute | solution.py:45
  108.2 13.4 %all-to-all-start.4 = ((f32[8,1,128]{2,1,0:T(1,128)}), f32[8,1,128]{2,1,0:T(1,128)S(1)}, u32[]{:S(2)}, u32[]{:S(2)}) async-start(f32[8,1,128]{2,1,0:T(1,128)} %broadcast_in_dim.64), calls=%async_computation.4 | async-start | bytes 8192 | tf_op jit(solution)/shard_map/all_to_all | solution.py:37
  112.8 10.8 %collective-permute-start = (f32[96,128]{1,0:T(8,128)S(1)}, f32[96,128]{1,0:T(8,128)S(1)}, u32[]{:S(2)}, u32[]{:S(2)}) collective-permute-start(f32[96,128]{1,0:T(8,128)S(1)} %pad_maximum_fusion.3), channel_id=1, source_target_pairs={{0,0},{64,8},{8,16},{72,24},{16,32},{80,40},{24,48},{88,56},{32,64... | collective-permute-start | bytes 147464 | tf_op jit(solution)/shard_map/ppermute | solution.py:82
  124.3 10.5 %all-to-all-start.5 = ((bf16[8,32,128]{2,1,0:T(8,128)(2,1)}), bf16[8,32,128]{2,1,0:T(8,128)(2,1)S(1)}, u32[]{:S(2)}, u32[]{:S(2)}) async-start(bf16[8,32,128]{2,1,0:T(8,128)(2,1)} %broadcast_in_dim.66), calls=%async_computation.5 | async-start | bytes 131072 | tf_op jit(solution)/shard_map/all_to_all | solution.py:37
  136.4 19.4 %all-to-all-start.6 = ((f32[64,1,128]{2,1,0:T(1,128)}), f32[64,1,128]{2,1,0:T(1,128)S(1)}, u32[]{:S(2)}, u32[]{:S(2)}) async-start(f32[64,1,128]{2,1,0:T(1,128)} %broadcast_in_dim.68), calls=%async_computation.6 | async-start | bytes 65536 | tf_op jit(solution)/shard_map/all_to_all | solution.py:37
  158.0 12.7 %all-to-all-start.7 = ((bf16[32,8,128]{2,1,0:T(8,128)(2,1)}), bf16[32,8,128]{2,1,0:T(8,128)(2,1)S(1)}, u32[]{:S(2)}, u32[]{:S(2)}) async-start(bf16[32,8,128]{2,1,0:T(8,128)(2,1)} %broadcast_in_dim.70), calls=%async_computation.7 | async-start | bytes 131072 | tf_op jit(solution)/shard_map/all_to_all | solution.py:37
  269.0 14.8 %all-to-all-start.14 = ((bf16[64,4,128]{2,1,0:T(4,128)(2,1)}), bf16[64,4,128]{2,1,0:T(4,128)(2,1)S(1)}, u32[]{:S(2)}, u32[]{:S(2)}) async-start(bf16[64,4,128]{2,1,0:T(4,128)(2,1)} %broadcast_in_dim.82), calls=%async_computation.14 | async-start | bytes 131072 | tf_op jit(solution)/shard_map/all_to_all | solution.py:37
  273.9 8.4 %collective-permute-start.3 = (f32[32,128]{1,0:T(8,128)S(1)}, f32[32,128]{1,0:T(8,128)S(1)}, u32[]{:S(2)}, u32[]{:S(2)}) collective-permute-start(f32[32,128]{1,0:T(8,128)S(1)} %get-tuple-element.9), channel_id=1, source_target_pairs={{0,0},{8,64},{16,8},{24,72},{32,16},{40,80},{48,24},{56,88},{64,32... | collective-permute-start | bytes 49160 | tf_op jit(solution)/shard_map/ppermute | solution.py:146
Sparse Core Ops, SparseCore 0:
  10.1 108.9 all-gather.1

commit v4 on v3

--- a/solution.py
+++ b/solution.py
@@ -75,8 +75,6 @@
     minor = lax.axis_index(("yb", "yc", "core"))
     part = x * 2 + core
 
-    rows = lax.all_gather(base_weight, Y, axis=0, tiled=True)
-
     there = [(c * 8 + r, r * 2 + c) for r in range(8) for c in range(2)]
     back = [(b, a) for a, b in there]
     old = lax.ppermute(
@@ -93,6 +91,8 @@
     weighted = (cotangent.astype(f32) * weight[:, None]).astype(bf16)
 
     mine = share(factors[0].astype(bf16), XY, 32)
+    mine, rows = lax.optimization_barrier((mine, base_weight))
+    rows = lax.all_gather(rows, Y, axis=0, tiled=True)
     other = core_swap(mine)
     low = jnp.where(core == 0, jnp.stack([mine, other], 1), jnp.stack([other, mine], 1))
     low = low.reshape(BLOCK, 2 * RANK)
@@ -110,44 +110,60 @@
     dims = (((0,), (0,)), ((), ()))
     grad_down = lax.dot_general(tokens, both[:, RANK:], dims, preferred_element_type=f32)
     grad_up = lax.dot_general(weighted, both[:, :RANK], dims, preferred_element_type=f32)
-    grads = jnp.concatenate([grad_down, grad_up], axis=1).astype(bf16).reshape(4, 2, 8, OWN, 128)
+    grads = jnp.concatenate([grad_down, grad_up], axis=1).astype(bf16).reshape(4, 2, TILE, 128)
     first = jnp.dot(first, base_weight, preferred_element_type=f32)
     first = first.reshape(8, 2, 4, 2, TILE)
 
     def half(which):
-        base = pick(first, which, 3).transpose(2, 0, 1, 3).reshape(32, 4, 128)
-        return pick(grads, which, 1).reshape(32, OWN, 128), base
+        base = pick(first, which, 3).transpose(2, 0, 1, 3).reshape(4, 32, 128)
+        return pick(grads, which, 1), base
 
     give, give_base = half(1 - core)
     keep, keep_base = half(core)
     got = core_swap(jnp.concatenate([give, *high_low(give_base)], axis=1)).astype(f32)
-    keep = (keep.astype(f32) + got[:, :OWN]).astype(bf16)
-    keep_base = keep_base + got[:, OWN : OWN + 4] + got[:, OWN + 4 :]
-    pieces = swap(jnp.concatenate([keep, *high_low(keep_base)], axis=1), XY).astype(f32)
-    pieces = jnp.sum(pieces, axis=0)
-    grads = scale * pieces[:OWN]
+    keep = (keep.astype(f32) + got[:, :TILE]).astype(bf16)
+    keep_base = keep_base + got[:, TILE : TILE + 32] + got[:, TILE + 32 :]
+    got = swap(jnp.concatenate([keep, *high_low(keep_base)], axis=1), "x").astype(f32)
+    got = jnp.sum(got, axis=0)
+    keep = got[:TILE].astype(bf16)
+    keep_base = (got[TILE : TILE + 32] + got[TILE + 32 :]).reshape(8, 4, 128)
+    keep = jnp.concatenate([keep, old[OWN:].astype(bf16)], axis=0)
+    keep = jnp.broadcast_to(keep[None], (8, TILE + 2 * OWN, 128))
+    got = swap(jnp.concatenate([keep, *high_low(keep_base)], axis=1), Y)
+    grads = scale * jnp.sum(got[:, :TILE].astype(f32), axis=0)
+    moments = got[:, TILE : TILE + 2 * OWN].astype(f32)
+    own_base = jnp.sum(got[:, TILE + 2 * OWN :].astype(f32), axis=0)
     own_state = lax.dynamic_slice(state, (2 * y, part * TILE), (2, TILE))
-    own_base = (pieces[OWN : OWN + 4] + pieces[OWN + 4 :]).reshape(2, TILE)
-    own_base = own_base + own_state.astype(f32)
+    own_base = (own_base[:4] + own_base[4:]).reshape(2, TILE) + own_state.astype(f32)
 
     squared = jnp.broadcast_to(jnp.sum(grads * grads), (1, 128))
-    squared = jnp.sum(share(squared, ("yb", "yc", "core", "z"), 64), axis=0)
-    squared = jnp.sum(share(squared, ("x", "ya"), 8), axis=0)
+    squared = jnp.sum(share(squared, ("x", "core", "z"), 64), axis=0)
     clip = jnp.minimum(f32(1.0), f32(1.0) / (jnp.sqrt(squared) + 1e-06))
     grads = clip * grads
-    moment_one = beta_one * old[OWN : 2 * OWN] + (1.0 - beta_one) * grads
-    moment_two = beta_two * old[2 * OWN :] + (1.0 - beta_two) * grads * grads
-    step_size = (
-        moment_one
-        / (1.0 - beta_one**adam_count)
-        / (jnp.sqrt(moment_two / (1.0 - beta_two**adam_count)) + 1e-08)
-    )
-    updated = old[:OWN] - rate * step_size
+
+    def update(values, first, second, slopes):
+        moment_one = beta_one * first + (1.0 - beta_one) * slopes
+        moment_two = beta_two * second + (1.0 - beta_two) * slopes * slopes
+        step_size = (
+            moment_one
+            / (1.0 - beta_one**adam_count)
+            / (jnp.sqrt(moment_two / (1.0 - beta_two**adam_count)) + 1e-08)
+        )
+        return values - rate * step_size
+
+    own_grads = lax.dynamic_slice_in_dim(grads, y * OWN, OWN, 0)
+    updated = update(old[:OWN], old[OWN : 2 * OWN], old[2 * OWN :], own_grads)
     new_factors = lax.ppermute(updated, Y + ("core",), back)[None]
 
-    near = share(updated.astype(bf16), Y, 8).reshape(TILE, 2 * RANK)
-    down = near[:, :RANK]
-    up = near[:, RANK:].astype(f32).T
+    near = lax.dynamic_slice_in_dim(low, part * TILE, TILE, 0).astype(f32)
+    near = update(
+        near,
+        moments[:, :OWN].reshape(TILE, 128),
+        moments[:, OWN:].reshape(TILE, 128),
+        grads,
+    )
+    down = near[:, :RANK].astype(bf16)
+    up = near[:, RANK:].astype(bf16).astype(f32).T
     own_gain = lax.dynamic_slice_in_dim(gain, part * TILE, TILE, 0)
 
     def spread(pair):
@@ -167,7 +183,7 @@
         current = current.transpose(2, 1, 0, 3).reshape(2, BLOCK)
         pairs = jnp.sum(got[:, :, 4:].astype(f32), axis=(0, 1))
         pairs = 0.25 * (pairs[:2] + pairs[2:])
-        sums = jnp.dot(current, rows, preferred_element_type=f32)
+        sums = lax.optimization_barrier(jnp.dot(current, rows, preferred_element_type=f32))
         sums = sums.reshape(2, 8, TILE).transpose(1, 0, 2).reshape(8, 4, 128)
         sent = jnp.concatenate([sums, jnp.broadcast_to(pairs[None], (8, 2, 128))], axis=1)
         got = jnp.sum(swap(sent, ("x", "core")), axis=0)

time: 294 us -> 274 us (0.932)
  blocking collectives: 120 us -> 70.9 us
  waiting for transfers between devices: 48 us -> 87.2 us
  local copies, waits for them, and re-layouts: 24.6 us -> 12.8 us
  starting transfers between devices: 56.1 us -> 60.1 us
  matrix products: 23.4 us -> 20.2 us
    all_to_all x9 -> x6, blocking collectives: 120 us -> 70.9 us  [swap(): return lax.all_to_all(chunks, axes, 0, 0, tiled=False)]
    all_to_all x6 -> x8, waiting for transfers between devices: 43.3 us -> 77.6 us  [swap(): return lax.all_to_all(chunks, axes, 0, 0, tiled=False)]
    dot_general x2 -> x0, local copies, waits for them, and re-layouts: 12.6 us -> none  [the longest x1 12.4 us: body(): sums = jnp.dot(current, rows, preferred_element_type=f32)]
    ppermute x1, waiting for transfers between devices: 1.97 us -> 7.59 us  [body(): lax.ppermute(jnp.concatenate([factors[0], first_moment[0], second_moment[...]
    all_to_all x6 -> x8, starting transfers between devices: 37 us -> 41 us  [swap(): return lax.all_to_all(chunks, axes, 0, 0, tiled=False)]
    dot_general x3, matrix products: 16.9 us -> 13.7 us  [body(): jnp.dot(current, rows, preferred_element_type=f32)]
  transfers between devices with their start and end apart: 11 -> 13, of which waited for: 9 -> 10; matrix products, arithmetic and copies ran while one was open for 5% -> 6% of each run, Pallas kernels for 0% -> 0%
where the time goes in v4:
time: 274 us; the launch traced here: 273 us
  waiting for transfers between devices  87.2 us (32%)
  blocking collectives  70.9 us (26%)
  starting transfers between devices  60.1 us (22%)
  matrix products  20.2 us (7%)
  between operations  16.8 us (6%)
  local copies, waits for them, and re-layouts  12.8 us (5%)
  other arithmetic  4.99 us (2%)
    all_to_all x8, waiting for transfers between devices, swap(): return lax.all_to_all(chunks, axes, 0, 0, tiled=False)  77.6 us
    all_to_all x6, blocking collectives, swap(): return lax.all_to_all(chunks, axes, 0, 0, tiled=False)  70.9 us
    all_to_all x8, starting transfers between devices, swap(): return lax.all_to_all(chunks, axes, 0, 0, tiled=False)  41 us
    dot_general x3, matrix products, body(): jnp.dot(current, rows, preferred_element_type=f32)  13.7 us
    ppermute x2, starting transfers between devices, core_swap(): return lax.ppermute(value, 'core', [(0, 1), (1, 0)])  8.01 us
    ppermute x1, waiting for transfers between devices, body(): lax.ppermute(jnp.concatenate([factors[0], first_moment[0], second_moment[...  7.59 us
    ppermute x1, starting transfers between devices, body(): new_factors = lax.ppermute(updated, Y + ('core',), back)[None]  7.49 us
  transfers between devices with their start and end apart: 13, of which 10 were waited for; matrix products, arithmetic and copies ran while one was open for 6% of the time, Pallas kernels for 0%

profile of v4, /device:TPU:1, one launch (start us, length us, event | category | flops | bytes accessed | tf_op | source)
XLA Modules:
  0.0 272.9 jit_solution(5606832593774080761)
XLA Ops:
  8.1 20.0 %all_to_all.70 = bf16[32,32,128]{2,1,0:T(8,128)(2,1)S(1)} all-to-all(bf16[32,32,128]{2,1,0:T(8,128)(2,1)S(1)} %broadcast_in_dim.57), channel_id=1, replica_groups=mesh['x'=4,'ya'=2,'yb'=2,'yc'=2,'core'=2,'z'=8] {'x','ya','yb','yc'}, dimensions={0} | all-to-all | bytes 524288 | tf_op jit(solution)/shard_map/all_to_all | solution.py:37
  28.1 5.6 %collective-permute-start.1 = (bf16[32,32,128]{2,1,0:T(8,128)(2,1)S(1)}, bf16[32,32,128]{2,1,0:T(8,128)(2,1)S(1)}, u32[]{:S(2)}, u32[]{:S(2)}) collective-permute-start(bf16[32,32,128]{2,1,0:T(8,128)(2,1)S(1)} %all_to_all.70), channel_id=1, source_target_pairs={{0,8},{8,0},{1,9},{9,1},{2,10},{10,2},{3,11},{11,3},{4,12},{12,4},... | collective-permute-start | bytes 786440 | tf_op jit(solution)/shard_map/ppermute | solution.py:45
  37.0 1.7 convolution_convert_fusion.2
  39.7 10.0 %all-to-all-start.1 = ((bf16[8,160,128]{2,1,0:T(8,128)(2,1)}), bf16[8,160,128]{2,1,0:T(8,128)(2,1)S(1)}, u32[]{:S(2)}, u32[]{:S(2)}) async-start(bf16[8,160,128]{2,1,0:T(8,128)(2,1)} %broadcast_in_dim.61), calls=%async_computation.1 | async-start | bytes 655360 | tf_op jit(solution)/shard_map/all_to_all | solution.py:37
  49.7 1.5 copy.87
  51.2 12.3 %all-to-all-done.1 = bf16[8,160,128]{2,1,0:T(8,128)(2,1)S(1)} async-done(((bf16[8,160,128]{2,1,0:T(8,128)(2,1)}), bf16[8,160,128]{2,1,0:T(8,128)(2,1)S(1)}, u32[]{:S(2)}, u32[]{:S(2)}) %all-to-all-start.1) | async-done | bytes 327712 | tf_op jit(solution)/shard_map/all_to_all | solution.py:37
  66.0 2.4 collective-permute-start.2
  70.7 3.5 %all-to-all-start.2 = ((bf16[4,320,128]{2,1,0:T(8,128)(2,1)}), bf16[4,320,128]{2,1,0:T(8,128)(2,1)S(1)}, u32[]{:S(2)}, u32[]{:S(2)}) async-start(bf16[4,320,128]{2,1,0:T(8,128)(2,1)} %pad_maximum_fusion.2), calls=%async_computation.2 | async-start | bytes 655360 | tf_op jit(solution)/shard_map/all_to_all | solution.py:37
  74.2 3.5 %collective-permute-start = (f32[96,128]{1,0:T(8,128)S(1)}, f32[96,128]{1,0:T(8,128)S(1)}, u32[]{:S(2)}, u32[]{:S(2)}) collective-permute-start(f32[96,128]{1,0:T(8,128)S(1)} %pad_maximum_fusion.5), channel_id=1, source_target_pairs={{0,0},{64,8},{8,16},{72,24},{16,32},{80,40},{24,48},{88,56},{32,64... | collective-permute-start | bytes 147464 | tf_op jit(solution)/shard_map/ppermute | solution.py:80
  77.7 7.6 %collective-permute-done = f32[96,128]{1,0:T(8,128)S(1)} collective-permute-done((f32[96,128]{1,0:T(8,128)S(1)}, f32[96,128]{1,0:T(8,128)S(1)}, u32[]{:S(2)}, u32[]{:S(2)}) %collective-permute-start) | collective-permute-done | bytes 49184 | tf_op jit(solution)/shard_map/ppermute | solution.py:80
  86.4 3.5 %all-to-all-start.3 = ((bf16[8,328,128]{2,1,0:T(8,128)(2,1)}), bf16[8,328,128]{2,1,0:T(8,128)(2,1)S(1)}, u32[]{:S(2)}, u32[]{:S(2)}) async-start(bf16[8,328,128]{2,1,0:T(8,128)(2,1)} %pad_maximum_fusion), calls=%async_computation.3 | async-start | bytes 1343488 | tf_op jit(solution)/shard_map/all_to_all | solution.py:37
  90.8 27.5 %all-to-all-done.3 = bf16[8,328,128]{2,1,0:T(8,128)(2,1)S(1)} async-done(((bf16[8,328,128]{2,1,0:T(8,128)(2,1)}), bf16[8,328,128]{2,1,0:T(8,128)(2,1)S(1)}, u32[]{:S(2)}, u32[]{:S(2)}) %all-to-all-start.3) | async-done | bytes 671776 | tf_op jit(solution)/shard_map/all_to_all | solution.py:37
  119.0 1.3 broadcast_in_dim_broadcast_in_dim_broadcast_in_dim.3
  120.2 5.5 %all-to-all-start.4 = ((f32[64,1,128]{2,1,0:T(1,128)}), f32[64,1,128]{2,1,0:T(1,128)S(1)}, u32[]{:S(2)}, u32[]{:S(2)}) async-start(f32[64,1,128]{2,1,0:T(1,128)} %broadcast_in_dim_broadcast_in_dim_broadcast_in_dim.3), calls=%async_computation.4 | async-start | bytes 65536 | tf_op jit(solution)/shard_map/all_to_all | solution.py:37
  125.9 9.1 %all-to-all-done.4 = f32[64,1,128]{2,1,0:T(1,128)S(1)} async-done(((f32[64,1,128]{2,1,0:T(1,128)}), f32[64,1,128]{2,1,0:T(1,128)S(1)}, u32[]{:S(2)}, u32[]{:S(2)}) %all-to-all-start.4) | async-done | bytes 32800 | tf_op jit(solution)/shard_map/all_to_all | solution.py:37
  136.7 4.9 %all-to-all-start.5 = ((f32[64,1,128]{2,1,0:T(1,128)}), f32[64,1,128]{2,1,0:T(1,128)S(1)}, u32[]{:S(2)}, u32[]{:S(2)}) async-start(f32[64,1,128]{2,1,0:T(1,128)} %broadcast_in_dim.65), calls=%async_computation.5 | async-start | bytes 65536 | tf_op jit(solution)/shard_map/all_to_all | solution.py:37
  141.6 9.2 %all-to-all-done.5 = f32[64,1,128]{2,1,0:T(1,128)S(1)} async-done(((f32[64,1,128]{2,1,0:T(1,128)}), f32[64,1,128]{2,1,0:T(1,128)S(1)}, u32[]{:S(2)}, u32[]{:S(2)}) %all-to-all-start.5) | async-done | bytes 32800 | tf_op jit(solution)/shard_map/all_to_all | solution.py:37
  153.0 3.9 %all-to-all-start.6 = ((bf16[32,8,128]{2,1,0:T(8,128)(2,1)}), bf16[32,8,128]{2,1,0:T(8,128)(2,1)S(1)}, u32[]{:S(2)}, u32[]{:S(2)}) async-start(bf16[32,8,128]{2,1,0:T(8,128)(2,1)} %broadcast_in_dim.67), calls=%async_computation.6 | async-start | bytes 131072 | tf_op jit(solution)/shard_map/all_to_all | solution.py:37
  156.9 8.9 %all-to-all-done.6 = bf16[32,8,128]{2,1,0:T(8,128)(2,1)S(1)} async-done(((bf16[32,8,128]{2,1,0:T(8,128)(2,1)}), bf16[32,8,128]{2,1,0:T(8,128)(2,1)S(1)}, u32[]{:S(2)}, u32[]{:S(2)}) %all-to-all-start.6) | async-done | bytes 65568 | tf_op jit(solution)/shard_map/all_to_all | solution.py:37
  165.9 4.6 %fusion.55 = f32[2,2048]{1,0:T(2,128)S(1)} fusion(bf16[2,2048]{1,0:T(2,128)(2,1)S(1)} %reshape.206, bf16[2048,2048]{1,0:T(8,128)(2,1)} %all-gather.2.cloned.1.call-done), kind=kOutput, calls=%fused_computation.151 | convolution fusion | flops 16777216 | bytes 8413184 | tf_op jit(solution)/shard_map/dot_general | solution.py:186
  170.6 9.1 %all_to_all.71 = f32[8,6,128]{2,1,0:T(8,128)S(1)} all-to-all(f32[8,6,128]{2,1,0:T(8,128)S(1)} %pad_maximum_fusion.6), channel_id=1, replica_groups=mesh['x'=4,'ya'=2,'yb'=2,'yc'=2,'core'=2,'z'=8] {'x','core'}, dimensions={0} | all-to-all | bytes 49152 | tf_op jit(solution)/shard_map/all_to_all | solution.py:37
  180.8 11.8 %all_to_all.72 = bf16[32,8,128]{2,1,0:T(8,128)(2,1)S(1)} all-to-all(bf16[32,8,128]{2,1,0:T(8,128)(2,1)S(1)} %broadcast_in_dim.70), channel_id=1, replica_groups=mesh['x'=4,'ya'=2,'yb'=2,'yc'=2,'core'=2,'z'=8] {'x','z'}, dimensions={0} | all-to-all | bytes 131072 | tf_op jit(solution)/shard_map/all_to_all | solution.py:37
  192.8 4.6 %fusion.56 = f32[2,2048]{1,0:T(2,128)S(1)} fusion(bf16[2,2048]{1,0:T(2,128)(2,1)S(1)} %reshape.215, bf16[2048,2048]{1,0:T(8,128)(2,1)} %all-gather.2.cloned.1.call-done), kind=kOutput, calls=%fused_computation.152 | convolution fusion | flops 16777216 | bytes 8413184 | tf_op jit(solution)/shard_map/dot_general | solution.py:186
  197.5 9.1 %all_to_all.73 = f32[8,6,128]{2,1,0:T(8,128)S(1)} all-to-all(f32[8,6,128]{2,1,0:T(8,128)S(1)} %pad_maximum_fusion.7), channel_id=1, replica_groups=mesh['x'=4,'ya'=2,'yb'=2,'yc'=2,'core'=2,'z'=8] {'x','core'}, dimensions={0} | all-to-all | bytes 49152 | tf_op jit(solution)/shard_map/all_to_all | solution.py:37
  207.7 11.8 %all_to_all.74 = bf16[32,8,128]{2,1,0:T(8,128)(2,1)S(1)} all-to-all(bf16[32,8,128]{2,1,0:T(8,128)(2,1)S(1)} %broadcast_in_dim.73), channel_id=1, replica_groups=mesh['x'=4,'ya'=2,'yb'=2,'yc'=2,'core'=2,'z'=8] {'x','z'}, dimensions={0} | all-to-all | bytes 131072 | tf_op jit(solution)/shard_map/all_to_all | solution.py:37
  219.7 4.6 %fusion.57 = f32[2,2048]{1,0:T(2,128)S(1)} fusion(bf16[2,2048]{1,0:T(2,128)(2,1)S(1)} %reshape.224, bf16[2048,2048]{1,0:T(8,128)(2,1)} %all-gather.2.cloned.1.call-done), kind=kOutput, calls=%fused_computation.153 | convolution fusion | flops 16777216 | bytes 8413184 | tf_op jit(solution)/shard_map/dot_general | solution.py:186
  224.3 9.1 %all_to_all.75 = f32[8,6,128]{2,1,0:T(8,128)S(1)} all-to-all(f32[8,6,128]{2,1,0:T(8,128)S(1)} %pad_maximum_fusion.8), channel_id=1, replica_groups=mesh['x'=4,'ya'=2,'yb'=2,'yc'=2,'core'=2,'z'=8] {'x','core'}, dimensions={0} | all-to-all | bytes 49152 | tf_op jit(solution)/shard_map/all_to_all | solution.py:37
  234.9 4.8 %all-to-all-start.12 = ((f32[64,1,128]{2,1,0:T(1,128)}), f32[64,1,128]{2,1,0:T(1,128)S(1)}, u32[]{:S(2)}, u32[]{:S(2)}) async-start(f32[64,1,128]{2,1,0:T(1,128)} %broadcast_in_dim.77), calls=%async_computation.12 | async-start | bytes 65536 | tf_op jit(solution)/shard_map/all_to_all | solution.py:37
  239.7 9.2 %all-to-all-done.12 = f32[64,1,128]{2,1,0:T(1,128)S(1)} async-done(((f32[64,1,128]{2,1,0:T(1,128)}), f32[64,1,128]{2,1,0:T(1,128)S(1)}, u32[]{:S(2)}, u32[]{:S(2)}) %all-to-all-start.12) | async-done | bytes 32800 | tf_op jit(solution)/shard_map/all_to_all | solution.py:37
  249.9 4.9 %all-to-all-start.13 = ((bf16[64,4,128]{2,1,0:T(4,128)(2,1)}), bf16[64,4,128]{2,1,0:T(4,128)(2,1)S(1)}, u32[]{:S(2)}, u32[]{:S(2)}) async-start(bf16[64,4,128]{2,1,0:T(4,128)(2,1)} %broadcast_in_dim.150), calls=%async_computation.13 | async-start | bytes 131072 | tf_op jit(solution)/shard_map/all_to_all | solution.py:37
  254.8 7.5 %collective-permute-start.3 = (f32[32,128]{1,0:T(8,128)S(1)}, f32[32,128]{1,0:T(8,128)S(1)}, u32[]{:S(2)}, u32[]{:S(2)}) collective-permute-start(f32[32,128]{1,0:T(8,128)S(1)} %fusion.47), channel_id=1, source_target_pairs={{0,0},{8,64},{16,8},{24,72},{32,16},{40,80},{48,24},{56,88},{64,32... | collective-permute-start | bytes 49160 | tf_op jit(solution)/shard_map/ppermute | solution.py:156
  263.1 1.5 all-to-all-done.13
  (169 shorter events, 21.8 us)
Async XLA Ops:
  7.2 29.5 %copy-start = (bf16[128,2048]{1,0:T(8,128)(2,1)S(1)}, bf16[128,2048]{1,0:T(8,128)(2,1)}, u32[]{:S(2)}) copy-start(bf16[128,2048]{1,0:T(8,128)(2,1)} %param.11) | copy-start | bytes 1572868
  7.2 57.8 %copy-start.1 = (bf16[128,2048]{1,0:T(8,128)(2,1)S(1)}, bf16[128,2048]{1,0:T(8,128)(2,1)}, u32[]{:S(2)}) copy-start(bf16[128,2048]{1,0:T(8,128)(2,1)} %param.12) | copy-start | bytes 1572868
  7.2 158.7 %all-gather.2.cloned.1.call-start = ((), (), s32[]{:S(2)}) async-start(), calls=%async_computation.14 | async-start | bytes 9437184 | tf_op jit(solution)/shard_map/all_gather | solution.py:95
  28.1 8.5 %collective-permute-start.1 = (bf16[32,32,128]{2,1,0:T(8,128)(2,1)S(1)}, bf16[32,32,128]{2,1,0:T(8,128)(2,1)S(1)}, u32[]{:S(2)}, u32[]{:S(2)}) collective-permute-start(bf16[32,32,128]{2,1,0:T(8,128)(2,1)S(1)} %all_to_all.70), channel_id=1, source_target_pairs={{0,8},{8,0},{1,9},{9,1},{2,10},{10,2},{3,11},{11,3},{4,12},{12,4},... | collective-permute-start | bytes 786440 | tf_op jit(solution)/shard_map/ppermute | solution.py:45
  38.7 35.4 %copy-start.2 = (f32[1,32,128]{2,1,0:T(8,128)S(1)}, f32[1,32,128]{2,1,0:T(8,128)}, u32[]{:S(2)}) copy-start(f32[1,32,128]{2,1,0:T(8,128)} %param.16) | copy-start | bytes 49156
  38.7 35.4 %copy-start.3 = (f32[1,32,128]{2,1,0:T(8,128)S(1)}, f32[1,32,128]{2,1,0:T(8,128)}, u32[]{:S(2)}) copy-start(f32[1,32,128]{2,1,0:T(8,128)} %param.18) | copy-start | bytes 49156
  38.7 35.4 %copy-start.4 = (f32[1,32,128]{2,1,0:T(8,128)S(1)}, f32[1,32,128]{2,1,0:T(8,128)}, u32[]{:S(2)}) copy-start(f32[1,32,128]{2,1,0:T(8,128)} %param.17) | copy-start | bytes 49156
  39.7 23.8 %all-to-all-start.1 = ((bf16[8,160,128]{2,1,0:T(8,128)(2,1)}), bf16[8,160,128]{2,1,0:T(8,128)(2,1)S(1)}, u32[]{:S(2)}, u32[]{:S(2)}) async-start(bf16[8,160,128]{2,1,0:T(8,128)(2,1)} %broadcast_in_dim.61), calls=%async_computation.1 | async-start | bytes 655360 | tf_op jit(solution)/shard_map/all_to_all | solution.py:37
  66.0 3.6 %collective-permute-start.2 = (bf16[4,320,128]{2,1,0:T(8,128)(2,1)S(1)}, bf16[4,320,128]{2,1,0:T(8,128)(2,1)S(1)}, u32[]{:S(2)}, u32[]{:S(2)}) collective-permute-start(bf16[4,320,128]{2,1,0:T(8,128)(2,1)S(1)} %pad_maximum_fusion.1), channel_id=1, source_target_pairs={{0,8},{8,0},{1,9},{9,1},{2,10},{10,2},{3,11},{11,3},{4,12},{12,4},... | collective-permute-start | bytes 983048 | tf_op jit(solution)/shard_map/ppermute | solution.py:45
  70.7 14.6 %all-to-all-start.2 = ((bf16[4,320,128]{2,1,0:T(8,128)(2,1)}), bf16[4,320,128]{2,1,0:T(8,128)(2,1)S(1)}, u32[]{:S(2)}, u32[]{:S(2)}) async-start(bf16[4,320,128]{2,1,0:T(8,128)(2,1)} %pad_maximum_fusion.2), calls=%async_computation.2 | async-start | bytes 655360 | tf_op jit(solution)/shard_map/all_to_all | solution.py:37
  74.2 11.1 %collective-permute-start = (f32[96,128]{1,0:T(8,128)S(1)}, f32[96,128]{1,0:T(8,128)S(1)}, u32[]{:S(2)}, u32[]{:S(2)}) collective-permute-start(f32[96,128]{1,0:T(8,128)S(1)} %pad_maximum_fusion.5), channel_id=1, source_target_pairs={{0,0},{64,8},{8,16},{72,24},{16,32},{80,40},{24,48},{88,56},{32,64... | collective-permute-start | bytes 147464 | tf_op jit(solution)/shard_map/ppermute | solution.py:80
  86.4 31.8 %all-to-all-start.3 = ((bf16[8,328,128]{2,1,0:T(8,128)(2,1)}), bf16[8,328,128]{2,1,0:T(8,128)(2,1)S(1)}, u32[]{:S(2)}, u32[]{:S(2)}) async-start(bf16[8,328,128]{2,1,0:T(8,128)(2,1)} %pad_maximum_fusion), calls=%async_computation.3 | async-start | bytes 1343488 | tf_op jit(solution)/shard_map/all_to_all | solution.py:37
  120.2 14.7 %all-to-all-start.4 = ((f32[64,1,128]{2,1,0:T(1,128)}), f32[64,1,128]{2,1,0:T(1,128)S(1)}, u32[]{:S(2)}, u32[]{:S(2)}) async-start(f32[64,1,128]{2,1,0:T(1,128)} %broadcast_in_dim_broadcast_in_dim_broadcast_in_dim.3), calls=%async_computation.4 | async-start | bytes 65536 | tf_op jit(solution)/shard_map/all_to_all | solution.py:37
  136.7 14.1 %all-to-all-start.5 = ((f32[64,1,128]{2,1,0:T(1,128)}), f32[64,1,128]{2,1,0:T(1,128)S(1)}, u32[]{:S(2)}, u32[]{:S(2)}) async-start(f32[64,1,128]{2,1,0:T(1,128)} %broadcast_in_dim.65), calls=%async_computation.5 | async-start | bytes 65536 | tf_op jit(solution)/shard_map/all_to_all | solution.py:37
  153.0 12.7 %all-to-all-start.6 = ((bf16[32,8,128]{2,1,0:T(8,128)(2,1)}), bf16[32,8,128]{2,1,0:T(8,128)(2,1)S(1)}, u32[]{:S(2)}, u32[]{:S(2)}) async-start(bf16[32,8,128]{2,1,0:T(8,128)(2,1)} %broadcast_in_dim.67), calls=%async_computation.6 | async-start | bytes 131072 | tf_op jit(solution)/shard_map/all_to_all | solution.py:37
  234.9 14.0 %all-to-all-start.12 = ((f32[64,1,128]{2,1,0:T(1,128)}), f32[64,1,128]{2,1,0:T(1,128)S(1)}, u32[]{:S(2)}, u32[]{:S(2)}) async-start(f32[64,1,128]{2,1,0:T(1,128)} %broadcast_in_dim.77), calls=%async_computation.12 | async-start | bytes 65536 | tf_op jit(solution)/shard_map/all_to_all | solution.py:37
  249.9 14.8 %all-to-all-start.13 = ((bf16[64,4,128]{2,1,0:T(4,128)(2,1)}), bf16[64,4,128]{2,1,0:T(4,128)(2,1)S(1)}, u32[]{:S(2)}, u32[]{:S(2)}) async-start(bf16[64,4,128]{2,1,0:T(4,128)(2,1)} %broadcast_in_dim.150), calls=%async_computation.13 | async-start | bytes 131072 | tf_op jit(solution)/shard_map/all_to_all | solution.py:37
  254.8 8.4 %collective-permute-start.3 = (f32[32,128]{1,0:T(8,128)S(1)}, f32[32,128]{1,0:T(8,128)S(1)}, u32[]{:S(2)}, u32[]{:S(2)}) collective-permute-start(f32[32,128]{1,0:T(8,128)S(1)} %fusion.47), channel_id=1, source_target_pairs={{0,0},{8,64},{16,8},{24,72},{32,16},{40,80},{48,24},{56,88},{64,32... | collective-permute-start | bytes 49160 | tf_op jit(solution)/shard_map/ppermute | solution.py:156
Sparse Core Ops, SparseCore 0:
  28.2 113.5 all-gather.1

commit v5 on v4

v5 whole, which is shorter than its diff:
```python
import math

import jax
import jax.numpy as jnp
from jax import lax
from jax.sharding import Mesh
from jax.sharding import PartitionSpec as P

MODEL_WIDTH = 16384
SEQLEN = 128
GROUP = 8
DECODE_STEPS = 4
RANK = 64
BATCH = 16
BLOCK = 2048
TILE = 256
OWN = 32

adapter_alpha = 2.0
beta_one = 0.9
beta_two = 0.999
rate = 0.1
adam_count = 200.0
scale = adapter_alpha / (RANK * math.sqrt(MODEL_WIDTH))

bf16 = jnp.bfloat16
f32 = jnp.float32
HIGHEST = lax.Precision.HIGHEST

AXES = ("x", "ya", "yb", "yc", "core", "z")
DP = ("x", "ya", "yb", "yc", "core")
XY = ("x", "ya", "yb", "yc")
MINOR = ("yb", "yc", "core")
CROSS = ("x", "ya", "z")


def swap(chunks, axes):
    return lax.all_to_all(chunks, axes, 0, 0, tiled=False)


def share(piece, axes, count):
    return swap(jnp.broadcast_to(piece[None], (count,) + piece.shape), axes)


def core_swap(value):
    return lax.ppermute(value, "core", [(0, 1), (1, 0)])


def high_low(value):
    high = lax.reduce_precision(value, 8, 7)
    return high.astype(bf16), (value - high).astype(bf16)


def pick(value, index, axis):
    return lax.dynamic_index_in_dim(value, index, axis, keepdims=False)


def body(
    tokens,
    cotangent,
    prompt_len,
    resp_len,
    ranks,
    factors,
    first_moment,
    second_moment,
    base_weight,
    gain,
    state,
):
    core = lax.axis_index("core")
    z = lax.axis_index("z")
    major = lax.axis_index(("x", "ya"))
    minor = lax.axis_index(MINOR)

    panel = lax.all_gather(base_weight, "z", axis=0, tiled=False)

    there = [((k * 8 + i) * 8 + t, (t * 8 + k) * 8 + i) for k in range(8) for i in range(8) for t in range(8)]
    back = [(b, a) for a, b in there]
    old = lax.ppermute(
        jnp.concatenate([factors[0], first_moment[0], second_moment[0]], axis=0), AXES, there
    )

    positions = jnp.arange(SEQLEN, dtype=jnp.int32)
    lower = prompt_len[:, None]
    upper = lower + resp_len[:, None]
    inside = (positions[None, :] >= lower) & (positions[None, :] < upper)
    advantage = (2 * ranks - (GROUP - 1)).astype(f32) / (GROUP - 1)
    per_seq = advantage / resp_len.astype(f32)
    weight = jnp.where(inside, per_seq[:, None], f32(0.0)).reshape(-1)
    weighted = (cotangent.astype(f32) * weight[:, None]).astype(bf16)

    mine = share(factors[0].astype(bf16), XY, 32)
    other = core_swap(mine)
    low = jnp.where(core == 0, jnp.stack([mine, other], 1), jnp.stack([other, mine], 1))
    low = low.reshape(BLOCK, 2 * RANK)
    hidden = jnp.dot(tokens, low[:, :RANK], preferred_element_type=f32)
    projected = jnp.dot(weighted, low[:, RANK:], preferred_element_type=f32)
    state_tile = lax.dynamic_slice_in_dim(state, minor * TILE, TILE, 1)
    tile_gain = lax.dynamic_slice_in_dim(gain, minor * TILE, TILE, 0)
    sent = jnp.concatenate(
        [
            jnp.concatenate([hidden, projected], axis=1).astype(bf16),
            state_tile.reshape(32, 128),
            *[part.reshape(2, 128) for part in high_low(tile_gain)],
        ],
        axis=0,
    )
    got = share(sent, "z", 8)
    both = jnp.sum(got[:, :SEQLEN].astype(f32), axis=0).astype(bf16)
    home = pick(got[:, SEQLEN:], major, 0)
    first = home[:32].reshape(BATCH, TILE)
    tile_gain = home[32:].astype(f32)
    tile_gain = (tile_gain[:2] + tile_gain[2:]).reshape(TILE)
    own_state = lax.dynamic_slice_in_dim(first, 2 * z, 2, 0)

    dims = (((0,), (0,)), ((), ()))
    grad_down = lax.dot_general(tokens, both[:, RANK:], dims, preferred_element_type=f32)
    grad_up = lax.dot_general(weighted, both[:, :RANK], dims, preferred_element_type=f32)
    grads = jnp.concatenate([grad_down, grad_up], axis=1).astype(bf16).reshape(8, TILE, 128)
    first = jnp.dot(first, base_weight, preferred_element_type=f32)
    first = first.reshape(BATCH, 8, TILE).transpose(1, 0, 2).reshape(8, 32, 128)
    got = swap(jnp.concatenate([grads, *high_low(first)], axis=1), MINOR).astype(f32)
    got = jnp.sum(got, axis=0)
    first = got[TILE : TILE + 32] + got[TILE + 32 :]
    got = lax.ppermute(
        jnp.concatenate([got[:TILE].astype(bf16), *high_low(first)], axis=0),
        CROSS,
        [(k * 8 + t, t * 8 + k) for k in range(8) for t in range(8)],
    )
    rows = jnp.concatenate([got[:TILE], old.astype(bf16)], axis=0)
    rows = jnp.broadcast_to(rows[None], (8, TILE + 3 * OWN, 128))
    first = [got[TILE : TILE + 32].reshape(8, 4, 128), got[TILE + 32 :].reshape(8, 4, 128)]
    got = swap(jnp.concatenate([rows, *first], axis=1), "z").astype(f32)
    grads = scale * jnp.sum(got[:, :TILE], axis=0)
    former = got[:, TILE : TILE + 3 * OWN]
    base = jnp.sum(got[:, TILE + 3 * OWN :], axis=0)
    base = (base[:4] + base[4:]).reshape(2, TILE) + own_state.astype(f32)

    squared = jnp.broadcast_to(jnp.sum(grads * grads), (1, 128))
    squared = jnp.sum(share(squared, DP, 64), axis=0)
    clip = jnp.minimum(f32(1.0), f32(1.0) / (jnp.sqrt(squared) + 1e-06))
    grads = clip * grads

    def update(values, first, second, slopes):
        moment_one = beta_one * first + (1.0 - beta_one) * slopes
        moment_two = beta_two * second + (1.0 - beta_two) * slopes * slopes
        step_size = (
            moment_one
            / (1.0 - beta_one**adam_count)
            / (jnp.sqrt(moment_two / (1.0 - beta_two**adam_count)) + 1e-08)
        )
        return values - rate * step_size

    own_grads = lax.dynamic_slice_in_dim(grads, z * OWN, OWN, 0)
    updated = update(old[:OWN], old[OWN : 2 * OWN], old[2 * OWN :], own_grads)
    new_factors = lax.ppermute(updated, AXES, back)[None]

    near = update(
        former[:, :OWN].reshape(TILE, 128),
        former[:, OWN : 2 * OWN].reshape(TILE, 128),
        former[:, 2 * OWN :].reshape(TILE, 128),
        grads,
    )
    down = near[:, :RANK].astype(bf16)
    up = near[:, RANK:].astype(bf16).astype(f32).T

    thin = jnp.dot(own_state, down, preferred_element_type=f32).reshape(1, 128)
    thin = jnp.sum(share(thin, DP, 64), axis=0).reshape(2, RANK)
    resid = base + scale * jnp.dot(thin, up, precision=HIGHEST)

    def packed(sums):
        halves = [jnp.broadcast_to(half[:, None], (2, 32)) for half in high_low(sums)]
        return jnp.concatenate(halves, axis=1).reshape(1, 128)

    for step in range(1, DECODE_STEPS):
        own = (resid * tile_gain).astype(bf16)
        thin = jnp.dot(own, down, preferred_element_type=f32).astype(bf16).reshape(1, 128)
        extra = jnp.concatenate([thin, packed(jnp.sum(resid * resid, axis=1))], axis=0)
        sums = jnp.einsum(
            "zsk,zkn->zsn",
            jnp.broadcast_to(own[None], (8, 2, TILE)),
            panel,
            preferred_element_type=f32,
        )
        sums = lax.optimization_barrier(sums.astype(bf16))
        sums = sums.reshape(8, 2, 8, TILE).transpose(0, 2, 1, 3).reshape(64, 4, 128)
        sent = jnp.concatenate([sums, jnp.broadcast_to(extra[None], (64, 2, 128))], axis=1)
        got = jnp.sum(swap(sent, DP).astype(f32), axis=0)
        thin = got[4].reshape(2, RANK)
        squares = got[5].reshape(2, 2, 32)[:, :, 0]
        norm = lax.rsqrt((squares[:, :1] + squares[:, 1:]) / MODEL_WIDTH + 1e-05)
        total = own.astype(f32) + got[:4].reshape(2, TILE)
        resid = norm * (total + scale * jnp.dot(thin, up, precision=HIGHEST))

    own = (resid * tile_gain).astype(bf16).reshape(4, 128)
    sent = jnp.concatenate([own, packed(jnp.sum(resid * resid, axis=1))], axis=0)
    got = share(sent, CROSS, 64).reshape(8, 8, 5, 128)
    sums = jnp.sum(got[:, :, 4].astype(f32), axis=0).reshape(BATCH, 2, 32)[:, :, :8]
    sums = (sums[:, 0] + sums[:, 1]).reshape(1, 128)
    sent = jnp.concatenate([pick(got[:, :, :4], z, 0).reshape(32, 128), *high_low(sums)], axis=0)
    got = share(sent, MINOR, 8)
    sums = jnp.sum(got[:, 32:].astype(f32), axis=(0, 1)).reshape(BATCH, 8)[:, :1]
    norm = lax.rsqrt(sums / MODEL_WIDTH + 1e-05)
    result = got[:, :32].reshape(8, BATCH, TILE).transpose(1, 0, 2).reshape(BATCH, BLOCK)
    result = (result.astype(f32) * norm).astype(bf16)
    return (new_factors, result)


def solution(mesh):
    fine = Mesh(mesh.devices.reshape(4, 2, 2, 2, 2, 8), AXES)
    return jax.shard_map(
        body,
        mesh=fine,
        in_specs=(
            P(DP, "z"),
            P(DP, "z"),
            P(DP),
            P(DP),
            P(DP),
            P("z", DP, None),
            P("z", DP, None),
            P("z", DP, None),
            P(DP, "z"),
            P("z"),
            P(None, "z"),
        ),
        out_specs=(P("z", DP, None), P(None, "z")),
        check_vma=False,
    )
```

time: 274 us -> 293 us (1.069)
  the two profiles are of different devices: /device:TPU:1 before, /device:TPU:85 now
where the time goes in v5:
time: 293 us; the launch traced here: 292 us
  waiting for transfers between devices  89.9 us (31%)
  starting transfers between devices  83.9 us (29%)
  blocking collectives  65.4 us (22%)
  matrix products  17.7 us (6%)
  between operations  16.7 us (6%)
  local copies, waits for them, and re-layouts  11.5 us (4%)
  other arithmetic  6.58 us (2%)
    all_to_all x7, waiting for transfers between devices, swap(): return lax.all_to_all(chunks, axes, 0, 0, tiled=False)  73.6 us
    all_to_all x4, blocking collectives, swap(): return lax.all_to_all(chunks, axes, 0, 0, tiled=False)  65.4 us
    all_to_all x7, starting transfers between devices, swap(): return lax.all_to_all(chunks, axes, 0, 0, tiled=False)  63.8 us
    ppermute x1, waiting for transfers between devices, body(): new_factors = lax.ppermute(updated, AXES, back)[None]  14.2 us
    dot_general x3, matrix products, body(): jnp.einsum('zsk,zkn->zsn', jnp.broadcast_to(own[None], (8, 2, TILE)), pan...  13.7 us
    ppermute x1, starting transfers between devices, body(): lax.ppermute(jnp.concatenate([factors[0], first_moment[0], second_moment[...  10.3 us
  transfers between devices with their start and end apart: 12, of which 8 were waited for; matrix products, arithmetic and copies ran while one was open for 5% of the time, Pallas kernels for 0%

profile of v5, /device:TPU:85, one launch (start us, length us, event | category | flops | bytes accessed | tf_op | source)
XLA Modules:
  0.0 291.7 jit_solution(1438495132760424767)
XLA Ops:
  7.9 0.7 convert_bitcast_fusion
  8.6 0.7 broadcast_in_dim.61
  9.4 9.6 %all-to-all-start = ((bf16[32,32,128]{2,1,0:T(8,128)(2,1)}), bf16[32,32,128]{2,1,0:T(8,128)(2,1)S(1)}, u32[]{:S(2)}, u32[]{:S(2)}) async-start(bf16[32,32,128]{2,1,0:T(8,128)(2,1)} %broadcast_in_dim.61), calls=%async_computation | async-start | bytes 524288 | tf_op jit(solution)/shard_map/all_to_all | solution.py:38
  19.0 9.3 %all-to-all-done = bf16[32,32,128]{2,1,0:T(8,128)(2,1)S(1)} async-done(((bf16[32,32,128]{2,1,0:T(8,128)(2,1)}), bf16[32,32,128]{2,1,0:T(8,128)(2,1)S(1)}, u32[]{:S(2)}, u32[]{:S(2)}) %all-to-all-start) | async-done | bytes 262176 | tf_op jit(solution)/shard_map/all_to_all | solution.py:38
  28.3 3.9 %collective-permute-start.1 = (bf16[32,32,128]{2,1,0:T(8,128)(2,1)S(1)}, bf16[32,32,128]{2,1,0:T(8,128)(2,1)S(1)}, u32[]{:S(2)}, u32[]{:S(2)}) collective-permute-start(bf16[32,32,128]{2,1,0:T(8,128)(2,1)S(1)} %all-to-all-done), channel_id=1, source_target_pairs={{0,8},{8,0},{1,9},{9,1},{2,10},{10,2},{3,11},{11,3},{4,12},{12,4},... | collective-permute-start | bytes 786440 | tf_op jit(solution)/shard_map/ppermute | solution.py:46
  32.2 0.8 fusion.55
  37.4 0.8 broadcast_in_dim.65
  38.2 9.4 %all-to-all-start.1 = ((bf16[8,164,128]{2,1,0:T(8,128)(2,1)}), bf16[8,164,128]{2,1,0:T(8,128)(2,1)S(1)}, u32[]{:S(2)}, u32[]{:S(2)}) async-start(bf16[8,164,128]{2,1,0:T(8,128)(2,1)} %broadcast_in_dim.65), calls=%async_computation.1 | async-start | bytes 688128 | tf_op jit(solution)/shard_map/all_to_all | solution.py:38
  48.1 15.7 %all-to-all-done.1 = bf16[8,164,128]{2,1,0:T(8,128)(2,1)S(1)} async-done(((bf16[8,164,128]{2,1,0:T(8,128)(2,1)}), bf16[8,164,128]{2,1,0:T(8,128)(2,1)S(1)}, u32[]{:S(2)}, u32[]{:S(2)}) %all-to-all-start.1) | async-done | bytes 335904 | tf_op jit(solution)/shard_map/all_to_all | solution.py:38
  66.0 20.0 %all_to_all.55 = bf16[8,320,128]{2,1,0:T(8,128)(2,1)S(1)} all-to-all(bf16[8,320,128]{2,1,0:T(8,128)(2,1)S(1)} %pad_maximum_fusion.1), channel_id=1, replica_groups=mesh['x'=4,'ya'=2,'yb'=2,'yc'=2,'core'=2,'z'=8] {'yb','yc','core'}, dimensions={0} | all-to-all | bytes 1310720 | tf_op jit(solution)/shard_map/all_to_all | solution.py:38
  86.5 4.1 %collective-permute-start.2 = (bf16[320,128]{0,1:T(8,128)(2,1)S(1)}, bf16[320,128]{0,1:T(8,128)(2,1)S(1)}, u32[]{:S(2)}, u32[]{:S(2)}) collective-permute-start(bf16[320,128]{0,1:T(8,128)(2,1)S(1)} %pad_maximum_fusion.5), channel_id=1, source_target_pairs={{0,0},{1,64},{2,128},{3,192},{4,256},{5,320},{6,384},{7,448},{64,1... | collective-permute-start | bytes 245768 | tf_op jit(solution)/shard_map/ppermute | solution.py:126
  90.6 10.3 %collective-permute-start = (f32[96,128]{1,0:T(8,128)S(1)}, f32[96,128]{1,0:T(8,128)S(1)}, u32[]{:S(2)}, u32[]{:S(2)}) collective-permute-start(f32[96,128]{1,0:T(8,128)S(1)} %pad_maximum_fusion.8), channel_id=1, source_target_pairs={{0,0},{1,64},{2,128},{3,192},{4,256},{5,320},{6,384},{7,448},{8,1}... | collective-permute-start | bytes 147464 | tf_op jit(solution)/shard_map/ppermute | solution.py:80
  100.9 1.3 collective-permute-done
  102.9 1.0 pad_maximum_fusion
  103.8 6.8 %all-to-all-start.3 = ((bf16[8,360,128]{2,1,0:T(8,128)(2,1)}), bf16[8,360,128]{2,1,0:T(8,128)(2,1)S(1)}, u32[]{:S(2)}, u32[]{:S(2)}) async-start(bf16[8,360,128]{2,1,0:T(8,128)(2,1)} %pad_maximum_fusion), calls=%async_computation.3 | async-start | bytes 1474560 | tf_op jit(solution)/shard_map/all_to_all | solution.py:38
  110.7 25.7 %all-to-all-done.3 = bf16[8,360,128]{2,1,0:T(8,128)(2,1)S(1)} async-done(((bf16[8,360,128]{2,1,0:T(8,128)(2,1)}), bf16[8,360,128]{2,1,0:T(8,128)(2,1)S(1)}, u32[]{:S(2)}, u32[]{:S(2)}) %all-to-all-start.3) | async-done | bytes 737312 | tf_op jit(solution)/shard_map/all_to_all | solution.py:38
  137.2 1.3 broadcast_in_dim_broadcast_in_dim_broadcast_in_dim.3
  138.5 15.5 %all-to-all-start.4 = ((f32[64,1,128]{2,1,0:T(1,128)}), f32[64,1,128]{2,1,0:T(1,128)S(1)}, u32[]{:S(2)}, u32[]{:S(2)}) async-start(f32[64,1,128]{2,1,0:T(1,128)} %broadcast_in_dim_broadcast_in_dim_broadcast_in_dim.3), calls=%async_computation.4 | async-start | bytes 65536 | tf_op jit(solution)/shard_map/all_to_all | solution.py:38
  154.0 5.5 %all-to-all-done.4 = f32[64,1,128]{2,1,0:T(1,128)S(1)} async-done(((f32[64,1,128]{2,1,0:T(1,128)}), f32[64,1,128]{2,1,0:T(1,128)S(1)}, u32[]{:S(2)}, u32[]{:S(2)}) %all-to-all-start.4) | async-done | bytes 32800 | tf_op jit(solution)/shard_map/all_to_all | solution.py:38
  160.6 8.4 %all-to-all-start.5 = ((f32[64,1,128]{2,1,0:T(1,128)}), f32[64,1,128]{2,1,0:T(1,128)S(1)}, u32[]{:S(2)}, u32[]{:S(2)}) async-start(f32[64,1,128]{2,1,0:T(1,128)} %broadcast_in_dim.69), calls=%async_computation.5 | async-start | bytes 65536 | tf_op jit(solution)/shard_map/all_to_all | solution.py:38
  169.0 5.6 %all-to-all-done.5 = f32[64,1,128]{2,1,0:T(1,128)S(1)} async-done(((f32[64,1,128]{2,1,0:T(1,128)}), f32[64,1,128]{2,1,0:T(1,128)S(1)}, u32[]{:S(2)}, u32[]{:S(2)}) %all-to-all-start.5) | async-done | bytes 32800 | tf_op jit(solution)/shard_map/all_to_all | solution.py:38
  175.7 4.6 %convolution_convert_fusion.4 = bf16[8,2,2048]{2,1,0:T(2,128)(2,1)S(1)} fusion(bf16[8,256,2048]{2,1,0:T(8,128)(2,1)} %bitcast.76, bf16[2,256]{1,0:T(2,128)(2,1)S(1)} %get-tuple-element.38), kind=kOutput, calls=%fused_computation.5 | convolution fusion | flops 16809984 | bytes 8455168 | tf_op jit(solution)/shard_map/zsk,zkn->zsn/dot_general | solution.py:180
  180.4 15.3 %all_to_all.56 = bf16[64,6,128]{2,1,0:T(8,128)(2,1)S(1)} all-to-all(bf16[64,6,128]{2,1,0:T(8,128)(2,1)S(1)} %pad_maximum_fusion.2), channel_id=1, replica_groups=mesh['x'=4,'ya'=2,'yb'=2,'yc'=2,'core'=2,'z'=8] {'x','ya','yb','yc','core'}, dimensions={0} | all-to-all | bytes 196608 | tf_op jit(solution)/shard_map/all_to_all | solution.py:38
  196.8 4.6 %convolution_convert_fusion.3 = bf16[8,2,2048]{2,1,0:T(2,128)(2,1)S(1)} fusion(bf16[8,256,2048]{2,1,0:T(8,128)(2,1)} %bitcast.77, bf16[2,256]{1,0:T(2,128)(2,1)S(1)} %get-tuple-element.36), kind=kOutput, calls=%fused_computation.4 | convolution fusion | flops 16809984 | bytes 8455168 | tf_op jit(solution)/shard_map/zsk,zkn->zsn/dot_general | solution.py:180
  202.0 15.0 %all_to_all.57 = bf16[64,6,128]{2,1,0:T(8,128)(2,1)S(1)} all-to-all(bf16[64,6,128]{2,1,0:T(8,128)(2,1)S(1)} %pad_maximum_fusion.3), channel_id=1, replica_groups=mesh['x'=4,'ya'=2,'yb'=2,'yc'=2,'core'=2,'z'=8] {'x','ya','yb','yc','core'}, dimensions={0} | all-to-all | bytes 196608 | tf_op jit(solution)/shard_map/all_to_all | solution.py:38
  218.1 4.6 %convolution_convert_fusion.2 = bf16[8,2,2048]{2,1,0:T(2,128)(2,1)S(1)} fusion(bf16[8,256,2048]{2,1,0:T(8,128)(2,1)} %bitcast.78, bf16[2,256]{1,0:T(2,128)(2,1)S(1)} %get-tuple-element.34), kind=kOutput, calls=%fused_computation.3 | convolution fusion | flops 16809984 | bytes 8455168 | tf_op jit(solution)/shard_map/zsk,zkn->zsn/dot_general | solution.py:180
  223.2 15.0 %all_to_all.58 = bf16[64,6,128]{2,1,0:T(8,128)(2,1)S(1)} all-to-all(bf16[64,6,128]{2,1,0:T(8,128)(2,1)S(1)} %pad_maximum_fusion.4), channel_id=1, replica_groups=mesh['x'=4,'ya'=2,'yb'=2,'yc'=2,'core'=2,'z'=8] {'x','ya','yb','yc','core'}, dimensions={0} | all-to-all | bytes 196608 | tf_op jit(solution)/shard_map/all_to_all | solution.py:38
  240.2 8.4 %all-to-all-start.9 = ((bf16[64,5,128]{2,1,0:T(8,128)(2,1)}), bf16[64,5,128]{2,1,0:T(8,128)(2,1)S(1)}, u32[]{:S(2)}, u32[]{:S(2)}) async-start(bf16[64,5,128]{2,1,0:T(8,128)(2,1)} %broadcast_in_dim.84), calls=%async_computation.9 | async-start | bytes 262144 | tf_op jit(solution)/shard_map/all_to_all | solution.py:38
  248.6 11.7 %all-to-all-done.9 = bf16[64,5,128]{2,1,0:T(8,128)(2,1)S(1)} async-done(((bf16[64,5,128]{2,1,0:T(8,128)(2,1)}), bf16[64,5,128]{2,1,0:T(8,128)(2,1)S(1)}, u32[]{:S(2)}, u32[]{:S(2)}) %all-to-all-start.9) | async-done | bytes 81952 | tf_op jit(solution)/shard_map/all_to_all | solution.py:38
  261.3 5.7 %all-to-all-start.10 = ((bf16[8,34,128]{2,1,0:T(8,128)(2,1)}), bf16[8,34,128]{2,1,0:T(8,128)(2,1)S(1)}, u32[]{:S(2)}, u32[]{:S(2)}) async-start(bf16[8,34,128]{2,1,0:T(8,128)(2,1)} %broadcast_in_dim.85), calls=%async_computation.10 | async-start | bytes 163840 | tf_op jit(solution)/shard_map/all_to_all | solution.py:38
  267.0 1.9 collective-permute-start.3
  269.0 14.2 %collective-permute-done.3 = f32[32,128]{1,0:T(8,128)S(1)} collective-permute-done((f32[32,128]{1,0:T(8,128)S(1)}, f32[32,128]{1,0:T(8,128)S(1)}, u32[]{:S(2)}, u32[]{:S(2)}) %collective-permute-start.3) | collective-permute-done | bytes 16416 | tf_op jit(solution)/shard_map/ppermute | solution.py:157
  (168 shorter events, 17.5 us)
Async XLA Ops:
  7.2 29.0 %copy-start = (bf16[128,2048]{1,0:T(8,128)(2,1)S(1)}, bf16[128,2048]{1,0:T(8,128)(2,1)}, u32[]{:S(2)}) copy-start(bf16[128,2048]{1,0:T(8,128)(2,1)} %param.11) | copy-start | bytes 1572868
  7.2 168.5 %all-gather.3.cloned.1.call-start = ((), (), s32[]{:S(2)}) async-start(), calls=%async_computation.11 | async-start | bytes 9437184 | tf_op jit(solution)/shard_map/all_gather | solution.py:76
  9.4 27.1 %copy-start.2 = (bf16[128,2048]{1,0:T(8,128)(2,1)S(1)}, bf16[128,2048]{1,0:T(8,128)(2,1)}, u32[]{:S(2)}) copy-start(bf16[128,2048]{1,0:T(8,128)(2,1)} %param.12) | copy-start | bytes 1572868
  9.4 18.9 %all-to-all-start = ((bf16[32,32,128]{2,1,0:T(8,128)(2,1)}), bf16[32,32,128]{2,1,0:T(8,128)(2,1)S(1)}, u32[]{:S(2)}, u32[]{:S(2)}) async-start(bf16[32,32,128]{2,1,0:T(8,128)(2,1)} %broadcast_in_dim.61), calls=%async_computation | async-start | bytes 524288 | tf_op jit(solution)/shard_map/all_to_all | solution.py:38
  28.3 7.8 %collective-permute-start.1 = (bf16[32,32,128]{2,1,0:T(8,128)(2,1)S(1)}, bf16[32,32,128]{2,1,0:T(8,128)(2,1)S(1)}, u32[]{:S(2)}, u32[]{:S(2)}) collective-permute-start(bf16[32,32,128]{2,1,0:T(8,128)(2,1)S(1)} %all-to-all-done), channel_id=1, source_target_pairs={{0,8},{8,0},{1,9},{9,1},{2,10},{10,2},{3,11},{11,3},{4,12},{12,4},... | collective-permute-start | bytes 786440 | tf_op jit(solution)/shard_map/ppermute | solution.py:46
  36.5 11.1 %copy-start.1 = (bf16[256,2048]{1,0:T(8,128)(2,1)S(1)}, bf16[256,2048]{1,0:T(8,128)(2,1)}, u32[]{:S(2)}) copy-start(bf16[256,2048]{1,0:T(8,128)(2,1)} %param.19) | copy-start | bytes 3145732
  38.2 25.7 %all-to-all-start.1 = ((bf16[8,164,128]{2,1,0:T(8,128)(2,1)}), bf16[8,164,128]{2,1,0:T(8,128)(2,1)S(1)}, u32[]{:S(2)}, u32[]{:S(2)}) async-start(bf16[8,164,128]{2,1,0:T(8,128)(2,1)} %broadcast_in_dim.65), calls=%async_computation.1 | async-start | bytes 688128 | tf_op jit(solution)/shard_map/all_to_all | solution.py:38
  48.1 16.3 %copy-start.3 = (bf16[128,2048]{1,0:T(8,128)(2,1)S(1)}, bf16[128,2048]{1,0:T(8,128)(2,1)}, u32[]{:S(2)}) copy-start(bf16[128,2048]{1,0:T(8,128)(2,1)} %param.12) | copy-start | bytes 1572868
  65.9 24.6 %copy-start.4 = (f32[1,32,128]{2,1,0:T(8,128)S(1)}, f32[1,32,128]{2,1,0:T(8,128)}, u32[]{:S(2)}) copy-start(f32[1,32,128]{2,1,0:T(8,128)} %param.16) | copy-start | bytes 49156
  65.9 24.6 %copy-start.5 = (f32[1,32,128]{2,1,0:T(8,128)S(1)}, f32[1,32,128]{2,1,0:T(8,128)}, u32[]{:S(2)}) copy-start(f32[1,32,128]{2,1,0:T(8,128)} %param.18) | copy-start | bytes 49156
  65.9 24.6 %copy-start.6 = (f32[1,32,128]{2,1,0:T(8,128)S(1)}, f32[1,32,128]{2,1,0:T(8,128)}, u32[]{:S(2)}) copy-start(f32[1,32,128]{2,1,0:T(8,128)} %param.17) | copy-start | bytes 49156
  86.5 15.9 %collective-permute-start.2 = (bf16[320,128]{0,1:T(8,128)(2,1)S(1)}, bf16[320,128]{0,1:T(8,128)(2,1)S(1)}, u32[]{:S(2)}, u32[]{:S(2)}) collective-permute-start(bf16[320,128]{0,1:T(8,128)(2,1)S(1)} %pad_maximum_fusion.5), channel_id=1, source_target_pairs={{0,0},{1,64},{2,128},{3,192},{4,256},{5,320},{6,384},{7,448},{64,1... | collective-permute-start | bytes 245768 | tf_op jit(solution)/shard_map/ppermute | solution.py:126
  90.6 11.6 %collective-permute-start = (f32[96,128]{1,0:T(8,128)S(1)}, f32[96,128]{1,0:T(8,128)S(1)}, u32[]{:S(2)}, u32[]{:S(2)}) collective-permute-start(f32[96,128]{1,0:T(8,128)S(1)} %pad_maximum_fusion.8), channel_id=1, source_target_pairs={{0,0},{1,64},{2,128},{3,192},{4,256},{5,320},{6,384},{7,448},{8,1}... | collective-permute-start | bytes 147464 | tf_op jit(solution)/shard_map/ppermute | solution.py:80
  103.8 32.6 %all-to-all-start.3 = ((bf16[8,360,128]{2,1,0:T(8,128)(2,1)}), bf16[8,360,128]{2,1,0:T(8,128)(2,1)S(1)}, u32[]{:S(2)}, u32[]{:S(2)}) async-start(bf16[8,360,128]{2,1,0:T(8,128)(2,1)} %pad_maximum_fusion), calls=%async_computation.3 | async-start | bytes 1474560 | tf_op jit(solution)/shard_map/all_to_all | solution.py:38
  138.5 21.1 %all-to-all-start.4 = ((f32[64,1,128]{2,1,0:T(1,128)}), f32[64,1,128]{2,1,0:T(1,128)S(1)}, u32[]{:S(2)}, u32[]{:S(2)}) async-start(f32[64,1,128]{2,1,0:T(1,128)} %broadcast_in_dim_broadcast_in_dim_broadcast_in_dim.3), calls=%async_computation.4 | async-start | bytes 65536 | tf_op jit(solution)/shard_map/all_to_all | solution.py:38
  160.6 14.0 %all-to-all-start.5 = ((f32[64,1,128]{2,1,0:T(1,128)}), f32[64,1,128]{2,1,0:T(1,128)S(1)}, u32[]{:S(2)}, u32[]{:S(2)}) async-start(f32[64,1,128]{2,1,0:T(1,128)} %broadcast_in_dim.69), calls=%async_computation.5 | async-start | bytes 65536 | tf_op jit(solution)/shard_map/all_to_all | solution.py:38
  240.2 20.1 %all-to-all-start.9 = ((bf16[64,5,128]{2,1,0:T(8,128)(2,1)}), bf16[64,5,128]{2,1,0:T(8,128)(2,1)S(1)}, u32[]{:S(2)}, u32[]{:S(2)}) async-start(bf16[64,5,128]{2,1,0:T(8,128)(2,1)} %broadcast_in_dim.84), calls=%async_computation.9 | async-start | bytes 262144 | tf_op jit(solution)/shard_map/all_to_all | solution.py:38
  261.3 21.9 %all-to-all-start.10 = ((bf16[8,34,128]{2,1,0:T(8,128)(2,1)}), bf16[8,34,128]{2,1,0:T(8,128)(2,1)S(1)}, u32[]{:S(2)}, u32[]{:S(2)}) async-start(bf16[8,34,128]{2,1,0:T(8,128)(2,1)} %broadcast_in_dim.85), calls=%async_computation.10 | async-start | bytes 163840 | tf_op jit(solution)/shard_map/all_to_all | solution.py:38
  267.0 16.2 %collective-permute-start.3 = (f32[32,128]{1,0:T(8,128)S(1)}, f32[32,128]{1,0:T(8,128)S(1)}, u32[]{:S(2)}, u32[]{:S(2)}) collective-permute-start(f32[32,128]{1,0:T(8,128)S(1)} %fusion.39), channel_id=1, source_target_pairs={{0,0},{64,1},{128,2},{192,3},{256,4},{320,5},{384,6},{448,7},{1,8}... | collective-permute-start | bytes 49160 | tf_op jit(solution)/shard_map/ppermute | solution.py:157
Sparse Core Ops, SparseCore 0:
  10.1 129.0 all-gather.2

commit v6 on v5

--- a/solution.py
+++ b/solution.py
@@ -91,6 +91,7 @@
     weighted = (cotangent.astype(f32) * weight[:, None]).astype(bf16)
 
     mine = share(factors[0].astype(bf16), XY, 32)
+    mine, old = lax.optimization_barrier((mine, old))
     other = core_swap(mine)
     low = jnp.where(core == 0, jnp.stack([mine, other], 1), jnp.stack([other, mine], 1))
     low = low.reshape(BLOCK, 2 * RANK)
@@ -117,25 +118,32 @@
     dims = (((0,), (0,)), ((), ()))
     grad_down = lax.dot_general(tokens, both[:, RANK:], dims, preferred_element_type=f32)
     grad_up = lax.dot_general(weighted, both[:, :RANK], dims, preferred_element_type=f32)
-    grads = jnp.concatenate([grad_down, grad_up], axis=1).astype(bf16).reshape(8, TILE, 128)
+    grads = jnp.concatenate([grad_down, grad_up], axis=1).astype(bf16).reshape(4, 2, 8, OWN, 128)
     first = jnp.dot(first, base_weight, preferred_element_type=f32)
-    first = first.reshape(BATCH, 8, TILE).transpose(1, 0, 2).reshape(8, 32, 128)
-    got = swap(jnp.concatenate([grads, *high_low(first)], axis=1), MINOR).astype(f32)
+    first = first.reshape(8, 2, 4, 2, TILE)
+
+    def half(which):
+        base = pick(first, which, 3).transpose(0, 2, 1, 3).reshape(32, 4, 128)
+        return pick(grads, which, 1).transpose(1, 0, 2, 3).reshape(32, OWN, 128), base
+
+    give, give_base = half(1 - core)
+    keep, keep_base = half(core)
+    got = core_swap(jnp.concatenate([give, *high_low(give_base)], axis=1)).astype(f32)
+    keep = (keep.astype(f32) + got[:, :OWN]).astype(bf16)
+    keep_base = keep_base + got[:, OWN : OWN + 4] + got[:, OWN + 4 :]
+    got = swap(jnp.concatenate([keep, *high_low(keep_base)], axis=1), XY).astype(f32)
     got = jnp.sum(got, axis=0)
-    first = got[TILE : TILE + 32] + got[TILE + 32 :]
+    base = got[OWN : OWN + 4] + got[OWN + 4 :]
     got = lax.ppermute(
-        jnp.concatenate([got[:TILE].astype(bf16), *high_low(first)], axis=0),
+        jnp.concatenate([got[:OWN].astype(bf16), *high_low(base)], axis=0),
         CROSS,
         [(k * 8 + t, t * 8 + k) for k in range(8) for t in range(8)],
     )
-    rows = jnp.concatenate([got[:TILE], old.astype(bf16)], axis=0)
-    rows = jnp.broadcast_to(rows[None], (8, TILE + 3 * OWN, 128))
-    first = [got[TILE : TILE + 32].reshape(8, 4, 128), got[TILE + 32 :].reshape(8, 4, 128)]
-    got = swap(jnp.concatenate([rows, *first], axis=1), "z").astype(f32)
-    grads = scale * jnp.sum(got[:, :TILE], axis=0)
-    former = got[:, TILE : TILE + 3 * OWN]
-    base = jnp.sum(got[:, TILE + 3 * OWN :], axis=0)
-    base = (base[:4] + base[4:]).reshape(2, TILE) + own_state.astype(f32)
+    base = (got[OWN : OWN + 4].astype(f32) + got[OWN + 4 :].astype(f32)).reshape(2, TILE)
+    base = base + own_state.astype(f32)
+    got = share(jnp.concatenate([got[:OWN], old.astype(bf16)], axis=0), "z", 8).astype(f32)
+    grads = scale * got[:, :OWN].reshape(TILE, 128)
+    former = got[:, OWN:]
 
     squared = jnp.broadcast_to(jnp.sum(grads * grads), (1, 128))
     squared = jnp.sum(share(squared, DP, 64), axis=0)
@@ -187,6 +195,8 @@
         sums = sums.reshape(8, 2, 8, TILE).transpose(0, 2, 1, 3).reshape(64, 4, 128)
         sent = jnp.concatenate([sums, jnp.broadcast_to(extra[None], (64, 2, 128))], axis=1)
         got = jnp.sum(swap(sent, DP).astype(f32), axis=0)
+        if step == 1:
+            got, new_factors = lax.optimization_barrier((got, new_factors))
         thin = got[4].reshape(2, RANK)
         squares = got[5].reshape(2, 2, 32)[:, :, 0]
         norm = lax.rsqrt((squares[:, :1] + squares[:, 1:]) / MODEL_WIDTH + 1e-05)

time: 293 us -> 284 us (0.969)
  the two profiles are of different devices: /device:TPU:85 before, /device:TPU:1 now
where the time goes in v6:
time: 284 us; the launch traced here: 283 us
  starting transfers between devices  90.2 us (32%)
  waiting for transfers between devices  77.5 us (27%)
  blocking collectives  59.8 us (21%)
  matrix products  18.6 us (7%)
  between operations  16.6 us (6%)
  local copies, waits for them, and re-layouts  12.6 us (4%)
  other arithmetic  7.22 us (3%)
    all_to_all x8, starting transfers between devices, swap(): return lax.all_to_all(chunks, axes, 0, 0, tiled=False)  72 us
    all_to_all x8, waiting for transfers between devices, swap(): return lax.all_to_all(chunks, axes, 0, 0, tiled=False)  68.4 us
    all_to_all x3, blocking collectives, swap(): return lax.all_to_all(chunks, axes, 0, 0, tiled=False)  59.8 us
    dot_general x3, matrix products, body(): jnp.einsum('zsk,zkn->zsn', jnp.broadcast_to(own[None], (8, 2, TILE)), pan...  13.7 us
    ppermute x1, starting transfers between devices, body(): new_factors = lax.ppermute(updated, AXES, back)[None]  7.49 us
    ppermute x1, waiting for transfers between devices, body(): lax.ppermute(jnp.concatenate([factors[0], first_moment[0], second_moment[...  7.41 us
  transfers between devices with their start and end apart: 14, of which 9 were waited for; matrix products, arithmetic and copies ran while one was open for 6% of the time, Pallas kernels for 0%

profile of v6, /device:TPU:1, one launch (start us, length us, event | category | flops | bytes accessed | tf_op | source)
XLA Modules:
  0.0 282.6 jit_solution(17097437466697087287)
XLA Ops:
  9.4 10.5 %all-to-all-start = ((bf16[32,32,128]{2,1,0:T(8,128)(2,1)}), bf16[32,32,128]{2,1,0:T(8,128)(2,1)S(1)}, u32[]{:S(2)}, u32[]{:S(2)}) async-start(bf16[32,32,128]{2,1,0:T(8,128)(2,1)} %broadcast_in_dim.61), calls=%async_computation | async-start | bytes 524288 | tf_op jit(solution)/shard_map/all_to_all | solution.py:38
  20.7 4.8 %collective-permute-start = (f32[96,128]{1,0:T(8,128)S(1)}, f32[96,128]{1,0:T(8,128)S(1)}, u32[]{:S(2)}, u32[]{:S(2)}) collective-permute-start(f32[96,128]{1,0:T(8,128)S(1)} %pad_maximum_fusion.6), channel_id=1, source_target_pairs={{0,0},{1,64},{2,128},{3,192},{4,256},{5,320},{6,384},{7,448},{8,1}... | collective-permute-start | bytes 147464 | tf_op jit(solution)/shard_map/ppermute | solution.py:80
  25.5 7.4 %collective-permute-done = f32[96,128]{1,0:T(8,128)S(1)} collective-permute-done((f32[96,128]{1,0:T(8,128)S(1)}, f32[96,128]{1,0:T(8,128)S(1)}, u32[]{:S(2)}, u32[]{:S(2)}) %collective-permute-start) | collective-permute-done | bytes 49184 | tf_op jit(solution)/shard_map/ppermute | solution.py:80
  32.9 2.3 collective-permute-start.1
  35.2 0.8 fusion.61
  39.5 1.7 convolution_convert_fusion.5
  41.4 0.8 broadcast_in_dim.65
  42.3 12.7 %all-to-all-start.1 = ((bf16[8,164,128]{2,1,0:T(8,128)(2,1)}), bf16[8,164,128]{2,1,0:T(8,128)(2,1)S(1)}, u32[]{:S(2)}, u32[]{:S(2)}) async-start(bf16[8,164,128]{2,1,0:T(8,128)(2,1)} %broadcast_in_dim.65), calls=%async_computation.1 | async-start | bytes 688128 | tf_op jit(solution)/shard_map/all_to_all | solution.py:38
  54.9 1.5 copy.80
  56.4 16.1 %all-to-all-done.1 = bf16[8,164,128]{2,1,0:T(8,128)(2,1)S(1)} async-done(((bf16[8,164,128]{2,1,0:T(8,128)(2,1)}), bf16[8,164,128]{2,1,0:T(8,128)(2,1)S(1)}, u32[]{:S(2)}, u32[]{:S(2)}) %all-to-all-start.1) | async-done | bytes 335904 | tf_op jit(solution)/shard_map/all_to_all | solution.py:38
  74.7 2.9 %collective-permute-start.2 = (bf16[32,40,128]{2,1,0:T(8,128)(2,1)S(1)}, bf16[32,40,128]{2,1,0:T(8,128)(2,1)S(1)}, u32[]{:S(2)}, u32[]{:S(2)}) collective-permute-start(bf16[32,40,128]{2,1,0:T(8,128)(2,1)S(1)} %pad_maximum_fusion), channel_id=1, source_target_pairs={{0,8},{8,0},{1,9},{9,1},{2,10},{10,2},{3,11},{11,3},{4,12},{12,4},... | collective-permute-start | bytes 983048 | tf_op jit(solution)/shard_map/ppermute | solution.py:46
  77.8 1.1 collective-permute-done.2
  79.1 20.1 %all_to_all.55 = bf16[32,40,128]{2,1,0:T(8,128)(2,1)S(1)} all-to-all(bf16[32,40,128]{2,1,0:T(8,128)(2,1)S(1)} %pad_maximum_fusion.1), channel_id=1, replica_groups=mesh['x'=4,'ya'=2,'yb'=2,'yc'=2,'core'=2,'z'=8] {'x','ya','yb','yc'}, dimensions={0} | all-to-all | bytes 655360 | tf_op jit(solution)/shard_map/all_to_all | solution.py:38
  100.8 15.6 %all-to-all-start.3 = ((bf16[8,128,128]{2,1,0:T(8,128)(2,1)}), bf16[8,128,128]{2,1,0:T(8,128)(2,1)S(1)}, u32[]{:S(2)}, u32[]{:S(2)}) async-start(bf16[8,128,128]{2,1,0:T(8,128)(2,1)} %broadcast_in_dim.66), calls=%async_computation.3 | async-start | bytes 524288 | tf_op jit(solution)/shard_map/all_to_all | solution.py:38
  116.4 12.1 %all-to-all-done.3 = bf16[8,128,128]{2,1,0:T(8,128)(2,1)S(1)} async-done(((bf16[8,128,128]{2,1,0:T(8,128)(2,1)}), bf16[8,128,128]{2,1,0:T(8,128)(2,1)S(1)}, u32[]{:S(2)}, u32[]{:S(2)}) %all-to-all-start.3) | async-done | bytes 262176 | tf_op jit(solution)/shard_map/all_to_all | solution.py:38
  129.2 1.3 broadcast_in_dim_broadcast_in_dim_broadcast_in_dim.3
  130.4 12.1 %all-to-all-start.4 = ((f32[64,1,128]{2,1,0:T(1,128)}), f32[64,1,128]{2,1,0:T(1,128)S(1)}, u32[]{:S(2)}, u32[]{:S(2)}) async-start(f32[64,1,128]{2,1,0:T(1,128)} %broadcast_in_dim_broadcast_in_dim_broadcast_in_dim.3), calls=%async_computation.4 | async-start | bytes 65536 | tf_op jit(solution)/shard_map/all_to_all | solution.py:38
  142.5 9.2 %all-to-all-done.4 = f32[64,1,128]{2,1,0:T(1,128)S(1)} async-done(((f32[64,1,128]{2,1,0:T(1,128)}), f32[64,1,128]{2,1,0:T(1,128)S(1)}, u32[]{:S(2)}, u32[]{:S(2)}) %all-to-all-start.4) | async-done | bytes 32800 | tf_op jit(solution)/shard_map/all_to_all | solution.py:38
  152.7 4.7 %all-to-all-start.5 = ((f32[64,1,128]{2,1,0:T(1,128)}), f32[64,1,128]{2,1,0:T(1,128)S(1)}, u32[]{:S(2)}, u32[]{:S(2)}) async-start(f32[64,1,128]{2,1,0:T(1,128)} %broadcast_in_dim.68), calls=%async_computation.5 | async-start | bytes 65536 | tf_op jit(solution)/shard_map/all_to_all | solution.py:38
  157.5 9.3 %all-to-all-done.5 = f32[64,1,128]{2,1,0:T(1,128)S(1)} async-done(((f32[64,1,128]{2,1,0:T(1,128)}), f32[64,1,128]{2,1,0:T(1,128)S(1)}, u32[]{:S(2)}, u32[]{:S(2)}) %all-to-all-start.5) | async-done | bytes 32800 | tf_op jit(solution)/shard_map/all_to_all | solution.py:38
  167.8 4.6 %convolution_convert_fusion.4 = bf16[8,2,2048]{2,1,0:T(2,128)(2,1)S(1)} fusion(bf16[8,256,2048]{2,1,0:T(8,128)(2,1)} %bitcast.99, bf16[2,256]{1,0:T(2,128)(2,1)S(1)} %get-tuple-element.33), kind=kOutput, calls=%fused_computation.5 | convolution fusion | flops 16809984 | bytes 8455168 | tf_op jit(solution)/shard_map/zsk,zkn->zsn/dot_general | solution.py:188
  173.2 4.7 %all-to-all-start.6 = ((bf16[64,6,128]{2,1,0:T(8,128)(2,1)}), bf16[64,6,128]{2,1,0:T(8,128)(2,1)S(1)}, u32[]{:S(2)}, u32[]{:S(2)}) async-start(bf16[64,6,128]{2,1,0:T(8,128)(2,1)} %pad_maximum_fusion.2), calls=%async_computation.6 | async-start | bytes 262144 | tf_op jit(solution)/shard_map/all_to_all | solution.py:38
  178.0 7.5 %collective-permute-start.4 = (f32[32,128]{1,0:T(8,128)S(1)}, f32[32,128]{1,0:T(8,128)S(1)}, u32[]{:S(2)}, u32[]{:S(2)}) collective-permute-start(f32[32,128]{1,0:T(8,128)S(1)} %fusion.43), channel_id=1, source_target_pairs={{0,0},{64,1},{128,2},{192,3},{256,4},{320,5},{384,6},{448,7},{1,8}... | collective-permute-start | bytes 49160 | tf_op jit(solution)/shard_map/ppermute | solution.py:165
  185.5 2.9 %all-to-all-done.6 = bf16[64,6,128]{2,1,0:T(8,128)(2,1)S(1)} async-done(((bf16[64,6,128]{2,1,0:T(8,128)(2,1)}), bf16[64,6,128]{2,1,0:T(8,128)(2,1)S(1)}, u32[]{:S(2)}, u32[]{:S(2)}) %all-to-all-start.6) | async-done | bytes 98336 | tf_op jit(solution)/shard_map/all_to_all | solution.py:38
  189.3 4.6 %convolution_convert_fusion.3 = bf16[8,2,2048]{2,1,0:T(2,128)(2,1)S(1)} fusion(bf16[8,256,2048]{2,1,0:T(8,128)(2,1)} %bitcast.100, bf16[2,256]{1,0:T(2,128)(2,1)S(1)} %get-tuple-element.41), kind=kOutput, calls=%fused_computation.4 | convolution fusion | flops 16809984 | bytes 8455168 | tf_op jit(solution)/shard_map/zsk,zkn->zsn/dot_general | solution.py:188
  194.6 24.7 %all_to_all.56 = bf16[64,6,128]{2,1,0:T(8,128)(2,1)S(1)} all-to-all(bf16[64,6,128]{2,1,0:T(8,128)(2,1)S(1)} %pad_maximum_fusion.3), channel_id=1, replica_groups=mesh['x'=4,'ya'=2,'yb'=2,'yc'=2,'core'=2,'z'=8] {'x','ya','yb','yc','core'}, dimensions={0} | all-to-all | bytes 196608 | tf_op jit(solution)/shard_map/all_to_all | solution.py:38
  220.2 4.6 %convolution_convert_fusion.2 = bf16[8,2,2048]{2,1,0:T(2,128)(2,1)S(1)} fusion(bf16[8,256,2048]{2,1,0:T(8,128)(2,1)} %bitcast.101, bf16[2,256]{1,0:T(2,128)(2,1)S(1)} %get-tuple-element.39), kind=kOutput, calls=%fused_computation.3 | convolution fusion | flops 16809984 | bytes 8455168 | tf_op jit(solution)/shard_map/zsk,zkn->zsn/dot_general | solution.py:188
  225.5 15.0 %all_to_all.57 = bf16[64,6,128]{2,1,0:T(8,128)(2,1)S(1)} all-to-all(bf16[64,6,128]{2,1,0:T(8,128)(2,1)S(1)} %pad_maximum_fusion.4), channel_id=1, replica_groups=mesh['x'=4,'ya'=2,'yb'=2,'yc'=2,'core'=2,'z'=8] {'x','ya','yb','yc','core'}, dimensions={0} | all-to-all | bytes 196608 | tf_op jit(solution)/shard_map/all_to_all | solution.py:38
  242.5 5.5 %all-to-all-start.9 = ((bf16[64,5,128]{2,1,0:T(8,128)(2,1)}), bf16[64,5,128]{2,1,0:T(8,128)(2,1)S(1)}, u32[]{:S(2)}, u32[]{:S(2)}) async-start(bf16[64,5,128]{2,1,0:T(8,128)(2,1)} %broadcast_in_dim.84), calls=%async_computation.9 | async-start | bytes 262144 | tf_op jit(solution)/shard_map/all_to_all | solution.py:38
  248.0 13.6 %all-to-all-done.9 = bf16[64,5,128]{2,1,0:T(8,128)(2,1)S(1)} async-done(((bf16[64,5,128]{2,1,0:T(8,128)(2,1)}), bf16[64,5,128]{2,1,0:T(8,128)(2,1)S(1)}, u32[]{:S(2)}, u32[]{:S(2)}) %all-to-all-start.9) | async-done | bytes 81952 | tf_op jit(solution)/shard_map/all_to_all | solution.py:38
  262.6 6.3 %all-to-all-start.10 = ((bf16[8,34,128]{2,1,0:T(8,128)(2,1)}), bf16[8,34,128]{2,1,0:T(8,128)(2,1)S(1)}, u32[]{:S(2)}, u32[]{:S(2)}) async-start(bf16[8,34,128]{2,1,0:T(8,128)(2,1)} %broadcast_in_dim.85), calls=%async_computation.10 | async-start | bytes 163840 | tf_op jit(solution)/shard_map/all_to_all | solution.py:38
  268.9 5.3 %all-to-all-done.10 = bf16[8,34,128]{2,1,0:T(8,128)(2,1)S(1)} async-done(((bf16[8,34,128]{2,1,0:T(8,128)(2,1)}), bf16[8,34,128]{2,1,0:T(8,128)(2,1)S(1)}, u32[]{:S(2)}, u32[]{:S(2)}) %all-to-all-start.10) | async-done | bytes 69664 | tf_op jit(solution)/shard_map/all_to_all | solution.py:38
  (160 shorter events, 20.0 us)
Async XLA Ops:
  7.2 32.0 %copy-start = (bf16[128,2048]{1,0:T(8,128)(2,1)S(1)}, bf16[128,2048]{1,0:T(8,128)(2,1)}, u32[]{:S(2)}) copy-start(bf16[128,2048]{1,0:T(8,128)(2,1)} %param.11) | copy-start | bytes 1572868
  7.2 65.3 %copy-start.1 = (bf16[128,2048]{1,0:T(8,128)(2,1)S(1)}, bf16[128,2048]{1,0:T(8,128)(2,1)}, u32[]{:S(2)}) copy-start(bf16[128,2048]{1,0:T(8,128)(2,1)} %param.12) | copy-start | bytes 1572868
  7.2 160.6 %all-gather.3.cloned.1.call-start = ((), (), s32[]{:S(2)}) async-start(), calls=%async_computation.11 | async-start | bytes 9437184 | tf_op jit(solution)/shard_map/all_gather | solution.py:76
  9.4 23.5 %all-to-all-start = ((bf16[32,32,128]{2,1,0:T(8,128)(2,1)}), bf16[32,32,128]{2,1,0:T(8,128)(2,1)S(1)}, u32[]{:S(2)}, u32[]{:S(2)}) async-start(bf16[32,32,128]{2,1,0:T(8,128)(2,1)} %broadcast_in_dim.61), calls=%async_computation | async-start | bytes 524288 | tf_op jit(solution)/shard_map/all_to_all | solution.py:38
  20.7 12.3 %collective-permute-start = (f32[96,128]{1,0:T(8,128)S(1)}, f32[96,128]{1,0:T(8,128)S(1)}, u32[]{:S(2)}, u32[]{:S(2)}) collective-permute-start(f32[96,128]{1,0:T(8,128)S(1)} %pad_maximum_fusion.6), channel_id=1, source_target_pairs={{0,0},{1,64},{2,128},{3,192},{4,256},{5,320},{6,384},{7,448},{8,1}... | collective-permute-start | bytes 147464 | tf_op jit(solution)/shard_map/ppermute | solution.py:80
  32.9 6.2 %collective-permute-start.1 = (bf16[32,32,128]{2,1,0:T(8,128)(2,1)S(1)}, bf16[32,32,128]{2,1,0:T(8,128)(2,1)S(1)}, u32[]{:S(2)}, u32[]{:S(2)}) collective-permute-start(bf16[32,32,128]{2,1,0:T(8,128)(2,1)S(1)} %all-to-all-done), channel_id=1, source_target_pairs={{0,8},{8,0},{1,9},{9,1},{2,10},{10,2},{3,11},{11,3},{4,12},{12,4},... | collective-permute-start | bytes 786440 | tf_op jit(solution)/shard_map/ppermute | solution.py:46
  42.3 30.2 %all-to-all-start.1 = ((bf16[8,164,128]{2,1,0:T(8,128)(2,1)}), bf16[8,164,128]{2,1,0:T(8,128)(2,1)S(1)}, u32[]{:S(2)}, u32[]{:S(2)}) async-start(bf16[8,164,128]{2,1,0:T(8,128)(2,1)} %broadcast_in_dim.65), calls=%async_computation.1 | async-start | bytes 688128 | tf_op jit(solution)/shard_map/all_to_all | solution.py:38
  74.7 4.2 %collective-permute-start.2 = (bf16[32,40,128]{2,1,0:T(8,128)(2,1)S(1)}, bf16[32,40,128]{2,1,0:T(8,128)(2,1)S(1)}, u32[]{:S(2)}, u32[]{:S(2)}) collective-permute-start(bf16[32,40,128]{2,1,0:T(8,128)(2,1)S(1)} %pad_maximum_fusion), channel_id=1, source_target_pairs={{0,8},{8,0},{1,9},{9,1},{2,10},{10,2},{3,11},{11,3},{4,12},{12,4},... | collective-permute-start | bytes 983048 | tf_op jit(solution)/shard_map/ppermute | solution.py:46
  99.3 0.7 collective-permute-start.3
  100.8 27.7 %all-to-all-start.3 = ((bf16[8,128,128]{2,1,0:T(8,128)(2,1)}), bf16[8,128,128]{2,1,0:T(8,128)(2,1)S(1)}, u32[]{:S(2)}, u32[]{:S(2)}) async-start(bf16[8,128,128]{2,1,0:T(8,128)(2,1)} %broadcast_in_dim.66), calls=%async_computation.3 | async-start | bytes 524288 | tf_op jit(solution)/shard_map/all_to_all | solution.py:38
  130.4 21.3 %all-to-all-start.4 = ((f32[64,1,128]{2,1,0:T(1,128)}), f32[64,1,128]{2,1,0:T(1,128)S(1)}, u32[]{:S(2)}, u32[]{:S(2)}) async-start(f32[64,1,128]{2,1,0:T(1,128)} %broadcast_in_dim_broadcast_in_dim_broadcast_in_dim.3), calls=%async_computation.4 | async-start | bytes 65536 | tf_op jit(solution)/shard_map/all_to_all | solution.py:38
  152.7 14.0 %all-to-all-start.5 = ((f32[64,1,128]{2,1,0:T(1,128)}), f32[64,1,128]{2,1,0:T(1,128)S(1)}, u32[]{:S(2)}, u32[]{:S(2)}) async-start(f32[64,1,128]{2,1,0:T(1,128)} %broadcast_in_dim.68), calls=%async_computation.5 | async-start | bytes 65536 | tf_op jit(solution)/shard_map/all_to_all | solution.py:38
  173.2 15.2 %all-to-all-start.6 = ((bf16[64,6,128]{2,1,0:T(8,128)(2,1)}), bf16[64,6,128]{2,1,0:T(8,128)(2,1)S(1)}, u32[]{:S(2)}, u32[]{:S(2)}) async-start(bf16[64,6,128]{2,1,0:T(8,128)(2,1)} %pad_maximum_fusion.2), calls=%async_computation.6 | async-start | bytes 262144 | tf_op jit(solution)/shard_map/all_to_all | solution.py:38
  178.0 10.5 %collective-permute-start.4 = (f32[32,128]{1,0:T(8,128)S(1)}, f32[32,128]{1,0:T(8,128)S(1)}, u32[]{:S(2)}, u32[]{:S(2)}) collective-permute-start(f32[32,128]{1,0:T(8,128)S(1)} %fusion.43), channel_id=1, source_target_pairs={{0,0},{64,1},{128,2},{192,3},{256,4},{320,5},{384,6},{448,7},{1,8}... | collective-permute-start | bytes 49160 | tf_op jit(solution)/shard_map/ppermute | solution.py:165
  242.5 19.1 %all-to-all-start.9 = ((bf16[64,5,128]{2,1,0:T(8,128)(2,1)}), bf16[64,5,128]{2,1,0:T(8,128)(2,1)S(1)}, u32[]{:S(2)}, u32[]{:S(2)}) async-start(bf16[64,5,128]{2,1,0:T(8,128)(2,1)} %broadcast_in_dim.84), calls=%async_computation.9 | async-start | bytes 262144 | tf_op jit(solution)/shard_map/all_to_all | solution.py:38
  262.6 11.6 %all-to-all-start.10 = ((bf16[8,34,128]{2,1,0:T(8,128)(2,1)}), bf16[8,34,128]{2,1,0:T(8,128)(2,1)S(1)}, u32[]{:S(2)}, u32[]{:S(2)}) async-start(bf16[8,34,128]{2,1,0:T(8,128)(2,1)} %broadcast_in_dim.85), calls=%async_computation.10 | async-start | bytes 163840 | tf_op jit(solution)/shard_map/all_to_all | solution.py:38
Sparse Core Ops, SparseCore 0:
  10.1 116.9 all-gather.2

commit v7 on v6

--- a/solution.py
+++ b/solution.py
@@ -75,12 +75,6 @@
 
     panel = lax.all_gather(base_weight, "z", axis=0, tiled=False)
 
-    there = [((k * 8 + i) * 8 + t, (t * 8 + k) * 8 + i) for k in range(8) for i in range(8) for t in range(8)]
-    back = [(b, a) for a, b in there]
-    old = lax.ppermute(
-        jnp.concatenate([factors[0], first_moment[0], second_moment[0]], axis=0), AXES, there
-    )
-
     positions = jnp.arange(SEQLEN, dtype=jnp.int32)
     lower = prompt_len[:, None]
     upper = lower + resp_len[:, None]
@@ -91,7 +85,6 @@
     weighted = (cotangent.astype(f32) * weight[:, None]).astype(bf16)
 
     mine = share(factors[0].astype(bf16), XY, 32)
-    mine, old = lax.optimization_barrier((mine, old))
     other = core_swap(mine)
     low = jnp.where(core == 0, jnp.stack([mine, other], 1), jnp.stack([other, mine], 1))
     low = low.reshape(BLOCK, 2 * RANK)
@@ -118,13 +111,13 @@
     dims = (((0,), (0,)), ((), ()))
     grad_down = lax.dot_general(tokens, both[:, RANK:], dims, preferred_element_type=f32)
     grad_up = lax.dot_general(weighted, both[:, :RANK], dims, preferred_element_type=f32)
-    grads = jnp.concatenate([grad_down, grad_up], axis=1).astype(bf16).reshape(4, 2, 8, OWN, 128)
+    grads = jnp.concatenate([grad_down, grad_up], axis=1).astype(bf16).reshape(32, 2, OWN, 128)
     first = jnp.dot(first, base_weight, preferred_element_type=f32)
-    first = first.reshape(8, 2, 4, 2, TILE)
+    first = first.reshape(4, 2, 2, 8, TILE)
 
     def half(which):
-        base = pick(first, which, 3).transpose(0, 2, 1, 3).reshape(32, 4, 128)
-        return pick(grads, which, 1).transpose(1, 0, 2, 3).reshape(32, OWN, 128), base
+        base = pick(first, which, 1).transpose(2, 0, 1, 3).reshape(32, 4, 128)
+        return pick(grads, which, 1), base
 
     give, give_base = half(1 - core)
     keep, keep_base = half(core)
@@ -134,14 +127,16 @@
     got = swap(jnp.concatenate([keep, *high_low(keep_base)], axis=1), XY).astype(f32)
     got = jnp.sum(got, axis=0)
     base = got[OWN : OWN + 4] + got[OWN + 4 :]
+    own_grads = got[:OWN]
+    old = jnp.concatenate([factors[0], first_moment[0], second_moment[0]], axis=0)
     got = lax.ppermute(
-        jnp.concatenate([got[:OWN].astype(bf16), *high_low(base)], axis=0),
-        CROSS,
-        [(k * 8 + t, t * 8 + k) for k in range(8) for t in range(8)],
-    )
-    base = (got[OWN : OWN + 4].astype(f32) + got[OWN + 4 :].astype(f32)).reshape(2, TILE)
+        jnp.concatenate([own_grads.astype(bf16), old.astype(bf16), *high_low(base)], axis=0),
+        AXES,
+        [((k * 8 + i) * 8 + t, (t * 8 + k) * 8 + i) for k in range(8) for i in range(8) for t in range(8)],
+    )
+    base = (got[4 * OWN : 4 * OWN + 4].astype(f32) + got[4 * OWN + 4 :].astype(f32)).reshape(2, TILE)
     base = base + own_state.astype(f32)
-    got = share(jnp.concatenate([got[:OWN], old.astype(bf16)], axis=0), "z", 8).astype(f32)
+    got = share(got[: 4 * OWN], "z", 8).astype(f32)
     grads = scale * got[:, :OWN].reshape(TILE, 128)
     former = got[:, OWN:]
 
@@ -160,9 +155,8 @@
         )
         return values - rate * step_size
 
-    own_grads = lax.dynamic_slice_in_dim(grads, z * OWN, OWN, 0)
-    updated = update(old[:OWN], old[OWN : 2 * OWN], old[2 * OWN :], own_grads)
-    new_factors = lax.ppermute(updated, AXES, back)[None]
+    own_grads = clip * (scale * own_grads)
+    new_factors = update(factors[0], first_moment[0], second_moment[0], own_grads)[None]
 
     near = update(
         former[:, :OWN].reshape(TILE, 128),
@@ -195,8 +189,6 @@
         sums = sums.reshape(8, 2, 8, TILE).transpose(0, 2, 1, 3).reshape(64, 4, 128)
         sent = jnp.concatenate([sums, jnp.broadcast_to(extra[None], (64, 2, 128))], axis=1)
         got = jnp.sum(swap(sent, DP).astype(f32), axis=0)
-        if step == 1:
-            got, new_factors = lax.optimization_barrier((got, new_factors))
         thin = got[4].reshape(2, RANK)
         squares = got[5].reshape(2, 2, 32)[:, :, 0]
         norm = lax.rsqrt((squares[:, :1] + squares[:, 1:]) / MODEL_WIDTH + 1e-05)

time: 284 us -> 265 us (0.933)
  starting transfers between devices: 90.2 us -> 72.2 us
  waiting for transfers between devices: 77.5 us -> 93.1 us
  blocking collectives: 59.8 us -> 44.5 us
    all_to_all x8, waiting for transfers between devices: 68.4 us -> 87.4 us  [swap(): return lax.all_to_all(chunks, axes, 0, 0, tiled=False)]
    all_to_all x3, blocking collectives: 59.8 us -> 44.5 us  [swap(): return lax.all_to_all(chunks, axes, 0, 0, tiled=False)]
    all_to_all x8, starting transfers between devices: 72 us -> 57.5 us  [swap(): return lax.all_to_all(chunks, axes, 0, 0, tiled=False)]
    ppermute x3 -> x1, starting transfers between devices: 13 us -> 6.09 us  [body(): lax.ppermute(jnp.concatenate([own_grads.astype(bf16), old.astype(bf16), *...]
    ppermute x3 -> x1, waiting for transfers between devices: 7.41 us -> 3.86 us  [body(): lax.ppermute(jnp.concatenate([own_grads.astype(bf16), old.astype(bf16), *...]
    ppermute x2, starting transfers between devices: 5.21 us -> 8.56 us  [core_swap(): return lax.ppermute(value, 'core', [(0, 1), (1, 0)])]
  transfers between devices with their start and end apart: 14 -> 12, of which waited for: 9 -> 10; matrix products, arithmetic and copies ran while one was open for 6% -> 6% of each run, Pallas kernels for 0% -> 0%
where the time goes in v7:
time: 265 us; the launch traced here: 264 us
  waiting for transfers between devices  93.1 us (35%)
  starting transfers between devices  72.2 us (27%)
  blocking collectives  44.5 us (17%)
  matrix products  18.6 us (7%)
  between operations  16.6 us (6%)
  local copies, waits for them, and re-layouts  12 us (5%)
  other arithmetic  7.2 us (3%)
    all_to_all x8, waiting for transfers between devices, swap(): return lax.all_to_all(chunks, axes, 0, 0, tiled=False)  87.4 us
    all_to_all x8, starting transfers between devices, swap(): return lax.all_to_all(chunks, axes, 0, 0, tiled=False)  57.5 us
    all_to_all x3, blocking collectives, swap(): return lax.all_to_all(chunks, axes, 0, 0, tiled=False)  44.5 us
    dot_general x3, matrix products, body(): jnp.einsum('zsk,zkn->zsn', jnp.broadcast_to(own[None], (8, 2, TILE)), pan...  13.7 us
    ppermute x2, starting transfers between devices, core_swap(): return lax.ppermute(value, 'core', [(0, 1), (1, 0)])  8.56 us
    ppermute x1, starting transfers between devices, body(): lax.ppermute(jnp.concatenate([own_grads.astype(bf16), old.astype(bf16), *...  6.09 us
  transfers between devices with their start and end apart: 12, of which 10 were waited for; matrix products, arithmetic and copies ran while one was open for 6% of the time, Pallas kernels for 0%

profile of v7, /device:TPU:1, one launch (start us, length us, event | category | flops | bytes accessed | tf_op | source)
XLA Modules:
  0.0 264.2 jit_solution(4391618660941746861)
XLA Ops:
  9.5 10.5 %all-to-all-start = ((bf16[32,32,128]{2,1,0:T(8,128)(2,1)}), bf16[32,32,128]{2,1,0:T(8,128)(2,1)S(1)}, u32[]{:S(2)}, u32[]{:S(2)}) async-start(bf16[32,32,128]{2,1,0:T(8,128)(2,1)} %broadcast_in_dim.61), calls=%async_computation | async-start | bytes 524288 | tf_op jit(solution)/shard_map/all_to_all | solution.py:38
  20.0 9.7 %all-to-all-done = bf16[32,32,128]{2,1,0:T(8,128)(2,1)S(1)} async-done(((bf16[32,32,128]{2,1,0:T(8,128)(2,1)}), bf16[32,32,128]{2,1,0:T(8,128)(2,1)S(1)}, u32[]{:S(2)}, u32[]{:S(2)}) %all-to-all-start) | async-done | bytes 262176 | tf_op jit(solution)/shard_map/all_to_all | solution.py:38
  29.7 5.6 %collective-permute-start = (bf16[32,32,128]{2,1,0:T(8,128)(2,1)S(1)}, bf16[32,32,128]{2,1,0:T(8,128)(2,1)S(1)}, u32[]{:S(2)}, u32[]{:S(2)}) collective-permute-start(bf16[32,32,128]{2,1,0:T(8,128)(2,1)S(1)} %all-to-all-done), channel_id=1, source_target_pairs={{0,8},{8,0},{1,9},{9,1},{2,10},{10,2},{3,11},{11,3},{4,12},{12,4},... | collective-permute-start | bytes 786440 | tf_op jit(solution)/shard_map/ppermute | solution.py:46
  39.6 1.7 convolution_convert_fusion.5
  41.5 0.8 broadcast_in_dim.65
  42.4 10.0 %all-to-all-start.1 = ((bf16[8,164,128]{2,1,0:T(8,128)(2,1)}), bf16[8,164,128]{2,1,0:T(8,128)(2,1)S(1)}, u32[]{:S(2)}, u32[]{:S(2)}) async-start(bf16[8,164,128]{2,1,0:T(8,128)(2,1)} %broadcast_in_dim.65), calls=%async_computation.1 | async-start | bytes 688128 | tf_op jit(solution)/shard_map/all_to_all | solution.py:38
  52.4 1.5 copy.80
  53.9 16.0 %all-to-all-done.1 = bf16[8,164,128]{2,1,0:T(8,128)(2,1)S(1)} async-done(((bf16[8,164,128]{2,1,0:T(8,128)(2,1)}), bf16[8,164,128]{2,1,0:T(8,128)(2,1)S(1)}, u32[]{:S(2)}, u32[]{:S(2)}) %all-to-all-start.1) | async-done | bytes 335904 | tf_op jit(solution)/shard_map/all_to_all | solution.py:38
  72.0 2.9 %collective-permute-start.1 = (bf16[32,40,128]{2,1,0:T(8,128)(2,1)S(1)}, bf16[32,40,128]{2,1,0:T(8,128)(2,1)S(1)}, u32[]{:S(2)}, u32[]{:S(2)}) collective-permute-start(bf16[32,40,128]{2,1,0:T(8,128)(2,1)S(1)} %pad_maximum_fusion), channel_id=1, source_target_pairs={{0,8},{8,0},{1,9},{9,1},{2,10},{10,2},{3,11},{11,3},{4,12},{12,4},... | collective-permute-start | bytes 983048 | tf_op jit(solution)/shard_map/ppermute | solution.py:46
  75.1 1.1 collective-permute-done.1
  76.5 0.8 pad_maximum_fusion.1
  77.3 4.1 %all-to-all-start.2 = ((bf16[32,40,128]{2,1,0:T(8,128)(2,1)}), bf16[32,40,128]{2,1,0:T(8,128)(2,1)S(1)}, u32[]{:S(2)}, u32[]{:S(2)}) async-start(bf16[32,40,128]{2,1,0:T(8,128)(2,1)} %pad_maximum_fusion.1), calls=%async_computation.2 | async-start | bytes 655360 | tf_op jit(solution)/shard_map/all_to_all | solution.py:38
  81.5 10.4 %all-to-all-done.2 = bf16[32,40,128]{2,1,0:T(8,128)(2,1)S(1)} async-done(((bf16[32,40,128]{2,1,0:T(8,128)(2,1)}), bf16[32,40,128]{2,1,0:T(8,128)(2,1)S(1)}, u32[]{:S(2)}, u32[]{:S(2)}) %all-to-all-start.2) | async-done | bytes 327712 | tf_op jit(solution)/shard_map/all_to_all | solution.py:38
  92.1 6.1 %collective-permute-start.2 = (bf16[136,128]{1,0:T(8,128)(2,1)S(1)}, bf16[136,128]{1,0:T(8,128)(2,1)S(1)}, u32[]{:S(2)}, u32[]{:S(2)}) collective-permute-start(bf16[136,128]{1,0:T(8,128)(2,1)S(1)} %concatenate.71), channel_id=1, source_target_pairs={{0,0},{1,64},{2,128},{3,192},{4,256},{5,320},{6,384},{7,448},{8,1}... | collective-permute-start | bytes 104456 | tf_op jit(solution)/shard_map/ppermute | solution.py:132
  98.2 3.9 %collective-permute-done.2 = bf16[136,128]{1,0:T(8,128)(2,1)S(1)} collective-permute-done((bf16[136,128]{1,0:T(8,128)(2,1)S(1)}, bf16[136,128]{1,0:T(8,128)(2,1)S(1)}, u32[]{:S(2)}, u32[]{:S(2)}) %collective-permute-start.2) | collective-permute-done | bytes 34848 | tf_op jit(solution)/shard_map/ppermute | solution.py:132
  102.8 6.6 %all-to-all-start.3 = ((bf16[8,128,128]{2,1,0:T(8,128)(2,1)}), bf16[8,128,128]{2,1,0:T(8,128)(2,1)S(1)}, u32[]{:S(2)}, u32[]{:S(2)}) async-start(bf16[8,128,128]{2,1,0:T(8,128)(2,1)} %broadcast_in_dim.66), calls=%async_computation.3 | async-start | bytes 524288 | tf_op jit(solution)/shard_map/all_to_all | solution.py:38
  109.4 14.5 %all-to-all-done.3 = bf16[8,128,128]{2,1,0:T(8,128)(2,1)S(1)} async-done(((bf16[8,128,128]{2,1,0:T(8,128)(2,1)}), bf16[8,128,128]{2,1,0:T(8,128)(2,1)S(1)}, u32[]{:S(2)}, u32[]{:S(2)}) %all-to-all-start.3) | async-done | bytes 262176 | tf_op jit(solution)/shard_map/all_to_all | solution.py:38
  124.6 1.3 broadcast_in_dim_broadcast_in_dim_broadcast_in_dim.3
  125.9 10.8 %all-to-all-start.4 = ((f32[64,1,128]{2,1,0:T(1,128)}), f32[64,1,128]{2,1,0:T(1,128)S(1)}, u32[]{:S(2)}, u32[]{:S(2)}) async-start(f32[64,1,128]{2,1,0:T(1,128)} %broadcast_in_dim_broadcast_in_dim_broadcast_in_dim.3), calls=%async_computation.4 | async-start | bytes 65536 | tf_op jit(solution)/shard_map/all_to_all | solution.py:38
  136.7 9.2 %all-to-all-done.4 = f32[64,1,128]{2,1,0:T(1,128)S(1)} async-done(((f32[64,1,128]{2,1,0:T(1,128)}), f32[64,1,128]{2,1,0:T(1,128)S(1)}, u32[]{:S(2)}, u32[]{:S(2)}) %all-to-all-start.4) | async-done | bytes 32800 | tf_op jit(solution)/shard_map/all_to_all | solution.py:38
  146.9 4.7 %all-to-all-start.5 = ((f32[64,1,128]{2,1,0:T(1,128)}), f32[64,1,128]{2,1,0:T(1,128)S(1)}, u32[]{:S(2)}, u32[]{:S(2)}) async-start(f32[64,1,128]{2,1,0:T(1,128)} %broadcast_in_dim.69), calls=%async_computation.5 | async-start | bytes 65536 | tf_op jit(solution)/shard_map/all_to_all | solution.py:38
  151.6 9.3 %all-to-all-done.5 = f32[64,1,128]{2,1,0:T(1,128)S(1)} async-done(((f32[64,1,128]{2,1,0:T(1,128)}), f32[64,1,128]{2,1,0:T(1,128)S(1)}, u32[]{:S(2)}, u32[]{:S(2)}) %all-to-all-start.5) | async-done | bytes 32800 | tf_op jit(solution)/shard_map/all_to_all | solution.py:38
  162.0 4.6 %convolution_convert_fusion.4 = bf16[8,2,2048]{2,1,0:T(2,128)(2,1)S(1)} fusion(bf16[8,256,2048]{2,1,0:T(8,128)(2,1)} %bitcast.114, bf16[2,256]{1,0:T(2,128)(2,1)S(1)} %get-tuple-element.23), kind=kOutput, calls=%fused_computation.5 | convolution fusion | flops 16809984 | bytes 8455168 | tf_op jit(solution)/shard_map/zsk,zkn->zsn/dot_general | solution.py:182
  166.7 14.4 %all_to_all.55 = bf16[64,6,128]{2,1,0:T(8,128)(2,1)S(1)} all-to-all(bf16[64,6,128]{2,1,0:T(8,128)(2,1)S(1)} %pad_maximum_fusion.2), channel_id=1, replica_groups=mesh['x'=4,'ya'=2,'yb'=2,'yc'=2,'core'=2,'z'=8] {'x','ya','yb','yc','core'}, dimensions={0} | all-to-all | bytes 196608 | tf_op jit(solution)/shard_map/all_to_all | solution.py:38
  182.2 4.6 %convolution_convert_fusion.3 = bf16[8,2,2048]{2,1,0:T(2,128)(2,1)S(1)} fusion(bf16[8,256,2048]{2,1,0:T(8,128)(2,1)} %bitcast.115, bf16[2,256]{1,0:T(2,128)(2,1)S(1)} %get-tuple-element.31), kind=kOutput, calls=%fused_computation.4 | convolution fusion | flops 16809984 | bytes 8455168 | tf_op jit(solution)/shard_map/zsk,zkn->zsn/dot_general | solution.py:182
  187.3 15.0 %all_to_all.56 = bf16[64,6,128]{2,1,0:T(8,128)(2,1)S(1)} all-to-all(bf16[64,6,128]{2,1,0:T(8,128)(2,1)S(1)} %pad_maximum_fusion.3), channel_id=1, replica_groups=mesh['x'=4,'ya'=2,'yb'=2,'yc'=2,'core'=2,'z'=8] {'x','ya','yb','yc','core'}, dimensions={0} | all-to-all | bytes 196608 | tf_op jit(solution)/shard_map/all_to_all | solution.py:38
  203.5 4.6 %convolution_convert_fusion.2 = bf16[8,2,2048]{2,1,0:T(2,128)(2,1)S(1)} fusion(bf16[8,256,2048]{2,1,0:T(8,128)(2,1)} %bitcast.116, bf16[2,256]{1,0:T(2,128)(2,1)S(1)} %get-tuple-element.29), kind=kOutput, calls=%fused_computation.3 | convolution fusion | flops 16809984 | bytes 8455168 | tf_op jit(solution)/shard_map/zsk,zkn->zsn/dot_general | solution.py:182
  208.6 15.0 %all_to_all.57 = bf16[64,6,128]{2,1,0:T(8,128)(2,1)S(1)} all-to-all(bf16[64,6,128]{2,1,0:T(8,128)(2,1)S(1)} %pad_maximum_fusion.4), channel_id=1, replica_groups=mesh['x'=4,'ya'=2,'yb'=2,'yc'=2,'core'=2,'z'=8] {'x','ya','yb','yc','core'}, dimensions={0} | all-to-all | bytes 196608 | tf_op jit(solution)/shard_map/all_to_all | solution.py:38
  225.6 4.6 %all-to-all-start.9 = ((bf16[64,5,128]{2,1,0:T(8,128)(2,1)}), bf16[64,5,128]{2,1,0:T(8,128)(2,1)S(1)}, u32[]{:S(2)}, u32[]{:S(2)}) async-start(bf16[64,5,128]{2,1,0:T(8,128)(2,1)} %broadcast_in_dim.84), calls=%async_computation.9 | async-start | bytes 262144 | tf_op jit(solution)/shard_map/all_to_all | solution.py:38
  230.2 13.7 %all-to-all-done.9 = bf16[64,5,128]{2,1,0:T(8,128)(2,1)S(1)} async-done(((bf16[64,5,128]{2,1,0:T(8,128)(2,1)}), bf16[64,5,128]{2,1,0:T(8,128)(2,1)S(1)}, u32[]{:S(2)}, u32[]{:S(2)}) %all-to-all-start.9) | async-done | bytes 81952 | tf_op jit(solution)/shard_map/all_to_all | solution.py:38
  244.9 6.2 %all-to-all-start.10 = ((bf16[8,34,128]{2,1,0:T(8,128)(2,1)}), bf16[8,34,128]{2,1,0:T(8,128)(2,1)S(1)}, u32[]{:S(2)}, u32[]{:S(2)}) async-start(bf16[8,34,128]{2,1,0:T(8,128)(2,1)} %broadcast_in_dim.85), calls=%async_computation.10 | async-start | bytes 163840 | tf_op jit(solution)/shard_map/all_to_all | solution.py:38
  251.7 4.6 %all-to-all-done.10 = bf16[8,34,128]{2,1,0:T(8,128)(2,1)S(1)} async-done(((bf16[8,34,128]{2,1,0:T(8,128)(2,1)}), bf16[8,34,128]{2,1,0:T(8,128)(2,1)S(1)}, u32[]{:S(2)}, u32[]{:S(2)}) %all-to-all-start.10) | async-done | bytes 69664 | tf_op jit(solution)/shard_map/all_to_all | solution.py:38
  (158 shorter events, 18.7 us)
Async XLA Ops:
  7.2 32.1 %copy-start = (bf16[128,2048]{1,0:T(8,128)(2,1)S(1)}, bf16[128,2048]{1,0:T(8,128)(2,1)}, u32[]{:S(2)}) copy-start(bf16[128,2048]{1,0:T(8,128)(2,1)} %param.11) | copy-start | bytes 1572868
  7.2 64.0 %copy-start.1 = (bf16[128,2048]{1,0:T(8,128)(2,1)S(1)}, bf16[128,2048]{1,0:T(8,128)(2,1)}, u32[]{:S(2)}) copy-start(bf16[128,2048]{1,0:T(8,128)(2,1)} %param.12) | copy-start | bytes 1572868
  7.2 154.8 %all-gather.3.cloned.1.call-start = ((), (), s32[]{:S(2)}) async-start(), calls=%async_computation.11 | async-start | bytes 9437184 | tf_op jit(solution)/shard_map/all_gather | solution.py:76
  9.5 20.2 %all-to-all-start = ((bf16[32,32,128]{2,1,0:T(8,128)(2,1)}), bf16[32,32,128]{2,1,0:T(8,128)(2,1)S(1)}, u32[]{:S(2)}, u32[]{:S(2)}) async-start(bf16[32,32,128]{2,1,0:T(8,128)(2,1)} %broadcast_in_dim.61), calls=%async_computation | async-start | bytes 524288 | tf_op jit(solution)/shard_map/all_to_all | solution.py:38
  29.7 9.5 %collective-permute-start = (bf16[32,32,128]{2,1,0:T(8,128)(2,1)S(1)}, bf16[32,32,128]{2,1,0:T(8,128)(2,1)S(1)}, u32[]{:S(2)}, u32[]{:S(2)}) collective-permute-start(bf16[32,32,128]{2,1,0:T(8,128)(2,1)S(1)} %all-to-all-done), channel_id=1, source_target_pairs={{0,8},{8,0},{1,9},{9,1},{2,10},{10,2},{3,11},{11,3},{4,12},{12,4},... | collective-permute-start | bytes 786440 | tf_op jit(solution)/shard_map/ppermute | solution.py:46
  39.6 41.8 %copy-start.2 = (f32[1,32,128]{2,1,0:T(8,128)S(1)}, f32[1,32,128]{2,1,0:T(8,128)}, u32[]{:S(2)}) copy-start(f32[1,32,128]{2,1,0:T(8,128)} %param.18) | copy-start | bytes 49156
  39.6 41.8 %copy-start.3 = (f32[1,32,128]{2,1,0:T(8,128)S(1)}, f32[1,32,128]{2,1,0:T(8,128)}, u32[]{:S(2)}) copy-start(f32[1,32,128]{2,1,0:T(8,128)} %param.17) | copy-start | bytes 49156
  42.4 27.6 %all-to-all-start.1 = ((bf16[8,164,128]{2,1,0:T(8,128)(2,1)}), bf16[8,164,128]{2,1,0:T(8,128)(2,1)S(1)}, u32[]{:S(2)}, u32[]{:S(2)}) async-start(bf16[8,164,128]{2,1,0:T(8,128)(2,1)} %broadcast_in_dim.65), calls=%async_computation.1 | async-start | bytes 688128 | tf_op jit(solution)/shard_map/all_to_all | solution.py:38
  72.0 4.2 %collective-permute-start.1 = (bf16[32,40,128]{2,1,0:T(8,128)(2,1)S(1)}, bf16[32,40,128]{2,1,0:T(8,128)(2,1)S(1)}, u32[]{:S(2)}, u32[]{:S(2)}) collective-permute-start(bf16[32,40,128]{2,1,0:T(8,128)(2,1)S(1)} %pad_maximum_fusion), channel_id=1, source_target_pairs={{0,8},{8,0},{1,9},{9,1},{2,10},{10,2},{3,11},{11,3},{4,12},{12,4},... | collective-permute-start | bytes 983048 | tf_op jit(solution)/shard_map/ppermute | solution.py:46
  77.3 14.6 %all-to-all-start.2 = ((bf16[32,40,128]{2,1,0:T(8,128)(2,1)}), bf16[32,40,128]{2,1,0:T(8,128)(2,1)S(1)}, u32[]{:S(2)}, u32[]{:S(2)}) async-start(bf16[32,40,128]{2,1,0:T(8,128)(2,1)} %pad_maximum_fusion.1), calls=%async_computation.2 | async-start | bytes 655360 | tf_op jit(solution)/shard_map/all_to_all | solution.py:38
  92.1 10.0 %collective-permute-start.2 = (bf16[136,128]{1,0:T(8,128)(2,1)S(1)}, bf16[136,128]{1,0:T(8,128)(2,1)S(1)}, u32[]{:S(2)}, u32[]{:S(2)}) collective-permute-start(bf16[136,128]{1,0:T(8,128)(2,1)S(1)} %concatenate.71), channel_id=1, source_target_pairs={{0,0},{1,64},{2,128},{3,192},{4,256},{5,320},{6,384},{7,448},{8,1}... | collective-permute-start | bytes 104456 | tf_op jit(solution)/shard_map/ppermute | solution.py:132
  102.8 21.2 %all-to-all-start.3 = ((bf16[8,128,128]{2,1,0:T(8,128)(2,1)}), bf16[8,128,128]{2,1,0:T(8,128)(2,1)S(1)}, u32[]{:S(2)}, u32[]{:S(2)}) async-start(bf16[8,128,128]{2,1,0:T(8,128)(2,1)} %broadcast_in_dim.66), calls=%async_computation.3 | async-start | bytes 524288 | tf_op jit(solution)/shard_map/all_to_all | solution.py:38
  125.9 20.0 %all-to-all-start.4 = ((f32[64,1,128]{2,1,0:T(1,128)}), f32[64,1,128]{2,1,0:T(1,128)S(1)}, u32[]{:S(2)}, u32[]{:S(2)}) async-start(f32[64,1,128]{2,1,0:T(1,128)} %broadcast_in_dim_broadcast_in_dim_broadcast_in_dim.3), calls=%async_computation.4 | async-start | bytes 65536 | tf_op jit(solution)/shard_map/all_to_all | solution.py:38
  146.9 14.0 %all-to-all-start.5 = ((f32[64,1,128]{2,1,0:T(1,128)}), f32[64,1,128]{2,1,0:T(1,128)S(1)}, u32[]{:S(2)}, u32[]{:S(2)}) async-start(f32[64,1,128]{2,1,0:T(1,128)} %broadcast_in_dim.69), calls=%async_computation.5 | async-start | bytes 65536 | tf_op jit(solution)/shard_map/all_to_all | solution.py:38
  186.8 64.3 %copy-start.4 = (f32[1,32,128]{2,1,0:T(8,128)S(1)}, f32[1,32,128]{2,1,0:T(8,128)}, u32[]{:S(2)}) copy-start(f32[1,32,128]{2,1,0:T(8,128)} %param.16) | copy-start | bytes 49156
  225.6 18.3 %all-to-all-start.9 = ((bf16[64,5,128]{2,1,0:T(8,128)(2,1)}), bf16[64,5,128]{2,1,0:T(8,128)(2,1)S(1)}, u32[]{:S(2)}, u32[]{:S(2)}) async-start(bf16[64,5,128]{2,1,0:T(8,128)(2,1)} %broadcast_in_dim.84), calls=%async_computation.9 | async-start | bytes 262144 | tf_op jit(solution)/shard_map/all_to_all | solution.py:38
  244.9 11.4 %all-to-all-start.10 = ((bf16[8,34,128]{2,1,0:T(8,128)(2,1)}), bf16[8,34,128]{2,1,0:T(8,128)(2,1)S(1)}, u32[]{:S(2)}, u32[]{:S(2)}) async-start(bf16[8,34,128]{2,1,0:T(8,128)(2,1)} %broadcast_in_dim.85), calls=%async_computation.10 | async-start | bytes 163840 | tf_op jit(solution)/shard_map/all_to_all | solution.py:38
Sparse Core Ops, SparseCore 0:
  10.1 119.0 all-gather.2

commit v8 on v7

--- a/solution.py
+++ b/solution.py
@@ -83,6 +83,7 @@
     per_seq = advantage / resp_len.astype(f32)
     weight = jnp.where(inside, per_seq[:, None], f32(0.0)).reshape(-1)
     weighted = (cotangent.astype(f32) * weight[:, None]).astype(bf16)
+    weighted = lax.optimization_barrier(weighted)
 
     mine = share(factors[0].astype(bf16), XY, 32)
     other = core_swap(mine)
@@ -136,12 +137,14 @@
     )
     base = (got[4 * OWN : 4 * OWN + 4].astype(f32) + got[4 * OWN + 4 :].astype(f32)).reshape(2, TILE)
     base = base + own_state.astype(f32)
-    got = share(got[: 4 * OWN], "z", 8).astype(f32)
+    own_grads = scale * own_grads
+    squared = jnp.broadcast_to(jnp.sum(own_grads * own_grads), (1, 128))
+    squared = jnp.sum(share(squared, DP, 64), axis=0)
+    got = share(jnp.concatenate([got[: 4 * OWN], *high_low(squared)], axis=0), "z", 8).astype(f32)
     grads = scale * got[:, :OWN].reshape(TILE, 128)
-    former = got[:, OWN:]
-
-    squared = jnp.broadcast_to(jnp.sum(grads * grads), (1, 128))
-    squared = jnp.sum(share(squared, DP, 64), axis=0)
+    former = got[:, OWN : 4 * OWN]
+    squared = jnp.sum(got[:, 4 * OWN :], axis=(0, 1))[None]
+
     clip = jnp.minimum(f32(1.0), f32(1.0) / (jnp.sqrt(squared) + 1e-06))
     grads = clip * grads
 
@@ -155,7 +158,7 @@
         )
         return values - rate * step_size
 
-    own_grads = clip * (scale * own_grads)
+    own_grads = clip * own_grads
     new_factors = update(factors[0], first_moment[0], second_moment[0], own_grads)[None]
 
     near = update(

time: 265 us -> 256 us (0.966)
  waiting for transfers between devices: 93.1 us -> 82.9 us
    all_to_all x8, waiting for transfers between devices: 87.4 us -> 74.5 us  [swap(): return lax.all_to_all(chunks, axes, 0, 0, tiled=False)]
    all_to_all x8, starting transfers between devices: 57.5 us -> 61 us  [swap(): return lax.all_to_all(chunks, axes, 0, 0, tiled=False)]
    ppermute x1, starting transfers between devices: 6.09 us -> 2.77 us  [body(): lax.ppermute(jnp.concatenate([own_grads.astype(bf16), old.astype(bf16), *...]
    ppermute x1, waiting for transfers between devices: 3.86 us -> 6.6 us  [body(): lax.ppermute(jnp.concatenate([own_grads.astype(bf16), old.astype(bf16), *...]
  transfers between devices with their start and end apart: 12 -> 12, of which waited for: 10 -> 9; matrix products, arithmetic and copies ran while one was open for 6% -> 7% of each run, Pallas kernels for 0% -> 0%
where the time goes in v8:
time: 256 us; the launch traced here: 255 us
  waiting for transfers between devices  82.9 us (32%)
  starting transfers between devices  72.6 us (28%)
  blocking collectives  44.5 us (17%)
  matrix products  17.5 us (7%)
  between operations  16.6 us (6%)
  local copies, waits for them, and re-layouts  11.7 us (5%)
  other arithmetic  9.1 us (4%)
    all_to_all x8, waiting for transfers between devices, swap(): return lax.all_to_all(chunks, axes, 0, 0, tiled=False)  74.5 us
    all_to_all x8, starting transfers between devices, swap(): return lax.all_to_all(chunks, axes, 0, 0, tiled=False)  61 us
    all_to_all x3, blocking collectives, swap(): return lax.all_to_all(chunks, axes, 0, 0, tiled=False)  44.5 us
    dot_general x3, matrix products, body(): jnp.einsum('zsk,zkn->zsn', jnp.broadcast_to(own[None], (8, 2, TILE)), pan...  13.7 us
    ppermute x2, starting transfers between devices, core_swap(): return lax.ppermute(value, 'core', [(0, 1), (1, 0)])  8.83 us
    ppermute x1, waiting for transfers between devices, body(): lax.ppermute(jnp.concatenate([own_grads.astype(bf16), old.astype(bf16), *...  6.6 us
  transfers between devices with their start and end apart: 12, of which 9 were waited for; matrix products, arithmetic and copies ran while one was open for 7% of the time, Pallas kernels for 0%

profile of v8, /device:TPU:1, one launch (start us, length us, event | category | flops | bytes accessed | tf_op | source)
XLA Modules:
  0.0 254.8 jit_solution(6006389162315254038)
XLA Ops:
  7.9 0.8 bitcast_convert_fusion
  9.5 10.5 %all-to-all-start = ((bf16[32,32,128]{2,1,0:T(8,128)(2,1)}), bf16[32,32,128]{2,1,0:T(8,128)(2,1)S(1)}, u32[]{:S(2)}, u32[]{:S(2)}) async-start(bf16[32,32,128]{2,1,0:T(8,128)(2,1)} %broadcast_in_dim.61), calls=%async_computation | async-start | bytes 524288 | tf_op jit(solution)/shard_map/all_to_all | solution.py:38
  23.9 5.8 %all-to-all-done = bf16[32,32,128]{2,1,0:T(8,128)(2,1)S(1)} async-done(((bf16[32,32,128]{2,1,0:T(8,128)(2,1)}), bf16[32,32,128]{2,1,0:T(8,128)(2,1)S(1)}, u32[]{:S(2)}, u32[]{:S(2)}) %all-to-all-start) | async-done | bytes 262176 | tf_op jit(solution)/shard_map/all_to_all | solution.py:38
  29.7 5.6 %collective-permute-start = (bf16[32,32,128]{2,1,0:T(8,128)(2,1)S(1)}, bf16[32,32,128]{2,1,0:T(8,128)(2,1)S(1)}, u32[]{:S(2)}, u32[]{:S(2)}) collective-permute-start(bf16[32,32,128]{2,1,0:T(8,128)(2,1)S(1)} %all-to-all-done), channel_id=1, source_target_pairs={{0,8},{8,0},{1,9},{9,1},{2,10},{10,2},{3,11},{11,3},{4,12},{12,4},... | collective-permute-start | bytes 786440 | tf_op jit(solution)/shard_map/ppermute | solution.py:46
  35.3 1.2 multiply_convert_fusion
  37.8 0.8 broadcast_in_dim.65
  38.6 10.0 %all-to-all-start.1 = ((bf16[8,164,128]{2,1,0:T(8,128)(2,1)}), bf16[8,164,128]{2,1,0:T(8,128)(2,1)S(1)}, u32[]{:S(2)}, u32[]{:S(2)}) async-start(bf16[8,164,128]{2,1,0:T(8,128)(2,1)} %broadcast_in_dim.65), calls=%async_computation.1 | async-start | bytes 688128 | tf_op jit(solution)/shard_map/all_to_all | solution.py:38
  49.2 16.8 %all-to-all-done.1 = bf16[8,164,128]{2,1,0:T(8,128)(2,1)S(1)} async-done(((bf16[8,164,128]{2,1,0:T(8,128)(2,1)}), bf16[8,164,128]{2,1,0:T(8,128)(2,1)S(1)}, u32[]{:S(2)}, u32[]{:S(2)}) %all-to-all-start.1) | async-done | bytes 335904 | tf_op jit(solution)/shard_map/all_to_all | solution.py:38
  68.7 3.2 %collective-permute-start.1 = (bf16[32,40,128]{2,1,0:T(8,128)(2,1)S(1)}, bf16[32,40,128]{2,1,0:T(8,128)(2,1)S(1)}, u32[]{:S(2)}, u32[]{:S(2)}) collective-permute-start(bf16[32,40,128]{2,1,0:T(8,128)(2,1)S(1)} %pad_maximum_fusion), channel_id=1, source_target_pairs={{0,8},{8,0},{1,9},{9,1},{2,10},{10,2},{3,11},{11,3},{4,12},{12,4},... | collective-permute-start | bytes 983048 | tf_op jit(solution)/shard_map/ppermute | solution.py:46
  72.0 1.1 collective-permute-done.1
  73.4 0.8 pad_maximum_fusion.1
  74.2 4.1 %all-to-all-start.2 = ((bf16[32,40,128]{2,1,0:T(8,128)(2,1)}), bf16[32,40,128]{2,1,0:T(8,128)(2,1)S(1)}, u32[]{:S(2)}, u32[]{:S(2)}) async-start(bf16[32,40,128]{2,1,0:T(8,128)(2,1)} %pad_maximum_fusion.1), calls=%async_computation.2 | async-start | bytes 655360 | tf_op jit(solution)/shard_map/all_to_all | solution.py:38
  78.4 10.4 %all-to-all-done.2 = bf16[32,40,128]{2,1,0:T(8,128)(2,1)S(1)} async-done(((bf16[32,40,128]{2,1,0:T(8,128)(2,1)}), bf16[32,40,128]{2,1,0:T(8,128)(2,1)S(1)}, u32[]{:S(2)}, u32[]{:S(2)}) %all-to-all-start.2) | async-done | bytes 327712 | tf_op jit(solution)/shard_map/all_to_all | solution.py:38
  89.5 1.3 broadcast_in_dim_broadcast_in_dim_broadcast_in_dim.3
  90.7 8.9 %all-to-all-start.3 = ((f32[64,1,128]{2,1,0:T(1,128)}), f32[64,1,128]{2,1,0:T(1,128)S(1)}, u32[]{:S(2)}, u32[]{:S(2)}) async-start(f32[64,1,128]{2,1,0:T(1,128)} %broadcast_in_dim_broadcast_in_dim_broadcast_in_dim.3), calls=%async_computation.3 | async-start | bytes 65536 | tf_op jit(solution)/shard_map/all_to_all | solution.py:38
  99.8 2.8 %collective-permute-start.2 = (bf16[136,128]{1,0:T(8,128)(2,1)S(1)}, bf16[136,128]{1,0:T(8,128)(2,1)S(1)}, u32[]{:S(2)}, u32[]{:S(2)}) collective-permute-start(bf16[136,128]{1,0:T(8,128)(2,1)S(1)} %concatenate.74), channel_id=1, source_target_pairs={{0,0},{1,64},{2,128},{3,192},{4,256},{5,320},{6,384},{7,448},{8,1}... | collective-permute-start | bytes 104456 | tf_op jit(solution)/shard_map/ppermute | solution.py:133
  102.5 6.6 %collective-permute-done.2 = bf16[136,128]{1,0:T(8,128)(2,1)S(1)} collective-permute-done((bf16[136,128]{1,0:T(8,128)(2,1)S(1)}, bf16[136,128]{1,0:T(8,128)(2,1)S(1)}, u32[]{:S(2)}, u32[]{:S(2)}) %collective-permute-start.2) | collective-permute-done | bytes 34848 | tf_op jit(solution)/shard_map/ppermute | solution.py:133
  109.2 0.8 broadcast_in_dim.66
  110.0 7.4 %all-to-all-start.4 = ((bf16[8,130,128]{2,1,0:T(8,128)(2,1)}), bf16[8,130,128]{2,1,0:T(8,128)(2,1)S(1)}, u32[]{:S(2)}, u32[]{:S(2)}) async-start(bf16[8,130,128]{2,1,0:T(8,128)(2,1)} %broadcast_in_dim.66), calls=%async_computation.4 | async-start | bytes 557056 | tf_op jit(solution)/shard_map/all_to_all | solution.py:38
  118.0 14.0 %all-to-all-done.4 = bf16[8,130,128]{2,1,0:T(8,128)(2,1)S(1)} async-done(((bf16[8,130,128]{2,1,0:T(8,128)(2,1)}), bf16[8,130,128]{2,1,0:T(8,128)(2,1)S(1)}, u32[]{:S(2)}, u32[]{:S(2)}) %all-to-all-start.4) | async-done | bytes 266272 | tf_op jit(solution)/shard_map/all_to_all | solution.py:38
  133.2 9.1 %all-to-all-start.5 = ((f32[64,1,128]{2,1,0:T(1,128)}), f32[64,1,128]{2,1,0:T(1,128)S(1)}, u32[]{:S(2)}, u32[]{:S(2)}) async-start(f32[64,1,128]{2,1,0:T(1,128)} %broadcast_in_dim.69), calls=%async_computation.5 | async-start | bytes 65536 | tf_op jit(solution)/shard_map/all_to_all | solution.py:38
  142.3 9.2 %all-to-all-done.5 = f32[64,1,128]{2,1,0:T(1,128)S(1)} async-done(((f32[64,1,128]{2,1,0:T(1,128)}), f32[64,1,128]{2,1,0:T(1,128)S(1)}, u32[]{:S(2)}, u32[]{:S(2)}) %all-to-all-start.5) | async-done | bytes 32800 | tf_op jit(solution)/shard_map/all_to_all | solution.py:38
  152.5 4.6 %convolution_convert_fusion.4 = bf16[8,2,2048]{2,1,0:T(2,128)(2,1)S(1)} fusion(bf16[8,256,2048]{2,1,0:T(8,128)(2,1)} %bitcast.119, bf16[2,256]{1,0:T(2,128)(2,1)S(1)} %get-tuple-element.22), kind=kOutput, calls=%fused_computation.5 | convolution fusion | flops 16809984 | bytes 8455168 | tf_op jit(solution)/shard_map/zsk,zkn->zsn/dot_general | solution.py:185
  157.3 14.4 %all_to_all.55 = bf16[64,6,128]{2,1,0:T(8,128)(2,1)S(1)} all-to-all(bf16[64,6,128]{2,1,0:T(8,128)(2,1)S(1)} %pad_maximum_fusion.2), channel_id=1, replica_groups=mesh['x'=4,'ya'=2,'yb'=2,'yc'=2,'core'=2,'z'=8] {'x','ya','yb','yc','core'}, dimensions={0} | all-to-all | bytes 196608 | tf_op jit(solution)/shard_map/all_to_all | solution.py:38
  172.7 4.6 %convolution_convert_fusion.3 = bf16[8,2,2048]{2,1,0:T(2,128)(2,1)S(1)} fusion(bf16[8,256,2048]{2,1,0:T(8,128)(2,1)} %bitcast.120, bf16[2,256]{1,0:T(2,128)(2,1)S(1)} %get-tuple-element.30), kind=kOutput, calls=%fused_computation.4 | convolution fusion | flops 16809984 | bytes 8455168 | tf_op jit(solution)/shard_map/zsk,zkn->zsn/dot_general | solution.py:185
  177.9 15.0 %all_to_all.56 = bf16[64,6,128]{2,1,0:T(8,128)(2,1)S(1)} all-to-all(bf16[64,6,128]{2,1,0:T(8,128)(2,1)S(1)} %pad_maximum_fusion.3), channel_id=1, replica_groups=mesh['x'=4,'ya'=2,'yb'=2,'yc'=2,'core'=2,'z'=8] {'x','ya','yb','yc','core'}, dimensions={0} | all-to-all | bytes 196608 | tf_op jit(solution)/shard_map/all_to_all | solution.py:38
  194.0 4.6 %convolution_convert_fusion.2 = bf16[8,2,2048]{2,1,0:T(2,128)(2,1)S(1)} fusion(bf16[8,256,2048]{2,1,0:T(8,128)(2,1)} %bitcast.121, bf16[2,256]{1,0:T(2,128)(2,1)S(1)} %get-tuple-element.28), kind=kOutput, calls=%fused_computation.3 | convolution fusion | flops 16809984 | bytes 8455168 | tf_op jit(solution)/shard_map/zsk,zkn->zsn/dot_general | solution.py:185
  199.2 15.0 %all_to_all.57 = bf16[64,6,128]{2,1,0:T(8,128)(2,1)S(1)} all-to-all(bf16[64,6,128]{2,1,0:T(8,128)(2,1)S(1)} %pad_maximum_fusion.4), channel_id=1, replica_groups=mesh['x'=4,'ya'=2,'yb'=2,'yc'=2,'core'=2,'z'=8] {'x','ya','yb','yc','core'}, dimensions={0} | all-to-all | bytes 196608 | tf_op jit(solution)/shard_map/all_to_all | solution.py:38
  216.2 4.6 %all-to-all-start.9 = ((bf16[64,5,128]{2,1,0:T(8,128)(2,1)}), bf16[64,5,128]{2,1,0:T(8,128)(2,1)S(1)}, u32[]{:S(2)}, u32[]{:S(2)}) async-start(bf16[64,5,128]{2,1,0:T(8,128)(2,1)} %broadcast_in_dim.84), calls=%async_computation.9 | async-start | bytes 262144 | tf_op jit(solution)/shard_map/all_to_all | solution.py:38
  220.8 13.6 %all-to-all-done.9 = bf16[64,5,128]{2,1,0:T(8,128)(2,1)S(1)} async-done(((bf16[64,5,128]{2,1,0:T(8,128)(2,1)}), bf16[64,5,128]{2,1,0:T(8,128)(2,1)S(1)}, u32[]{:S(2)}, u32[]{:S(2)}) %all-to-all-start.9) | async-done | bytes 81952 | tf_op jit(solution)/shard_map/all_to_all | solution.py:38
  235.4 6.3 %all-to-all-start.10 = ((bf16[8,34,128]{2,1,0:T(8,128)(2,1)}), bf16[8,34,128]{2,1,0:T(8,128)(2,1)S(1)}, u32[]{:S(2)}, u32[]{:S(2)}) async-start(bf16[8,34,128]{2,1,0:T(8,128)(2,1)} %broadcast_in_dim.85), calls=%async_computation.10 | async-start | bytes 163840 | tf_op jit(solution)/shard_map/all_to_all | solution.py:38
  242.3 4.6 %all-to-all-done.10 = bf16[8,34,128]{2,1,0:T(8,128)(2,1)S(1)} async-done(((bf16[8,34,128]{2,1,0:T(8,128)(2,1)}), bf16[8,34,128]{2,1,0:T(8,128)(2,1)S(1)}, u32[]{:S(2)}, u32[]{:S(2)}) %all-to-all-start.10) | async-done | bytes 69664 | tf_op jit(solution)/shard_map/all_to_all | solution.py:38
  (165 shorter events, 19.6 us)
Async XLA Ops:
  7.2 30.0 %copy-start = (bf16[128,2048]{1,0:T(8,128)(2,1)S(1)}, bf16[128,2048]{1,0:T(8,128)(2,1)}, u32[]{:S(2)}) copy-start(bf16[128,2048]{1,0:T(8,128)(2,1)} %param.11) | copy-start | bytes 1572868
  7.2 41.4 %copy-start.1 = (bf16[256,2048]{1,0:T(8,128)(2,1)S(1)}, bf16[256,2048]{1,0:T(8,128)(2,1)}, u32[]{:S(2)}) copy-start(bf16[256,2048]{1,0:T(8,128)(2,1)} %param.19) | copy-start | bytes 3145732
  7.2 145.3 %all-gather.3.cloned.1.call-start = ((), (), s32[]{:S(2)}) async-start(), calls=%async_computation.11 | async-start | bytes 9437184 | tf_op jit(solution)/shard_map/all_gather | solution.py:76
  9.5 20.2 %all-to-all-start = ((bf16[32,32,128]{2,1,0:T(8,128)(2,1)}), bf16[32,32,128]{2,1,0:T(8,128)(2,1)S(1)}, u32[]{:S(2)}, u32[]{:S(2)}) async-start(bf16[32,32,128]{2,1,0:T(8,128)(2,1)} %broadcast_in_dim.61), calls=%async_computation | async-start | bytes 524288 | tf_op jit(solution)/shard_map/all_to_all | solution.py:38
  29.7 6.8 %collective-permute-start = (bf16[32,32,128]{2,1,0:T(8,128)(2,1)S(1)}, bf16[32,32,128]{2,1,0:T(8,128)(2,1)S(1)}, u32[]{:S(2)}, u32[]{:S(2)}) collective-permute-start(bf16[32,32,128]{2,1,0:T(8,128)(2,1)S(1)} %all-to-all-done), channel_id=1, source_target_pairs={{0,8},{8,0},{1,9},{9,1},{2,10},{10,2},{3,11},{11,3},{4,12},{12,4},... | collective-permute-start | bytes 786440 | tf_op jit(solution)/shard_map/ppermute | solution.py:46
  37.2 41.2 %copy-start.3 = (f32[1,32,128]{2,1,0:T(8,128)S(1)}, f32[1,32,128]{2,1,0:T(8,128)}, u32[]{:S(2)}) copy-start(f32[1,32,128]{2,1,0:T(8,128)} %param.18) | copy-start | bytes 49156
  37.2 41.2 %copy-start.4 = (f32[1,32,128]{2,1,0:T(8,128)S(1)}, f32[1,32,128]{2,1,0:T(8,128)}, u32[]{:S(2)}) copy-start(f32[1,32,128]{2,1,0:T(8,128)} %param.17) | copy-start | bytes 49156
  38.6 27.4 %all-to-all-start.1 = ((bf16[8,164,128]{2,1,0:T(8,128)(2,1)}), bf16[8,164,128]{2,1,0:T(8,128)(2,1)S(1)}, u32[]{:S(2)}, u32[]{:S(2)}) async-start(bf16[8,164,128]{2,1,0:T(8,128)(2,1)} %broadcast_in_dim.65), calls=%async_computation.1 | async-start | bytes 688128 | tf_op jit(solution)/shard_map/all_to_all | solution.py:38
  66.0 0.6 copy-start.2
  68.7 4.5 %collective-permute-start.1 = (bf16[32,40,128]{2,1,0:T(8,128)(2,1)S(1)}, bf16[32,40,128]{2,1,0:T(8,128)(2,1)S(1)}, u32[]{:S(2)}, u32[]{:S(2)}) collective-permute-start(bf16[32,40,128]{2,1,0:T(8,128)(2,1)S(1)} %pad_maximum_fusion), channel_id=1, source_target_pairs={{0,8},{8,0},{1,9},{9,1},{2,10},{10,2},{3,11},{11,3},{4,12},{12,4},... | collective-permute-start | bytes 983048 | tf_op jit(solution)/shard_map/ppermute | solution.py:46
  74.2 14.6 %all-to-all-start.2 = ((bf16[32,40,128]{2,1,0:T(8,128)(2,1)}), bf16[32,40,128]{2,1,0:T(8,128)(2,1)S(1)}, u32[]{:S(2)}, u32[]{:S(2)}) async-start(bf16[32,40,128]{2,1,0:T(8,128)(2,1)} %pad_maximum_fusion.1), calls=%async_computation.2 | async-start | bytes 655360 | tf_op jit(solution)/shard_map/all_to_all | solution.py:38
  90.7 18.4 %all-to-all-start.3 = ((f32[64,1,128]{2,1,0:T(1,128)}), f32[64,1,128]{2,1,0:T(1,128)S(1)}, u32[]{:S(2)}, u32[]{:S(2)}) async-start(f32[64,1,128]{2,1,0:T(1,128)} %broadcast_in_dim_broadcast_in_dim_broadcast_in_dim.3), calls=%async_computation.3 | async-start | bytes 65536 | tf_op jit(solution)/shard_map/all_to_all | solution.py:38
  99.8 9.4 %collective-permute-start.2 = (bf16[136,128]{1,0:T(8,128)(2,1)S(1)}, bf16[136,128]{1,0:T(8,128)(2,1)S(1)}, u32[]{:S(2)}, u32[]{:S(2)}) collective-permute-start(bf16[136,128]{1,0:T(8,128)(2,1)S(1)} %concatenate.74), channel_id=1, source_target_pairs={{0,0},{1,64},{2,128},{3,192},{4,256},{5,320},{6,384},{7,448},{8,1}... | collective-permute-start | bytes 104456 | tf_op jit(solution)/shard_map/ppermute | solution.py:133
  110.0 22.1 %all-to-all-start.4 = ((bf16[8,130,128]{2,1,0:T(8,128)(2,1)}), bf16[8,130,128]{2,1,0:T(8,128)(2,1)S(1)}, u32[]{:S(2)}, u32[]{:S(2)}) async-start(bf16[8,130,128]{2,1,0:T(8,128)(2,1)} %broadcast_in_dim.66), calls=%async_computation.4 | async-start | bytes 557056 | tf_op jit(solution)/shard_map/all_to_all | solution.py:38
  133.2 18.3 %all-to-all-start.5 = ((f32[64,1,128]{2,1,0:T(1,128)}), f32[64,1,128]{2,1,0:T(1,128)S(1)}, u32[]{:S(2)}, u32[]{:S(2)}) async-start(f32[64,1,128]{2,1,0:T(1,128)} %broadcast_in_dim.69), calls=%async_computation.5 | async-start | bytes 65536 | tf_op jit(solution)/shard_map/all_to_all | solution.py:38
  177.3 64.4 %copy-start.5 = (f32[1,32,128]{2,1,0:T(8,128)S(1)}, f32[1,32,128]{2,1,0:T(8,128)}, u32[]{:S(2)}) copy-start(f32[1,32,128]{2,1,0:T(8,128)} %param.16) | copy-start | bytes 49156
  216.2 18.2 %all-to-all-start.9 = ((bf16[64,5,128]{2,1,0:T(8,128)(2,1)}), bf16[64,5,128]{2,1,0:T(8,128)(2,1)S(1)}, u32[]{:S(2)}, u32[]{:S(2)}) async-start(bf16[64,5,128]{2,1,0:T(8,128)(2,1)} %broadcast_in_dim.84), calls=%async_computation.9 | async-start | bytes 262144 | tf_op jit(solution)/shard_map/all_to_all | solution.py:38
  235.4 11.6 %all-to-all-start.10 = ((bf16[8,34,128]{2,1,0:T(8,128)(2,1)}), bf16[8,34,128]{2,1,0:T(8,128)(2,1)S(1)}, u32[]{:S(2)}, u32[]{:S(2)}) async-start(bf16[8,34,128]{2,1,0:T(8,128)(2,1)} %broadcast_in_dim.85), calls=%async_computation.10 | async-start | bytes 163840 | tf_op jit(solution)/shard_map/all_to_all | solution.py:38
Sparse Core Ops, SparseCore 0:
  10.1 115.9 all-gather.2

commit v9 on v8

--- a/solution.py
+++ b/solution.py
@@ -14,6 +14,7 @@
 BATCH = 16
 BLOCK = 2048
 TILE = 256
+EARLY = 512
 OWN = 32
 
 adapter_alpha = 2.0
@@ -73,7 +74,7 @@
     major = lax.axis_index(("x", "ya"))
     minor = lax.axis_index(MINOR)
 
-    panel = lax.all_gather(base_weight, "z", axis=0, tiled=False)
+    left = lax.all_gather(base_weight[:, :EARLY], "z", axis=0, tiled=False)
 
     positions = jnp.arange(SEQLEN, dtype=jnp.int32)
     lower = prompt_len[:, None]
@@ -102,6 +103,8 @@
         axis=0,
     )
     got = share(sent, "z", 8)
+    got, later = lax.optimization_barrier((got, base_weight))
+    right = lax.all_gather(later[:, EARLY:], "z", axis=0, tiled=False)
     both = jnp.sum(got[:, :SEQLEN].astype(f32), axis=0).astype(bf16)
     home = pick(got[:, SEQLEN:], major, 0)
     first = home[:32].reshape(BATCH, TILE)
@@ -182,13 +185,12 @@
         own = (resid * tile_gain).astype(bf16)
         thin = jnp.dot(own, down, preferred_element_type=f32).astype(bf16).reshape(1, 128)
         extra = jnp.concatenate([thin, packed(jnp.sum(resid * resid, axis=1))], axis=0)
-        sums = jnp.einsum(
-            "zsk,zkn->zsn",
-            jnp.broadcast_to(own[None], (8, 2, TILE)),
-            panel,
-            preferred_element_type=f32,
-        )
-        sums = lax.optimization_barrier(sums.astype(bf16))
+        value = jnp.broadcast_to(own[None], (8, 2, TILE))
+        sums = [
+            jnp.einsum("zsk,zkn->zsn", value, panel, preferred_element_type=f32).astype(bf16)
+            for panel in (left, right)
+        ]
+        sums = lax.optimization_barrier(jnp.concatenate(sums, axis=2))
         sums = sums.reshape(8, 2, 8, TILE).transpose(0, 2, 1, 3).reshape(64, 4, 128)
         sent = jnp.concatenate([sums, jnp.broadcast_to(extra[None], (64, 2, 128))], axis=1)
         got = jnp.sum(swap(sent, DP).astype(f32), axis=0)

time: 256 us -> 264 us (1.031)
  blocking collectives: 44.5 us -> 70.5 us
  waiting for transfers between devices: 82.9 us -> 65.8 us
  starting transfers between devices: 72.6 us -> 69.3 us
    all_to_all x3 -> x4, blocking collectives: 44.5 us -> 70.5 us  [swap(): return lax.all_to_all(chunks, axes, 0, 0, tiled=False)]
    all_to_all x8 -> x7, waiting for transfers between devices: 74.5 us -> 58 us  [swap(): return lax.all_to_all(chunks, axes, 0, 0, tiled=False)]
    all_to_all x8 -> x7, starting transfers between devices: 61 us -> 57.9 us  [swap(): return lax.all_to_all(chunks, axes, 0, 0, tiled=False)]
    slice x0 -> x2, local copies, waits for them, and re-layouts: none -> 2.76 us  [the longest x1 1.76 us: body(): left = lax.all_gather(base_weight[:, :EARLY], 'z', axis=0, tiled=False)]
    dot_general x3 -> x6, matrix products: 13.7 us -> 14 us  [body(): jnp.einsum('zsk,zkn->zsn', value, panel, preferred_element_type=f32)]
  transfers between devices with their start and end apart: 12 -> 12, of which waited for: 9 -> 8; matrix products, arithmetic and copies ran while one was open for 7% -> 7% of each run, Pallas kernels for 0% -> 0%
where the time goes in v9:
time: 264 us; the launch traced here: 262 us
  blocking collectives  70.5 us (27%)
  starting transfers between devices  69.3 us (26%)
  waiting for transfers between devices  65.8 us (25%)
  matrix products  17.7 us (7%)
  between operations  16.7 us (6%)
  local copies, waits for them, and re-layouts  13.1 us (5%)
  other arithmetic  9.29 us (4%)
    all_to_all x4, blocking collectives, swap(): return lax.all_to_all(chunks, axes, 0, 0, tiled=False)  70.5 us
    all_to_all x7, waiting for transfers between devices, swap(): return lax.all_to_all(chunks, axes, 0, 0, tiled=False)  58 us
    all_to_all x7, starting transfers between devices, swap(): return lax.all_to_all(chunks, axes, 0, 0, tiled=False)  57.9 us
    dot_general x6, matrix products, body(): jnp.einsum('zsk,zkn->zsn', value, panel, preferred_element_type=f32)  14 us
    ppermute x2, starting transfers between devices, core_swap(): return lax.ppermute(value, 'core', [(0, 1), (1, 0)])  8.61 us
    ppermute x1, waiting for transfers between devices, body(): lax.ppermute(jnp.concatenate([own_grads.astype(bf16), old.astype(bf16), *...  6.63 us
  transfers between devices with their start and end apart: 12, of which 8 were waited for; matrix products, arithmetic and copies ran while one was open for 7% of the time, Pallas kernels for 0%

profile of v9, /device:TPU:1, one launch (start us, length us, event | category | flops | bytes accessed | tf_op | source)
XLA Modules:
  0.0 262.3 jit_solution(2093644427949672921)
XLA Ops:
  7.2 1.8 slice.198
  9.0 0.8 bitcast_convert_fusion
  10.6 10.5 %all-to-all-start = ((bf16[32,32,128]{2,1,0:T(8,128)(2,1)}), bf16[32,32,128]{2,1,0:T(8,128)(2,1)S(1)}, u32[]{:S(2)}, u32[]{:S(2)}) async-start(bf16[32,32,128]{2,1,0:T(8,128)(2,1)} %broadcast_in_dim.61), calls=%async_computation | async-start | bytes 524288 | tf_op jit(solution)/shard_map/all_to_all | solution.py:39
  25.0 5.7 %all-to-all-done = bf16[32,32,128]{2,1,0:T(8,128)(2,1)S(1)} async-done(((bf16[32,32,128]{2,1,0:T(8,128)(2,1)}), bf16[32,32,128]{2,1,0:T(8,128)(2,1)S(1)}, u32[]{:S(2)}, u32[]{:S(2)}) %all-to-all-start) | async-done | bytes 262176 | tf_op jit(solution)/shard_map/all_to_all | solution.py:39
  30.8 5.6 %collective-permute-start = (bf16[32,32,128]{2,1,0:T(8,128)(2,1)S(1)}, bf16[32,32,128]{2,1,0:T(8,128)(2,1)S(1)}, u32[]{:S(2)}, u32[]{:S(2)}) collective-permute-start(bf16[32,32,128]{2,1,0:T(8,128)(2,1)S(1)} %all-to-all-done), channel_id=1, source_target_pairs={{0,8},{8,0},{1,9},{9,1},{2,10},{10,2},{3,11},{11,3},{4,12},{12,4},... | collective-permute-start | bytes 786440 | tf_op jit(solution)/shard_map/ppermute | solution.py:47
  36.4 1.2 multiply_convert_fusion
  38.9 26.0 %all_to_all.55 = bf16[8,164,128]{2,1,0:T(8,128)(2,1)S(1)} all-to-all(bf16[8,164,128]{2,1,0:T(8,128)(2,1)S(1)} %broadcast_in_dim.65), channel_id=1, replica_groups=mesh['x'=4,'ya'=2,'yb'=2,'yc'=2,'core'=2,'z'=8] {'z'}, dimensions={0} | all-to-all | bytes 671744 | tf_op jit(solution)/shard_map/all_to_all | solution.py:39
  64.9 1.0 slice.199
  68.6 3.0 %collective-permute-start.1 = (bf16[32,40,128]{2,1,0:T(8,128)(2,1)S(1)}, bf16[32,40,128]{2,1,0:T(8,128)(2,1)S(1)}, u32[]{:S(2)}, u32[]{:S(2)}) collective-permute-start(bf16[32,40,128]{2,1,0:T(8,128)(2,1)S(1)} %pad_maximum_fusion), channel_id=1, source_target_pairs={{0,8},{8,0},{1,9},{9,1},{2,10},{10,2},{3,11},{11,3},{4,12},{12,4},... | collective-permute-start | bytes 983048 | tf_op jit(solution)/shard_map/ppermute | solution.py:47
  71.7 1.1 collective-permute-done.1
  73.1 0.8 pad_maximum_fusion.1
  73.9 5.2 %all-to-all-start.2 = ((bf16[32,40,128]{2,1,0:T(8,128)(2,1)}), bf16[32,40,128]{2,1,0:T(8,128)(2,1)S(1)}, u32[]{:S(2)}, u32[]{:S(2)}) async-start(bf16[32,40,128]{2,1,0:T(8,128)(2,1)} %pad_maximum_fusion.1), calls=%async_computation.2 | async-start | bytes 655360 | tf_op jit(solution)/shard_map/all_to_all | solution.py:39
  79.2 10.4 %all-to-all-done.2 = bf16[32,40,128]{2,1,0:T(8,128)(2,1)S(1)} async-done(((bf16[32,40,128]{2,1,0:T(8,128)(2,1)}), bf16[32,40,128]{2,1,0:T(8,128)(2,1)S(1)}, u32[]{:S(2)}, u32[]{:S(2)}) %all-to-all-start.2) | async-done | bytes 327712 | tf_op jit(solution)/shard_map/all_to_all | solution.py:39
  90.3 1.3 broadcast_in_dim_broadcast_in_dim_broadcast_in_dim.3
  91.6 8.9 %all-to-all-start.3 = ((f32[64,1,128]{2,1,0:T(1,128)}), f32[64,1,128]{2,1,0:T(1,128)S(1)}, u32[]{:S(2)}, u32[]{:S(2)}) async-start(f32[64,1,128]{2,1,0:T(1,128)} %broadcast_in_dim_broadcast_in_dim_broadcast_in_dim.3), calls=%async_computation.3 | async-start | bytes 65536 | tf_op jit(solution)/shard_map/all_to_all | solution.py:39
  100.6 2.7 %collective-permute-start.2 = (bf16[136,128]{1,0:T(8,128)(2,1)S(1)}, bf16[136,128]{1,0:T(8,128)(2,1)S(1)}, u32[]{:S(2)}, u32[]{:S(2)}) collective-permute-start(bf16[136,128]{1,0:T(8,128)(2,1)S(1)} %concatenate.83), channel_id=1, source_target_pairs={{0,0},{1,64},{2,128},{3,192},{4,256},{5,320},{6,384},{7,448},{8,1}... | collective-permute-start | bytes 104456 | tf_op jit(solution)/shard_map/ppermute | solution.py:136
  103.3 6.6 %collective-permute-done.2 = bf16[136,128]{1,0:T(8,128)(2,1)S(1)} collective-permute-done((bf16[136,128]{1,0:T(8,128)(2,1)S(1)}, bf16[136,128]{1,0:T(8,128)(2,1)S(1)}, u32[]{:S(2)}, u32[]{:S(2)}) %collective-permute-start.2) | collective-permute-done | bytes 34848 | tf_op jit(solution)/shard_map/ppermute | solution.py:136
  110.8 7.3 %all-to-all-start.4 = ((bf16[8,130,128]{2,1,0:T(8,128)(2,1)}), bf16[8,130,128]{2,1,0:T(8,128)(2,1)S(1)}, u32[]{:S(2)}, u32[]{:S(2)}) async-start(bf16[8,130,128]{2,1,0:T(8,128)(2,1)} %broadcast_in_dim.66), calls=%async_computation.4 | async-start | bytes 557056 | tf_op jit(solution)/shard_map/all_to_all | solution.py:39
  118.8 14.4 %all-to-all-done.4 = bf16[8,130,128]{2,1,0:T(8,128)(2,1)S(1)} async-done(((bf16[8,130,128]{2,1,0:T(8,128)(2,1)}), bf16[8,130,128]{2,1,0:T(8,128)(2,1)S(1)}, u32[]{:S(2)}, u32[]{:S(2)}) %all-to-all-start.4) | async-done | bytes 266272 | tf_op jit(solution)/shard_map/all_to_all | solution.py:39
  134.3 12.6 %all-to-all-start.5 = ((f32[64,1,128]{2,1,0:T(1,128)}), f32[64,1,128]{2,1,0:T(1,128)S(1)}, u32[]{:S(2)}, u32[]{:S(2)}) async-start(f32[64,1,128]{2,1,0:T(1,128)} %broadcast_in_dim.69), calls=%async_computation.5 | async-start | bytes 65536 | tf_op jit(solution)/shard_map/all_to_all | solution.py:39
  147.0 9.2 %all-to-all-done.5 = f32[64,1,128]{2,1,0:T(1,128)S(1)} async-done(((f32[64,1,128]{2,1,0:T(1,128)}), f32[64,1,128]{2,1,0:T(1,128)S(1)}, u32[]{:S(2)}, u32[]{:S(2)}) %all-to-all-start.5) | async-done | bytes 32800 | tf_op jit(solution)/shard_map/all_to_all | solution.py:39
  157.3 2.0 convolution_convert_fusion.7
  159.2 3.9 %convolution_convert_fusion.4 = bf16[8,2,1536]{2,1,0:T(2,128)(2,1)S(1)} fusion(bf16[8,256,1536]{2,1,0:T(8,128)(2,1)} %bitcast.123, bf16[2,256]{1,0:T(2,128)(2,1)S(1)} %get-tuple-element.26), kind=kOutput, calls=%fused_computation.5 | convolution fusion | flops 12607488 | bytes 6341632 | tf_op jit(solution)/shard_map/zsk,zkn->zsn/dot_general | solution.py:190
  163.3 14.4 %all_to_all.56 = bf16[64,6,128]{2,1,0:T(8,128)(2,1)S(1)} all-to-all(bf16[64,6,128]{2,1,0:T(8,128)(2,1)S(1)} %pad_maximum_fusion.2), channel_id=1, replica_groups=mesh['x'=4,'ya'=2,'yb'=2,'yc'=2,'core'=2,'z'=8] {'x','ya','yb','yc','core'}, dimensions={0} | all-to-all | bytes 196608 | tf_op jit(solution)/shard_map/all_to_all | solution.py:39
  179.0 3.7 %convolution_convert_fusion.3 = bf16[8,2,1536]{2,1,0:T(2,128)(2,1)S(1)} fusion(bf16[8,256,1536]{2,1,0:T(8,128)(2,1)} %bitcast.124, bf16[2,256]{1,0:T(2,128)(2,1)S(1)} %get-tuple-element.34), kind=kOutput, calls=%fused_computation.4 | convolution fusion | flops 12607488 | bytes 6341632 | tf_op jit(solution)/shard_map/zsk,zkn->zsn/dot_general | solution.py:190
  183.5 15.0 %all_to_all.57 = bf16[64,6,128]{2,1,0:T(8,128)(2,1)S(1)} all-to-all(bf16[64,6,128]{2,1,0:T(8,128)(2,1)S(1)} %pad_maximum_fusion.3), channel_id=1, replica_groups=mesh['x'=4,'ya'=2,'yb'=2,'yc'=2,'core'=2,'z'=8] {'x','ya','yb','yc','core'}, dimensions={0} | all-to-all | bytes 196608 | tf_op jit(solution)/shard_map/all_to_all | solution.py:39
  199.9 3.7 %convolution_convert_fusion.2 = bf16[8,2,1536]{2,1,0:T(2,128)(2,1)S(1)} fusion(bf16[8,256,1536]{2,1,0:T(8,128)(2,1)} %bitcast.125, bf16[2,256]{1,0:T(2,128)(2,1)S(1)} %get-tuple-element.32), kind=kOutput, calls=%fused_computation.3 | convolution fusion | flops 12607488 | bytes 6341632 | tf_op jit(solution)/shard_map/zsk,zkn->zsn/dot_general | solution.py:190
  204.4 15.0 %all_to_all.58 = bf16[64,6,128]{2,1,0:T(8,128)(2,1)S(1)} all-to-all(bf16[64,6,128]{2,1,0:T(8,128)(2,1)S(1)} %pad_maximum_fusion.4), channel_id=1, replica_groups=mesh['x'=4,'ya'=2,'yb'=2,'yc'=2,'core'=2,'z'=8] {'x','ya','yb','yc','core'}, dimensions={0} | all-to-all | bytes 196608 | tf_op jit(solution)/shard_map/all_to_all | solution.py:39
  221.4 6.9 %all-to-all-start.9 = ((bf16[64,5,128]{2,1,0:T(8,128)(2,1)}), bf16[64,5,128]{2,1,0:T(8,128)(2,1)S(1)}, u32[]{:S(2)}, u32[]{:S(2)}) async-start(bf16[64,5,128]{2,1,0:T(8,128)(2,1)} %broadcast_in_dim.84), calls=%async_computation.9 | async-start | bytes 262144 | tf_op jit(solution)/shard_map/all_to_all | solution.py:39
  228.3 13.6 %all-to-all-done.9 = bf16[64,5,128]{2,1,0:T(8,128)(2,1)S(1)} async-done(((bf16[64,5,128]{2,1,0:T(8,128)(2,1)}), bf16[64,5,128]{2,1,0:T(8,128)(2,1)S(1)}, u32[]{:S(2)}, u32[]{:S(2)}) %all-to-all-start.9) | async-done | bytes 81952 | tf_op jit(solution)/shard_map/all_to_all | solution.py:39
  242.9 6.3 %all-to-all-start.10 = ((bf16[8,34,128]{2,1,0:T(8,128)(2,1)}), bf16[8,34,128]{2,1,0:T(8,128)(2,1)S(1)}, u32[]{:S(2)}, u32[]{:S(2)}) async-start(bf16[8,34,128]{2,1,0:T(8,128)(2,1)} %broadcast_in_dim.85), calls=%async_computation.10 | async-start | bytes 163840 | tf_op jit(solution)/shard_map/all_to_all | solution.py:39
  249.8 4.6 %all-to-all-done.10 = bf16[8,34,128]{2,1,0:T(8,128)(2,1)S(1)} async-done(((bf16[8,34,128]{2,1,0:T(8,128)(2,1)}), bf16[8,34,128]{2,1,0:T(8,128)(2,1)S(1)}, u32[]{:S(2)}, u32[]{:S(2)}) %all-to-all-start.10) | async-done | bytes 69664 | tf_op jit(solution)/shard_map/all_to_all | solution.py:39
  (177 shorter events, 20.2 us)
Async XLA Ops:
  7.2 31.1 %copy-start = (bf16[128,2048]{1,0:T(8,128)(2,1)S(1)}, bf16[128,2048]{1,0:T(8,128)(2,1)}, u32[]{:S(2)}) copy-start(bf16[128,2048]{1,0:T(8,128)(2,1)} %param.11) | copy-start | bytes 1572868
  7.2 57.8 %copy-start.2 = (bf16[256,2048]{1,0:T(8,128)(2,1)S(1)}, bf16[256,2048]{1,0:T(8,128)(2,1)}, u32[]{:S(2)}) copy-start(bf16[256,2048]{1,0:T(8,128)(2,1)} %param.19) | copy-start | bytes 3145732
  7.2 150.1 %all-gather.5.cloned.1.call-start = ((), (), s32[]{:S(2)}) async-start(), calls=%async_computation.11 | async-start | bytes 2359296 | tf_op jit(solution)/shard_map/all_gather | solution.py:77
  10.6 20.2 %all-to-all-start = ((bf16[32,32,128]{2,1,0:T(8,128)(2,1)}), bf16[32,32,128]{2,1,0:T(8,128)(2,1)S(1)}, u32[]{:S(2)}, u32[]{:S(2)}) async-start(bf16[32,32,128]{2,1,0:T(8,128)(2,1)} %broadcast_in_dim.61), calls=%async_computation | async-start | bytes 524288 | tf_op jit(solution)/shard_map/all_to_all | solution.py:39
  21.1 138.2 %all-gather.7.cloned.1.call-start = ((), (), s32[]{:S(2)}) async-start(), calls=%async_computation.12 | async-start | bytes 7077888 | tf_op jit(solution)/shard_map/all_gather | solution.py:107
  30.8 6.8 %collective-permute-start = (bf16[32,32,128]{2,1,0:T(8,128)(2,1)S(1)}, bf16[32,32,128]{2,1,0:T(8,128)(2,1)S(1)}, u32[]{:S(2)}, u32[]{:S(2)}) collective-permute-start(bf16[32,32,128]{2,1,0:T(8,128)(2,1)S(1)} %all-to-all-done), channel_id=1, source_target_pairs={{0,8},{8,0},{1,9},{9,1},{2,10},{10,2},{3,11},{11,3},{4,12},{12,4},... | collective-permute-start | bytes 786440 | tf_op jit(solution)/shard_map/ppermute | solution.py:47
  66.5 12.7 %copy-start.4 = (f32[1,32,128]{2,1,0:T(8,128)S(1)}, f32[1,32,128]{2,1,0:T(8,128)}, u32[]{:S(2)}) copy-start(f32[1,32,128]{2,1,0:T(8,128)} %param.18) | copy-start | bytes 49156
  66.5 12.7 %copy-start.5 = (f32[1,32,128]{2,1,0:T(8,128)S(1)}, f32[1,32,128]{2,1,0:T(8,128)}, u32[]{:S(2)}) copy-start(f32[1,32,128]{2,1,0:T(8,128)} %param.17) | copy-start | bytes 49156
  66.5 1.8 copy-start.3
  68.6 4.2 %collective-permute-start.1 = (bf16[32,40,128]{2,1,0:T(8,128)(2,1)S(1)}, bf16[32,40,128]{2,1,0:T(8,128)(2,1)S(1)}, u32[]{:S(2)}, u32[]{:S(2)}) collective-permute-start(bf16[32,40,128]{2,1,0:T(8,128)(2,1)S(1)} %pad_maximum_fusion), channel_id=1, source_target_pairs={{0,8},{8,0},{1,9},{9,1},{2,10},{10,2},{3,11},{11,3},{4,12},{12,4},... | collective-permute-start | bytes 983048 | tf_op jit(solution)/shard_map/ppermute | solution.py:47
  73.9 15.7 %all-to-all-start.2 = ((bf16[32,40,128]{2,1,0:T(8,128)(2,1)}), bf16[32,40,128]{2,1,0:T(8,128)(2,1)S(1)}, u32[]{:S(2)}, u32[]{:S(2)}) async-start(bf16[32,40,128]{2,1,0:T(8,128)(2,1)} %pad_maximum_fusion.1), calls=%async_computation.2 | async-start | bytes 655360 | tf_op jit(solution)/shard_map/all_to_all | solution.py:39
  91.6 18.4 %all-to-all-start.3 = ((f32[64,1,128]{2,1,0:T(1,128)}), f32[64,1,128]{2,1,0:T(1,128)S(1)}, u32[]{:S(2)}, u32[]{:S(2)}) async-start(f32[64,1,128]{2,1,0:T(1,128)} %broadcast_in_dim_broadcast_in_dim_broadcast_in_dim.3), calls=%async_computation.3 | async-start | bytes 65536 | tf_op jit(solution)/shard_map/all_to_all | solution.py:39
  100.6 9.4 %collective-permute-start.2 = (bf16[136,128]{1,0:T(8,128)(2,1)S(1)}, bf16[136,128]{1,0:T(8,128)(2,1)S(1)}, u32[]{:S(2)}, u32[]{:S(2)}) collective-permute-start(bf16[136,128]{1,0:T(8,128)(2,1)S(1)} %concatenate.83), channel_id=1, source_target_pairs={{0,0},{1,64},{2,128},{3,192},{4,256},{5,320},{6,384},{7,448},{8,1}... | collective-permute-start | bytes 104456 | tf_op jit(solution)/shard_map/ppermute | solution.py:136
  110.8 22.4 %all-to-all-start.4 = ((bf16[8,130,128]{2,1,0:T(8,128)(2,1)}), bf16[8,130,128]{2,1,0:T(8,128)(2,1)S(1)}, u32[]{:S(2)}, u32[]{:S(2)}) async-start(bf16[8,130,128]{2,1,0:T(8,128)(2,1)} %broadcast_in_dim.66), calls=%async_computation.4 | async-start | bytes 557056 | tf_op jit(solution)/shard_map/all_to_all | solution.py:39
  134.3 21.8 %all-to-all-start.5 = ((f32[64,1,128]{2,1,0:T(1,128)}), f32[64,1,128]{2,1,0:T(1,128)S(1)}, u32[]{:S(2)}, u32[]{:S(2)}) async-start(f32[64,1,128]{2,1,0:T(1,128)} %broadcast_in_dim.69), calls=%async_computation.5 | async-start | bytes 65536 | tf_op jit(solution)/shard_map/all_to_all | solution.py:39
  159.2 19.4 %copy-start.1 = (bf16[2048,512]{1,0:T(8,128)(2,1)S(1)}, bf16[2048,512]{1,0:T(8,128)(2,1)}, u32[]{:S(2)}) copy-start(bf16[2048,512]{1,0:T(8,128)(2,1)} %all-gather.5.cloned.1.call-done) | copy-start | bytes 6291460
  199.9 49.3 %copy-start.6 = (f32[1,32,128]{2,1,0:T(8,128)S(1)}, f32[1,32,128]{2,1,0:T(8,128)}, u32[]{:S(2)}) copy-start(f32[1,32,128]{2,1,0:T(8,128)} %param.16) | copy-start | bytes 49156
  221.4 20.5 %all-to-all-start.9 = ((bf16[64,5,128]{2,1,0:T(8,128)(2,1)}), bf16[64,5,128]{2,1,0:T(8,128)(2,1)S(1)}, u32[]{:S(2)}, u32[]{:S(2)}) async-start(bf16[64,5,128]{2,1,0:T(8,128)(2,1)} %broadcast_in_dim.84), calls=%async_computation.9 | async-start | bytes 262144 | tf_op jit(solution)/shard_map/all_to_all | solution.py:39
  242.9 11.6 %all-to-all-start.10 = ((bf16[8,34,128]{2,1,0:T(8,128)(2,1)}), bf16[8,34,128]{2,1,0:T(8,128)(2,1)S(1)}, u32[]{:S(2)}, u32[]{:S(2)}) async-start(bf16[8,34,128]{2,1,0:T(8,128)(2,1)} %broadcast_in_dim.85), calls=%async_computation.10 | async-start | bytes 163840 | tf_op jit(solution)/shard_map/all_to_all | solution.py:39
Sparse Core Ops, SparseCore 0:
  10.1 51.6 all-gather.4
  66.1 87.5 all-gather.6

commit v10 on v8

--- a/solution.py
+++ b/solution.py
@@ -170,9 +170,17 @@
     down = near[:, :RANK].astype(bf16)
     up = near[:, RANK:].astype(bf16).astype(f32).T
 
+    def columns(value, panel):
+        value = jnp.broadcast_to(value[None], (8,) + value.shape)
+        return jnp.einsum("zsk,zkn->zsn", value, panel, preferred_element_type=f32)
+
     thin = jnp.dot(own_state, down, preferred_element_type=f32).reshape(1, 128)
-    thin = jnp.sum(share(thin, DP, 64), axis=0).reshape(2, RANK)
-    resid = base + scale * jnp.dot(thin, up, precision=HIGHEST)
+    inner = share(thin, DP, 64)
+    ahead = columns((jnp.concatenate([up, base], axis=0) * tile_gain).astype(bf16), panel)
+    ahead_up = ahead[:, :RANK].astype(bf16)
+    inner, ahead_up, ahead = lax.optimization_barrier((inner, ahead_up, ahead[:, RANK:]))
+    inner = jnp.sum(inner, axis=0).reshape(2, RANK)
+    resid = base + scale * jnp.dot(inner, up, precision=HIGHEST)
 
     def packed(sums):
         halves = [jnp.broadcast_to(half[:, None], (2, 32)) for half in high_low(sums)]
@@ -182,12 +190,11 @@
         own = (resid * tile_gain).astype(bf16)
         thin = jnp.dot(own, down, preferred_element_type=f32).astype(bf16).reshape(1, 128)
         extra = jnp.concatenate([thin, packed(jnp.sum(resid * resid, axis=1))], axis=0)
-        sums = jnp.einsum(
-            "zsk,zkn->zsn",
-            jnp.broadcast_to(own[None], (8, 2, TILE)),
-            panel,
-            preferred_element_type=f32,
-        )
+        if step == 1:
+            sums = columns(jnp.concatenate(high_low(inner), axis=0), ahead_up)
+            sums = ahead + scale * (sums[:, :2] + sums[:, 2:])
+        else:
+            sums = columns(own, panel)
         sums = lax.optimization_barrier(sums.astype(bf16))
         sums = sums.reshape(8, 2, 8, TILE).transpose(0, 2, 1, 3).reshape(64, 4, 128)
         sent = jnp.concatenate([sums, jnp.broadcast_to(extra[None], (64, 2, 128))], axis=1)

time: 256 us -> 254 us (level)
  waiting for transfers between devices: 82.9 us -> 76.2 us
    ppermute x1, waiting for transfers between devices: 6.6 us -> 0.01 us  [body(): lax.ppermute(jnp.concatenate([own_grads.astype(bf16), old.astype(bf16), *...]
    ppermute x1, starting transfers between devices: 2.77 us -> 6.15 us  [body(): lax.ppermute(jnp.concatenate([own_grads.astype(bf16), old.astype(bf16), *...]
    all_to_all x8, starting transfers between devices: 61 us -> 58.3 us  [swap(): return lax.all_to_all(chunks, axes, 0, 0, tiled=False)]
    dot_general x4 -> x5, matrix products: 13.9 us -> 14.7 us  [the longest x4 14.5 us: columns(): return jnp.einsum('zsk,zkn->zsn', value, panel, preferred_element_type=f32)]
  transfers between devices with their start and end apart: 12 -> 12, of which waited for: 9 -> 9; matrix products, arithmetic and copies ran while one was open for 7% -> 8% of each run, Pallas kernels for 0% -> 0%
where the time goes in v10:
time: 254 us; the launch traced here: 252 us
  waiting for transfers between devices  76.2 us (30%)
  starting transfers between devices  73.3 us (29%)
  blocking collectives  46.8 us (18%)
  matrix products  17.9 us (7%)
  between operations  16.7 us (7%)
  local copies, waits for them, and re-layouts  12.4 us (5%)
  other arithmetic  9.2 us (4%)
    all_to_all x8, waiting for transfers between devices, swap(): return lax.all_to_all(chunks, axes, 0, 0, tiled=False)  74.3 us
    all_to_all x8, starting transfers between devices, swap(): return lax.all_to_all(chunks, axes, 0, 0, tiled=False)  58.3 us
    all_to_all x3, blocking collectives, swap(): return lax.all_to_all(chunks, axes, 0, 0, tiled=False)  46.8 us
    dot_general x4, matrix products, columns(): return jnp.einsum('zsk,zkn->zsn', value, panel, preferred_element_type=f32)  14.5 us
    ppermute x2, starting transfers between devices, core_swap(): return lax.ppermute(value, 'core', [(0, 1), (1, 0)])  8.83 us
    ppermute x1, starting transfers between devices, body(): lax.ppermute(jnp.concatenate([own_grads.astype(bf16), old.astype(bf16), *...  6.15 us
  transfers between devices with their start and end apart: 12, of which 9 were waited for; matrix products, arithmetic and copies ran while one was open for 8% of the time, Pallas kernels for 0%

profile of v10, /device:TPU:1, one launch (start us, length us, event | category | flops | bytes accessed | tf_op | source)
XLA Modules:
  0.0 252.4 jit_solution(17915958071959646114)
XLA Ops:
  7.9 0.8 bitcast_convert_fusion
  9.5 10.5 %all-to-all-start = ((bf16[32,32,128]{2,1,0:T(8,128)(2,1)}), bf16[32,32,128]{2,1,0:T(8,128)(2,1)S(1)}, u32[]{:S(2)}, u32[]{:S(2)}) async-start(bf16[32,32,128]{2,1,0:T(8,128)(2,1)} %broadcast_in_dim.63), calls=%async_computation | async-start | bytes 524288 | tf_op jit(solution)/shard_map/all_to_all | solution.py:38
  23.9 5.8 %all-to-all-done = bf16[32,32,128]{2,1,0:T(8,128)(2,1)S(1)} async-done(((bf16[32,32,128]{2,1,0:T(8,128)(2,1)}), bf16[32,32,128]{2,1,0:T(8,128)(2,1)S(1)}, u32[]{:S(2)}, u32[]{:S(2)}) %all-to-all-start) | async-done | bytes 262176 | tf_op jit(solution)/shard_map/all_to_all | solution.py:38
  29.7 5.6 %collective-permute-start = (bf16[32,32,128]{2,1,0:T(8,128)(2,1)S(1)}, bf16[32,32,128]{2,1,0:T(8,128)(2,1)S(1)}, u32[]{:S(2)}, u32[]{:S(2)}) collective-permute-start(bf16[32,32,128]{2,1,0:T(8,128)(2,1)S(1)} %all-to-all-done), channel_id=1, source_target_pairs={{0,8},{8,0},{1,9},{9,1},{2,10},{10,2},{3,11},{11,3},{4,12},{12,4},... | collective-permute-start | bytes 786440 | tf_op jit(solution)/shard_map/ppermute | solution.py:46
  35.3 1.2 multiply_convert_fusion
  37.8 0.8 broadcast_in_dim.67
  38.6 10.0 %all-to-all-start.1 = ((bf16[8,164,128]{2,1,0:T(8,128)(2,1)}), bf16[8,164,128]{2,1,0:T(8,128)(2,1)S(1)}, u32[]{:S(2)}, u32[]{:S(2)}) async-start(bf16[8,164,128]{2,1,0:T(8,128)(2,1)} %broadcast_in_dim.67), calls=%async_computation.1 | async-start | bytes 688128 | tf_op jit(solution)/shard_map/all_to_all | solution.py:38
  49.1 16.8 %all-to-all-done.1 = bf16[8,164,128]{2,1,0:T(8,128)(2,1)S(1)} async-done(((bf16[8,164,128]{2,1,0:T(8,128)(2,1)}), bf16[8,164,128]{2,1,0:T(8,128)(2,1)S(1)}, u32[]{:S(2)}, u32[]{:S(2)}) %all-to-all-start.1) | async-done | bytes 335904 | tf_op jit(solution)/shard_map/all_to_all | solution.py:38
  68.7 3.2 %collective-permute-start.1 = (bf16[32,40,128]{2,1,0:T(8,128)(2,1)S(1)}, bf16[32,40,128]{2,1,0:T(8,128)(2,1)S(1)}, u32[]{:S(2)}, u32[]{:S(2)}) collective-permute-start(bf16[32,40,128]{2,1,0:T(8,128)(2,1)S(1)} %pad_maximum_fusion), channel_id=1, source_target_pairs={{0,8},{8,0},{1,9},{9,1},{2,10},{10,2},{3,11},{11,3},{4,12},{12,4},... | collective-permute-start | bytes 983048 | tf_op jit(solution)/shard_map/ppermute | solution.py:46
  72.0 1.1 collective-permute-done.1
  73.4 0.8 pad_maximum_fusion.1
  74.2 4.1 %all-to-all-start.2 = ((bf16[32,40,128]{2,1,0:T(8,128)(2,1)}), bf16[32,40,128]{2,1,0:T(8,128)(2,1)S(1)}, u32[]{:S(2)}, u32[]{:S(2)}) async-start(bf16[32,40,128]{2,1,0:T(8,128)(2,1)} %pad_maximum_fusion.1), calls=%async_computation.2 | async-start | bytes 655360 | tf_op jit(solution)/shard_map/all_to_all | solution.py:38
  78.4 10.4 %all-to-all-done.2 = bf16[32,40,128]{2,1,0:T(8,128)(2,1)S(1)} async-done(((bf16[32,40,128]{2,1,0:T(8,128)(2,1)}), bf16[32,40,128]{2,1,0:T(8,128)(2,1)S(1)}, u32[]{:S(2)}, u32[]{:S(2)}) %all-to-all-start.2) | async-done | bytes 327712 | tf_op jit(solution)/shard_map/all_to_all | solution.py:38
  89.0 6.2 %collective-permute-start.2 = (bf16[136,128]{1,0:T(8,128)(2,1)S(1)}, bf16[136,128]{1,0:T(8,128)(2,1)S(1)}, u32[]{:S(2)}, u32[]{:S(2)}) collective-permute-start(bf16[136,128]{1,0:T(8,128)(2,1)S(1)} %concatenate.84), channel_id=1, source_target_pairs={{0,0},{1,64},{2,128},{3,192},{4,256},{5,320},{6,384},{7,448},{8,1}... | collective-permute-start | bytes 104456 | tf_op jit(solution)/shard_map/ppermute | solution.py:133
  95.7 1.3 broadcast_in_dim_broadcast_in_dim_broadcast_in_dim.3
  97.0 7.9 %all-to-all-start.3 = ((f32[64,1,128]{2,1,0:T(1,128)}), f32[64,1,128]{2,1,0:T(1,128)S(1)}, u32[]{:S(2)}, u32[]{:S(2)}) async-start(f32[64,1,128]{2,1,0:T(1,128)} %broadcast_in_dim_broadcast_in_dim_broadcast_in_dim.3), calls=%async_computation.3 | async-start | bytes 65536 | tf_op jit(solution)/shard_map/all_to_all | solution.py:38
  105.6 8.5 %all-to-all-done.3 = f32[64,1,128]{2,1,0:T(1,128)S(1)} async-done(((f32[64,1,128]{2,1,0:T(1,128)}), f32[64,1,128]{2,1,0:T(1,128)S(1)}, u32[]{:S(2)}, u32[]{:S(2)}) %all-to-all-start.3) | async-done | bytes 32800 | tf_op jit(solution)/shard_map/all_to_all | solution.py:38
  114.1 0.8 broadcast_in_dim.68
  114.9 5.4 %all-to-all-start.4 = ((bf16[8,130,128]{2,1,0:T(8,128)(2,1)}), bf16[8,130,128]{2,1,0:T(8,128)(2,1)S(1)}, u32[]{:S(2)}, u32[]{:S(2)}) async-start(bf16[8,130,128]{2,1,0:T(8,128)(2,1)} %broadcast_in_dim.68), calls=%async_computation.4 | async-start | bytes 557056 | tf_op jit(solution)/shard_map/all_to_all | solution.py:38
  120.4 10.7 %all-to-all-done.4 = bf16[8,130,128]{2,1,0:T(8,128)(2,1)S(1)} async-done(((bf16[8,130,128]{2,1,0:T(8,128)(2,1)}), bf16[8,130,128]{2,1,0:T(8,128)(2,1)S(1)}, u32[]{:S(2)}, u32[]{:S(2)}) %all-to-all-start.4) | async-done | bytes 266272 | tf_op jit(solution)/shard_map/all_to_all | solution.py:38
  132.7 9.0 %all-to-all-start.5 = ((f32[64,1,128]{2,1,0:T(1,128)}), f32[64,1,128]{2,1,0:T(1,128)S(1)}, u32[]{:S(2)}, u32[]{:S(2)}) async-start(f32[64,1,128]{2,1,0:T(1,128)} %broadcast_in_dim.71), calls=%async_computation.5 | async-start | bytes 65536 | tf_op jit(solution)/shard_map/all_to_all | solution.py:38
  141.8 5.0 %fusion.16 = f32[8,66,2048]{2,1,0:T(8,128)S(1)} fusion(bf16[8,256,2048]{2,1,0:T(8,128)(2,1)} %bitcast.104, bf16[66,256]{1,0:T(8,128)(2,1)S(1)} %fusion.29), kind=kOutput, calls=%fused_computation.45 | convolution fusion | flops 553648128 | bytes 12747776 | tf_op jit(solution)/shard_map/zsk,zkn->zsn/dot_general | solution.py:175
  147.1 3.8 %all-to-all-done.5 = f32[64,1,128]{2,1,0:T(1,128)S(1)} async-done(((f32[64,1,128]{2,1,0:T(1,128)}), f32[64,1,128]{2,1,0:T(1,128)S(1)}, u32[]{:S(2)}, u32[]{:S(2)}) %all-to-all-start.5) | async-done | bytes 32800 | tf_op jit(solution)/shard_map/all_to_all | solution.py:38
  152.6 16.7 %all_to_all.55 = bf16[64,6,128]{2,1,0:T(8,128)(2,1)S(1)} all-to-all(bf16[64,6,128]{2,1,0:T(8,128)(2,1)S(1)} %pad_maximum_fusion.2), channel_id=1, replica_groups=mesh['x'=4,'ya'=2,'yb'=2,'yc'=2,'core'=2,'z'=8] {'x','ya','yb','yc','core'}, dimensions={0} | all-to-all | bytes 196608 | tf_op jit(solution)/shard_map/all_to_all | solution.py:38
  170.1 4.6 %convolution_convert_fusion.3 = bf16[8,2,2048]{2,1,0:T(2,128)(2,1)S(1)} fusion(bf16[8,256,2048]{2,1,0:T(8,128)(2,1)} %bitcast.105, bf16[2,256]{1,0:T(2,128)(2,1)S(1)} %get-tuple-element.34), kind=kOutput, calls=%fused_computation.5 | convolution fusion | flops 16809984 | bytes 8455168 | tf_op jit(solution)/shard_map/zsk,zkn->zsn/dot_general | solution.py:175
  175.4 15.0 %all_to_all.56 = bf16[64,6,128]{2,1,0:T(8,128)(2,1)S(1)} all-to-all(bf16[64,6,128]{2,1,0:T(8,128)(2,1)S(1)} %pad_maximum_fusion.3), channel_id=1, replica_groups=mesh['x'=4,'ya'=2,'yb'=2,'yc'=2,'core'=2,'z'=8] {'x','ya','yb','yc','core'}, dimensions={0} | all-to-all | bytes 196608 | tf_op jit(solution)/shard_map/all_to_all | solution.py:38
  191.2 4.6 %convolution_convert_fusion.2 = bf16[8,2,2048]{2,1,0:T(2,128)(2,1)S(1)} fusion(bf16[8,256,2048]{2,1,0:T(8,128)(2,1)} %bitcast.106, bf16[2,256]{1,0:T(2,128)(2,1)S(1)} %get-tuple-element.32), kind=kOutput, calls=%fused_computation.4 | convolution fusion | flops 16809984 | bytes 8455168 | tf_op jit(solution)/shard_map/zsk,zkn->zsn/dot_general | solution.py:175
  196.5 15.0 %all_to_all.57 = bf16[64,6,128]{2,1,0:T(8,128)(2,1)S(1)} all-to-all(bf16[64,6,128]{2,1,0:T(8,128)(2,1)S(1)} %pad_maximum_fusion.4), channel_id=1, replica_groups=mesh['x'=4,'ya'=2,'yb'=2,'yc'=2,'core'=2,'z'=8] {'x','ya','yb','yc','core'}, dimensions={0} | all-to-all | bytes 196608 | tf_op jit(solution)/shard_map/all_to_all | solution.py:38
  213.4 5.0 %all-to-all-start.9 = ((bf16[64,5,128]{2,1,0:T(8,128)(2,1)}), bf16[64,5,128]{2,1,0:T(8,128)(2,1)S(1)}, u32[]{:S(2)}, u32[]{:S(2)}) async-start(bf16[64,5,128]{2,1,0:T(8,128)(2,1)} %broadcast_in_dim.87), calls=%async_computation.9 | async-start | bytes 262144 | tf_op jit(solution)/shard_map/all_to_all | solution.py:38
  218.4 13.6 %all-to-all-done.9 = bf16[64,5,128]{2,1,0:T(8,128)(2,1)S(1)} async-done(((bf16[64,5,128]{2,1,0:T(8,128)(2,1)}), bf16[64,5,128]{2,1,0:T(8,128)(2,1)S(1)}, u32[]{:S(2)}, u32[]{:S(2)}) %all-to-all-start.9) | async-done | bytes 81952 | tf_op jit(solution)/shard_map/all_to_all | solution.py:38
  233.0 6.3 %all-to-all-start.10 = ((bf16[8,34,128]{2,1,0:T(8,128)(2,1)}), bf16[8,34,128]{2,1,0:T(8,128)(2,1)S(1)}, u32[]{:S(2)}, u32[]{:S(2)}) async-start(bf16[8,34,128]{2,1,0:T(8,128)(2,1)} %broadcast_in_dim.88), calls=%async_computation.10 | async-start | bytes 163840 | tf_op jit(solution)/shard_map/all_to_all | solution.py:38
  239.9 4.6 %all-to-all-done.10 = bf16[8,34,128]{2,1,0:T(8,128)(2,1)S(1)} async-done(((bf16[8,34,128]{2,1,0:T(8,128)(2,1)}), bf16[8,34,128]{2,1,0:T(8,128)(2,1)S(1)}, u32[]{:S(2)}, u32[]{:S(2)}) %all-to-all-start.10) | async-done | bytes 69664 | tf_op jit(solution)/shard_map/all_to_all | solution.py:38
  (177 shorter events, 20.5 us)
Async XLA Ops:
  7.2 30.0 %copy-start = (bf16[128,2048]{1,0:T(8,128)(2,1)S(1)}, bf16[128,2048]{1,0:T(8,128)(2,1)}, u32[]{:S(2)}) copy-start(bf16[128,2048]{1,0:T(8,128)(2,1)} %param.11) | copy-start | bytes 1572868
  7.2 41.4 %copy-start.1 = (bf16[256,2048]{1,0:T(8,128)(2,1)S(1)}, bf16[256,2048]{1,0:T(8,128)(2,1)}, u32[]{:S(2)}) copy-start(bf16[256,2048]{1,0:T(8,128)(2,1)} %param.19) | copy-start | bytes 3145732
  7.2 134.6 %all-gather.3.cloned.1.call-start = ((), (), s32[]{:S(2)}) async-start(), calls=%async_computation.11 | async-start | bytes 9437184 | tf_op jit(solution)/shard_map/all_gather | solution.py:76
  9.5 20.2 %all-to-all-start = ((bf16[32,32,128]{2,1,0:T(8,128)(2,1)}), bf16[32,32,128]{2,1,0:T(8,128)(2,1)S(1)}, u32[]{:S(2)}, u32[]{:S(2)}) async-start(bf16[32,32,128]{2,1,0:T(8,128)(2,1)} %broadcast_in_dim.63), calls=%async_computation | async-start | bytes 524288 | tf_op jit(solution)/shard_map/all_to_all | solution.py:38
  29.7 6.8 %collective-permute-start = (bf16[32,32,128]{2,1,0:T(8,128)(2,1)S(1)}, bf16[32,32,128]{2,1,0:T(8,128)(2,1)S(1)}, u32[]{:S(2)}, u32[]{:S(2)}) collective-permute-start(bf16[32,32,128]{2,1,0:T(8,128)(2,1)S(1)} %all-to-all-done), channel_id=1, source_target_pairs={{0,8},{8,0},{1,9},{9,1},{2,10},{10,2},{3,11},{11,3},{4,12},{12,4},... | collective-permute-start | bytes 786440 | tf_op jit(solution)/shard_map/ppermute | solution.py:46
  37.2 41.2 %copy-start.3 = (f32[1,32,128]{2,1,0:T(8,128)S(1)}, f32[1,32,128]{2,1,0:T(8,128)}, u32[]{:S(2)}) copy-start(f32[1,32,128]{2,1,0:T(8,128)} %param.18) | copy-start | bytes 49156
  37.2 41.1 %copy-start.4 = (f32[1,32,128]{2,1,0:T(8,128)S(1)}, f32[1,32,128]{2,1,0:T(8,128)}, u32[]{:S(2)}) copy-start(f32[1,32,128]{2,1,0:T(8,128)} %param.17) | copy-start | bytes 49156
  38.6 27.4 %all-to-all-start.1 = ((bf16[8,164,128]{2,1,0:T(8,128)(2,1)}), bf16[8,164,128]{2,1,0:T(8,128)(2,1)S(1)}, u32[]{:S(2)}, u32[]{:S(2)}) async-start(bf16[8,164,128]{2,1,0:T(8,128)(2,1)} %broadcast_in_dim.67), calls=%async_computation.1 | async-start | bytes 688128 | tf_op jit(solution)/shard_map/all_to_all | solution.py:38
  67.2 0.6 copy-start.2
  68.7 4.5 %collective-permute-start.1 = (bf16[32,40,128]{2,1,0:T(8,128)(2,1)S(1)}, bf16[32,40,128]{2,1,0:T(8,128)(2,1)S(1)}, u32[]{:S(2)}, u32[]{:S(2)}) collective-permute-start(bf16[32,40,128]{2,1,0:T(8,128)(2,1)S(1)} %pad_maximum_fusion), channel_id=1, source_target_pairs={{0,8},{8,0},{1,9},{9,1},{2,10},{10,2},{3,11},{11,3},{4,12},{12,4},... | collective-permute-start | bytes 983048 | tf_op jit(solution)/shard_map/ppermute | solution.py:46
  74.2 14.6 %all-to-all-start.2 = ((bf16[32,40,128]{2,1,0:T(8,128)(2,1)}), bf16[32,40,128]{2,1,0:T(8,128)(2,1)S(1)}, u32[]{:S(2)}, u32[]{:S(2)}) async-start(bf16[32,40,128]{2,1,0:T(8,128)(2,1)} %pad_maximum_fusion.1), calls=%async_computation.2 | async-start | bytes 655360 | tf_op jit(solution)/shard_map/all_to_all | solution.py:38
  89.0 16.6 %collective-permute-start.2 = (bf16[136,128]{1,0:T(8,128)(2,1)S(1)}, bf16[136,128]{1,0:T(8,128)(2,1)S(1)}, u32[]{:S(2)}, u32[]{:S(2)}) collective-permute-start(bf16[136,128]{1,0:T(8,128)(2,1)S(1)} %concatenate.84), channel_id=1, source_target_pairs={{0,0},{1,64},{2,128},{3,192},{4,256},{5,320},{6,384},{7,448},{8,1}... | collective-permute-start | bytes 104456 | tf_op jit(solution)/shard_map/ppermute | solution.py:133
  97.0 17.1 %all-to-all-start.3 = ((f32[64,1,128]{2,1,0:T(1,128)}), f32[64,1,128]{2,1,0:T(1,128)S(1)}, u32[]{:S(2)}, u32[]{:S(2)}) async-start(f32[64,1,128]{2,1,0:T(1,128)} %broadcast_in_dim_broadcast_in_dim_broadcast_in_dim.3), calls=%async_computation.3 | async-start | bytes 65536 | tf_op jit(solution)/shard_map/all_to_all | solution.py:38
  114.9 16.2 %all-to-all-start.4 = ((bf16[8,130,128]{2,1,0:T(8,128)(2,1)}), bf16[8,130,128]{2,1,0:T(8,128)(2,1)S(1)}, u32[]{:S(2)}, u32[]{:S(2)}) async-start(bf16[8,130,128]{2,1,0:T(8,128)(2,1)} %broadcast_in_dim.68), calls=%async_computation.4 | async-start | bytes 557056 | tf_op jit(solution)/shard_map/all_to_all | solution.py:38
  132.7 18.2 %all-to-all-start.5 = ((f32[64,1,128]{2,1,0:T(1,128)}), f32[64,1,128]{2,1,0:T(1,128)S(1)}, u32[]{:S(2)}, u32[]{:S(2)}) async-start(f32[64,1,128]{2,1,0:T(1,128)} %broadcast_in_dim.71), calls=%async_computation.5 | async-start | bytes 65536 | tf_op jit(solution)/shard_map/all_to_all | solution.py:38
  174.7 64.6 %copy-start.5 = (f32[1,32,128]{2,1,0:T(8,128)S(1)}, f32[1,32,128]{2,1,0:T(8,128)}, u32[]{:S(2)}) copy-start(f32[1,32,128]{2,1,0:T(8,128)} %param.16) | copy-start | bytes 49156
  213.4 18.6 %all-to-all-start.9 = ((bf16[64,5,128]{2,1,0:T(8,128)(2,1)}), bf16[64,5,128]{2,1,0:T(8,128)(2,1)S(1)}, u32[]{:S(2)}, u32[]{:S(2)}) async-start(bf16[64,5,128]{2,1,0:T(8,128)(2,1)} %broadcast_in_dim.87), calls=%async_computation.9 | async-start | bytes 262144 | tf_op jit(solution)/shard_map/all_to_all | solution.py:38
  233.0 11.6 %all-to-all-start.10 = ((bf16[8,34,128]{2,1,0:T(8,128)(2,1)}), bf16[8,34,128]{2,1,0:T(8,128)(2,1)S(1)}, u32[]{:S(2)}, u32[]{:S(2)}) async-start(bf16[8,34,128]{2,1,0:T(8,128)(2,1)} %broadcast_in_dim.88), calls=%async_computation.10 | async-start | bytes 163840 | tf_op jit(solution)/shard_map/all_to_all | solution.py:38
Sparse Core Ops, SparseCore 0:
  10.1 113.4 all-gather.2

commit v11 on v10

--- a/solution.py
+++ b/solution.py
@@ -207,15 +207,12 @@
 
     own = (resid * tile_gain).astype(bf16).reshape(4, 128)
     sent = jnp.concatenate([own, packed(jnp.sum(resid * resid, axis=1))], axis=0)
-    got = share(sent, CROSS, 64).reshape(8, 8, 5, 128)
-    sums = jnp.sum(got[:, :, 4].astype(f32), axis=0).reshape(BATCH, 2, 32)[:, :, :8]
-    sums = (sums[:, 0] + sums[:, 1]).reshape(1, 128)
-    sent = jnp.concatenate([pick(got[:, :, :4], z, 0).reshape(32, 128), *high_low(sums)], axis=0)
-    got = share(sent, MINOR, 8)
-    sums = jnp.sum(got[:, 32:].astype(f32), axis=(0, 1)).reshape(BATCH, 8)[:, :1]
-    norm = lax.rsqrt(sums / MODEL_WIDTH + 1e-05)
-    result = got[:, :32].reshape(8, BATCH, TILE).transpose(1, 0, 2).reshape(BATCH, BLOCK)
+    got = share(sent, DP, 64)
+    sums = jnp.sum(got[:, 4].astype(f32), axis=0).reshape(2, 2, 32)[:, :, 0]
+    norm = lax.rsqrt((sums[:, :1] + sums[:, 1:]) / MODEL_WIDTH + 1e-05)
+    result = got[:, :4].reshape(8, 8, 2, TILE).transpose(0, 2, 1, 3).reshape(8, 2, BLOCK)
     result = (result.astype(f32) * norm).astype(bf16)
+    result = swap(result, "z").reshape(BATCH, BLOCK)
     return (new_factors, result)
 
 

time: 254 us -> 248 us (0.976)
  blocking collectives: 46.8 us -> 61.8 us
  waiting for transfers between devices: 76.2 us -> 64.4 us
  starting transfers between devices: 73.3 us -> 65.3 us
    all_to_all x3 -> x4, blocking collectives: 46.8 us -> 61.8 us  [swap(): return lax.all_to_all(chunks, axes, 0, 0, tiled=False)]
    all_to_all x8 -> x7, waiting for transfers between devices: 74.3 us -> 62.5 us  [swap(): return lax.all_to_all(chunks, axes, 0, 0, tiled=False)]
    all_to_all x8 -> x7, starting transfers between devices: 58.3 us -> 50.3 us  [swap(): return lax.all_to_all(chunks, axes, 0, 0, tiled=False)]
  transfers between devices with their start and end apart: 12 -> 11, of which waited for: 9 -> 8; matrix products, arithmetic and copies ran while one was open for 8% -> 9% of each run, Pallas kernels for 0% -> 0%
where the time goes in v11:
time: 248 us; the launch traced here: 247 us
  starting transfers between devices  65.3 us (26%)
  waiting for transfers between devices  64.4 us (26%)
  blocking collectives  61.8 us (25%)
  matrix products  17.9 us (7%)
  between operations  16.7 us (7%)
  local copies, waits for them, and re-layouts  11.7 us (5%)
  other arithmetic  9.27 us (4%)
    all_to_all x7, waiting for transfers between devices, swap(): return lax.all_to_all(chunks, axes, 0, 0, tiled=False)  62.5 us
    all_to_all x4, blocking collectives, swap(): return lax.all_to_all(chunks, axes, 0, 0, tiled=False)  61.8 us
    all_to_all x7, starting transfers between devices, swap(): return lax.all_to_all(chunks, axes, 0, 0, tiled=False)  50.3 us
    dot_general x4, matrix products, columns(): return jnp.einsum('zsk,zkn->zsn', value, panel, preferred_element_type=f32)  14.5 us
    ppermute x2, starting transfers between devices, core_swap(): return lax.ppermute(value, 'core', [(0, 1), (1, 0)])  8.83 us
    ppermute x1, starting transfers between devices, body(): lax.ppermute(jnp.concatenate([own_grads.astype(bf16), old.astype(bf16), *...  6.15 us
  transfers between devices with their start and end apart: 11, of which 8 were waited for; matrix products, arithmetic and copies ran while one was open for 9% of the time, Pallas kernels for 0%

profile of v11, /device:TPU:1, one launch (start us, length us, event | category | flops | bytes accessed | tf_op | source)
XLA Modules:
  0.0 247.1 jit_solution(15434431454667336967)
XLA Ops:
  7.9 0.8 bitcast_convert_fusion
  9.5 10.5 %all-to-all-start = ((bf16[32,32,128]{2,1,0:T(8,128)(2,1)}), bf16[32,32,128]{2,1,0:T(8,128)(2,1)S(1)}, u32[]{:S(2)}, u32[]{:S(2)}) async-start(bf16[32,32,128]{2,1,0:T(8,128)(2,1)} %broadcast_in_dim.61), calls=%async_computation | async-start | bytes 524288 | tf_op jit(solution)/shard_map/all_to_all | solution.py:38
  20.0 0.8 fusion.67
  23.9 5.8 %all-to-all-done = bf16[32,32,128]{2,1,0:T(8,128)(2,1)S(1)} async-done(((bf16[32,32,128]{2,1,0:T(8,128)(2,1)}), bf16[32,32,128]{2,1,0:T(8,128)(2,1)S(1)}, u32[]{:S(2)}, u32[]{:S(2)}) %all-to-all-start) | async-done | bytes 262176 | tf_op jit(solution)/shard_map/all_to_all | solution.py:38
  29.7 5.6 %collective-permute-start = (bf16[32,32,128]{2,1,0:T(8,128)(2,1)S(1)}, bf16[32,32,128]{2,1,0:T(8,128)(2,1)S(1)}, u32[]{:S(2)}, u32[]{:S(2)}) collective-permute-start(bf16[32,32,128]{2,1,0:T(8,128)(2,1)S(1)} %all-to-all-done), channel_id=1, source_target_pairs={{0,8},{8,0},{1,9},{9,1},{2,10},{10,2},{3,11},{11,3},{4,12},{12,4},... | collective-permute-start | bytes 786440 | tf_op jit(solution)/shard_map/ppermute | solution.py:46
  35.3 1.2 multiply_convert_fusion
  37.8 0.8 broadcast_in_dim.65
  38.6 10.0 %all-to-all-start.1 = ((bf16[8,164,128]{2,1,0:T(8,128)(2,1)}), bf16[8,164,128]{2,1,0:T(8,128)(2,1)S(1)}, u32[]{:S(2)}, u32[]{:S(2)}) async-start(bf16[8,164,128]{2,1,0:T(8,128)(2,1)} %broadcast_in_dim.65), calls=%async_computation.1 | async-start | bytes 688128 | tf_op jit(solution)/shard_map/all_to_all | solution.py:38
  49.1 16.8 %all-to-all-done.1 = bf16[8,164,128]{2,1,0:T(8,128)(2,1)S(1)} async-done(((bf16[8,164,128]{2,1,0:T(8,128)(2,1)}), bf16[8,164,128]{2,1,0:T(8,128)(2,1)S(1)}, u32[]{:S(2)}, u32[]{:S(2)}) %all-to-all-start.1) | async-done | bytes 335904 | tf_op jit(solution)/shard_map/all_to_all | solution.py:38
  68.7 3.2 %collective-permute-start.1 = (bf16[32,40,128]{2,1,0:T(8,128)(2,1)S(1)}, bf16[32,40,128]{2,1,0:T(8,128)(2,1)S(1)}, u32[]{:S(2)}, u32[]{:S(2)}) collective-permute-start(bf16[32,40,128]{2,1,0:T(8,128)(2,1)S(1)} %pad_maximum_fusion), channel_id=1, source_target_pairs={{0,8},{8,0},{1,9},{9,1},{2,10},{10,2},{3,11},{11,3},{4,12},{12,4},... | collective-permute-start | bytes 983048 | tf_op jit(solution)/shard_map/ppermute | solution.py:46
  72.0 1.1 collective-permute-done.1
  73.4 0.8 pad_maximum_fusion.1
  74.2 4.1 %all-to-all-start.2 = ((bf16[32,40,128]{2,1,0:T(8,128)(2,1)}), bf16[32,40,128]{2,1,0:T(8,128)(2,1)S(1)}, u32[]{:S(2)}, u32[]{:S(2)}) async-start(bf16[32,40,128]{2,1,0:T(8,128)(2,1)} %pad_maximum_fusion.1), calls=%async_computation.2 | async-start | bytes 655360 | tf_op jit(solution)/shard_map/all_to_all | solution.py:38
  78.4 10.4 %all-to-all-done.2 = bf16[32,40,128]{2,1,0:T(8,128)(2,1)S(1)} async-done(((bf16[32,40,128]{2,1,0:T(8,128)(2,1)}), bf16[32,40,128]{2,1,0:T(8,128)(2,1)S(1)}, u32[]{:S(2)}, u32[]{:S(2)}) %all-to-all-start.2) | async-done | bytes 327712 | tf_op jit(solution)/shard_map/all_to_all | solution.py:38
  89.0 6.2 %collective-permute-start.2 = (bf16[136,128]{1,0:T(8,128)(2,1)S(1)}, bf16[136,128]{1,0:T(8,128)(2,1)S(1)}, u32[]{:S(2)}, u32[]{:S(2)}) collective-permute-start(bf16[136,128]{1,0:T(8,128)(2,1)S(1)} %concatenate.81), channel_id=1, source_target_pairs={{0,0},{1,64},{2,128},{3,192},{4,256},{5,320},{6,384},{7,448},{8,1}... | collective-permute-start | bytes 104456 | tf_op jit(solution)/shard_map/ppermute | solution.py:133
  95.7 1.3 broadcast_in_dim_broadcast_in_dim_broadcast_in_dim.3
  97.0 7.9 %all-to-all-start.3 = ((f32[64,1,128]{2,1,0:T(1,128)}), f32[64,1,128]{2,1,0:T(1,128)S(1)}, u32[]{:S(2)}, u32[]{:S(2)}) async-start(f32[64,1,128]{2,1,0:T(1,128)} %broadcast_in_dim_broadcast_in_dim_broadcast_in_dim.3), calls=%async_computation.3 | async-start | bytes 65536 | tf_op jit(solution)/shard_map/all_to_all | solution.py:38
  105.6 8.5 %all-to-all-done.3 = f32[64,1,128]{2,1,0:T(1,128)S(1)} async-done(((f32[64,1,128]{2,1,0:T(1,128)}), f32[64,1,128]{2,1,0:T(1,128)S(1)}, u32[]{:S(2)}, u32[]{:S(2)}) %all-to-all-start.3) | async-done | bytes 32800 | tf_op jit(solution)/shard_map/all_to_all | solution.py:38
  114.1 0.8 broadcast_in_dim.66
  114.9 5.4 %all-to-all-start.4 = ((bf16[8,130,128]{2,1,0:T(8,128)(2,1)}), bf16[8,130,128]{2,1,0:T(8,128)(2,1)S(1)}, u32[]{:S(2)}, u32[]{:S(2)}) async-start(bf16[8,130,128]{2,1,0:T(8,128)(2,1)} %broadcast_in_dim.66), calls=%async_computation.4 | async-start | bytes 557056 | tf_op jit(solution)/shard_map/all_to_all | solution.py:38
  120.4 10.7 %all-to-all-done.4 = bf16[8,130,128]{2,1,0:T(8,128)(2,1)S(1)} async-done(((bf16[8,130,128]{2,1,0:T(8,128)(2,1)}), bf16[8,130,128]{2,1,0:T(8,128)(2,1)S(1)}, u32[]{:S(2)}, u32[]{:S(2)}) %all-to-all-start.4) | async-done | bytes 266272 | tf_op jit(solution)/shard_map/all_to_all | solution.py:38
  132.7 9.0 %all-to-all-start.5 = ((f32[64,1,128]{2,1,0:T(1,128)}), f32[64,1,128]{2,1,0:T(1,128)S(1)}, u32[]{:S(2)}, u32[]{:S(2)}) async-start(f32[64,1,128]{2,1,0:T(1,128)} %broadcast_in_dim.69), calls=%async_computation.5 | async-start | bytes 65536 | tf_op jit(solution)/shard_map/all_to_all | solution.py:38
  141.8 5.0 %fusion.16 = f32[8,66,2048]{2,1,0:T(8,128)S(1)} fusion(bf16[8,256,2048]{2,1,0:T(8,128)(2,1)} %bitcast.102, bf16[66,256]{1,0:T(8,128)(2,1)S(1)} %fusion.29), kind=kOutput, calls=%fused_computation.45 | convolution fusion | flops 553648128 | bytes 12747776 | tf_op jit(solution)/shard_map/zsk,zkn->zsn/dot_general | solution.py:175
  147.1 3.8 %all-to-all-done.5 = f32[64,1,128]{2,1,0:T(1,128)S(1)} async-done(((f32[64,1,128]{2,1,0:T(1,128)}), f32[64,1,128]{2,1,0:T(1,128)S(1)}, u32[]{:S(2)}, u32[]{:S(2)}) %all-to-all-start.5) | async-done | bytes 32800 | tf_op jit(solution)/shard_map/all_to_all | solution.py:38
  152.6 16.7 %all_to_all.55 = bf16[64,6,128]{2,1,0:T(8,128)(2,1)S(1)} all-to-all(bf16[64,6,128]{2,1,0:T(8,128)(2,1)S(1)} %pad_maximum_fusion.2), channel_id=1, replica_groups=mesh['x'=4,'ya'=2,'yb'=2,'yc'=2,'core'=2,'z'=8] {'x','ya','yb','yc','core'}, dimensions={0} | all-to-all | bytes 196608 | tf_op jit(solution)/shard_map/all_to_all | solution.py:38
  170.1 4.6 %convolution_convert_fusion.3 = bf16[8,2,2048]{2,1,0:T(2,128)(2,1)S(1)} fusion(bf16[8,256,2048]{2,1,0:T(8,128)(2,1)} %bitcast.103, bf16[2,256]{1,0:T(2,128)(2,1)S(1)} %get-tuple-element.34), kind=kOutput, calls=%fused_computation.5 | convolution fusion | flops 16809984 | bytes 8455168 | tf_op jit(solution)/shard_map/zsk,zkn->zsn/dot_general | solution.py:175
  175.4 15.0 %all_to_all.56 = bf16[64,6,128]{2,1,0:T(8,128)(2,1)S(1)} all-to-all(bf16[64,6,128]{2,1,0:T(8,128)(2,1)S(1)} %pad_maximum_fusion.3), channel_id=1, replica_groups=mesh['x'=4,'ya'=2,'yb'=2,'yc'=2,'core'=2,'z'=8] {'x','ya','yb','yc','core'}, dimensions={0} | all-to-all | bytes 196608 | tf_op jit(solution)/shard_map/all_to_all | solution.py:38
  191.2 4.6 %convolution_convert_fusion.2 = bf16[8,2,2048]{2,1,0:T(2,128)(2,1)S(1)} fusion(bf16[8,256,2048]{2,1,0:T(8,128)(2,1)} %bitcast.104, bf16[2,256]{1,0:T(2,128)(2,1)S(1)} %get-tuple-element.32), kind=kOutput, calls=%fused_computation.4 | convolution fusion | flops 16809984 | bytes 8455168 | tf_op jit(solution)/shard_map/zsk,zkn->zsn/dot_general | solution.py:175
  196.5 15.0 %all_to_all.57 = bf16[64,6,128]{2,1,0:T(8,128)(2,1)S(1)} all-to-all(bf16[64,6,128]{2,1,0:T(8,128)(2,1)S(1)} %pad_maximum_fusion.4), channel_id=1, replica_groups=mesh['x'=4,'ya'=2,'yb'=2,'yc'=2,'core'=2,'z'=8] {'x','ya','yb','yc','core'}, dimensions={0} | all-to-all | bytes 196608 | tf_op jit(solution)/shard_map/all_to_all | solution.py:38
  212.8 15.0 %all_to_all.58 = bf16[64,5,128]{2,1,0:T(8,128)(2,1)S(1)} all-to-all(bf16[64,5,128]{2,1,0:T(8,128)(2,1)S(1)} %broadcast_in_dim.85), channel_id=1, replica_groups=mesh['x'=4,'ya'=2,'yb'=2,'yc'=2,'core'=2,'z'=8] {'x','ya','yb','yc','core'}, dimensions={0} | all-to-all | bytes 163840 | tf_op jit(solution)/shard_map/all_to_all | solution.py:38
  229.1 3.4 %all-to-all-start.10 = ((bf16[8,2,2048]{2,1,0:T(2,128)(2,1)}), bf16[8,2,2048]{2,1,0:T(2,128)(2,1)S(1)}, u32[]{:S(2)}, u32[]{:S(2)}) async-start(bf16[8,2,2048]{2,1,0:T(2,128)(2,1)} %multiply_convert_fusion.1), calls=%async_computation.10 | async-start | bytes 131072 | tf_op jit(solution)/shard_map/all_to_all | solution.py:38
  233.2 6.4 %all-to-all-done.10 = bf16[8,2,2048]{2,1,0:T(2,128)(2,1)S(1)} async-done(((bf16[8,2,2048]{2,1,0:T(2,128)(2,1)}), bf16[8,2,2048]{2,1,0:T(2,128)(2,1)S(1)}, u32[]{:S(2)}, u32[]{:S(2)}) %all-to-all-start.10) | async-done | bytes 65568 | tf_op jit(solution)/shard_map/all_to_all | solution.py:38
  (168 shorter events, 19.1 us)
Async XLA Ops:
  7.2 30.0 %copy-start = (bf16[128,2048]{1,0:T(8,128)(2,1)S(1)}, bf16[128,2048]{1,0:T(8,128)(2,1)}, u32[]{:S(2)}) copy-start(bf16[128,2048]{1,0:T(8,128)(2,1)} %param.11) | copy-start | bytes 1572868
  7.2 41.4 %copy-start.1 = (bf16[256,2048]{1,0:T(8,128)(2,1)S(1)}, bf16[256,2048]{1,0:T(8,128)(2,1)}, u32[]{:S(2)}) copy-start(bf16[256,2048]{1,0:T(8,128)(2,1)} %param.19) | copy-start | bytes 3145732
  7.2 134.6 %all-gather.3.cloned.1.call-start = ((), (), s32[]{:S(2)}) async-start(), calls=%async_computation.11 | async-start | bytes 9437184 | tf_op jit(solution)/shard_map/all_gather | solution.py:76
  9.5 20.2 %all-to-all-start = ((bf16[32,32,128]{2,1,0:T(8,128)(2,1)}), bf16[32,32,128]{2,1,0:T(8,128)(2,1)S(1)}, u32[]{:S(2)}, u32[]{:S(2)}) async-start(bf16[32,32,128]{2,1,0:T(8,128)(2,1)} %broadcast_in_dim.61), calls=%async_computation | async-start | bytes 524288 | tf_op jit(solution)/shard_map/all_to_all | solution.py:38
  29.7 6.8 %collective-permute-start = (bf16[32,32,128]{2,1,0:T(8,128)(2,1)S(1)}, bf16[32,32,128]{2,1,0:T(8,128)(2,1)S(1)}, u32[]{:S(2)}, u32[]{:S(2)}) collective-permute-start(bf16[32,32,128]{2,1,0:T(8,128)(2,1)S(1)} %all-to-all-done), channel_id=1, source_target_pairs={{0,8},{8,0},{1,9},{9,1},{2,10},{10,2},{3,11},{11,3},{4,12},{12,4},... | collective-permute-start | bytes 786440 | tf_op jit(solution)/shard_map/ppermute | solution.py:46
  37.2 41.2 %copy-start.3 = (f32[1,32,128]{2,1,0:T(8,128)S(1)}, f32[1,32,128]{2,1,0:T(8,128)}, u32[]{:S(2)}) copy-start(f32[1,32,128]{2,1,0:T(8,128)} %param.18) | copy-start | bytes 49156
  37.2 41.1 %copy-start.4 = (f32[1,32,128]{2,1,0:T(8,128)S(1)}, f32[1,32,128]{2,1,0:T(8,128)}, u32[]{:S(2)}) copy-start(f32[1,32,128]{2,1,0:T(8,128)} %param.17) | copy-start | bytes 49156
  38.6 27.4 %all-to-all-start.1 = ((bf16[8,164,128]{2,1,0:T(8,128)(2,1)}), bf16[8,164,128]{2,1,0:T(8,128)(2,1)S(1)}, u32[]{:S(2)}, u32[]{:S(2)}) async-start(bf16[8,164,128]{2,1,0:T(8,128)(2,1)} %broadcast_in_dim.65), calls=%async_computation.1 | async-start | bytes 688128 | tf_op jit(solution)/shard_map/all_to_all | solution.py:38
  67.2 0.6 copy-start.2
  68.7 4.5 %collective-permute-start.1 = (bf16[32,40,128]{2,1,0:T(8,128)(2,1)S(1)}, bf16[32,40,128]{2,1,0:T(8,128)(2,1)S(1)}, u32[]{:S(2)}, u32[]{:S(2)}) collective-permute-start(bf16[32,40,128]{2,1,0:T(8,128)(2,1)S(1)} %pad_maximum_fusion), channel_id=1, source_target_pairs={{0,8},{8,0},{1,9},{9,1},{2,10},{10,2},{3,11},{11,3},{4,12},{12,4},... | collective-permute-start | bytes 983048 | tf_op jit(solution)/shard_map/ppermute | solution.py:46
  74.2 14.6 %all-to-all-start.2 = ((bf16[32,40,128]{2,1,0:T(8,128)(2,1)}), bf16[32,40,128]{2,1,0:T(8,128)(2,1)S(1)}, u32[]{:S(2)}, u32[]{:S(2)}) async-start(bf16[32,40,128]{2,1,0:T(8,128)(2,1)} %pad_maximum_fusion.1), calls=%async_computation.2 | async-start | bytes 655360 | tf_op jit(solution)/shard_map/all_to_all | solution.py:38
  89.0 16.6 %collective-permute-start.2 = (bf16[136,128]{1,0:T(8,128)(2,1)S(1)}, bf16[136,128]{1,0:T(8,128)(2,1)S(1)}, u32[]{:S(2)}, u32[]{:S(2)}) collective-permute-start(bf16[136,128]{1,0:T(8,128)(2,1)S(1)} %concatenate.81), channel_id=1, source_target_pairs={{0,0},{1,64},{2,128},{3,192},{4,256},{5,320},{6,384},{7,448},{8,1}... | collective-permute-start | bytes 104456 | tf_op jit(solution)/shard_map/ppermute | solution.py:133
  97.0 17.1 %all-to-all-start.3 = ((f32[64,1,128]{2,1,0:T(1,128)}), f32[64,1,128]{2,1,0:T(1,128)S(1)}, u32[]{:S(2)}, u32[]{:S(2)}) async-start(f32[64,1,128]{2,1,0:T(1,128)} %broadcast_in_dim_broadcast_in_dim_broadcast_in_dim.3), calls=%async_computation.3 | async-start | bytes 65536 | tf_op jit(solution)/shard_map/all_to_all | solution.py:38
  114.9 16.2 %all-to-all-start.4 = ((bf16[8,130,128]{2,1,0:T(8,128)(2,1)}), bf16[8,130,128]{2,1,0:T(8,128)(2,1)S(1)}, u32[]{:S(2)}, u32[]{:S(2)}) async-start(bf16[8,130,128]{2,1,0:T(8,128)(2,1)} %broadcast_in_dim.66), calls=%async_computation.4 | async-start | bytes 557056 | tf_op jit(solution)/shard_map/all_to_all | solution.py:38
  132.7 18.2 %all-to-all-start.5 = ((f32[64,1,128]{2,1,0:T(1,128)}), f32[64,1,128]{2,1,0:T(1,128)S(1)}, u32[]{:S(2)}, u32[]{:S(2)}) async-start(f32[64,1,128]{2,1,0:T(1,128)} %broadcast_in_dim.69), calls=%async_computation.5 | async-start | bytes 65536 | tf_op jit(solution)/shard_map/all_to_all | solution.py:38
  174.7 57.8 %copy-start.5 = (f32[1,32,128]{2,1,0:T(8,128)S(1)}, f32[1,32,128]{2,1,0:T(8,128)}, u32[]{:S(2)}) copy-start(f32[1,32,128]{2,1,0:T(8,128)} %param.16) | copy-start | bytes 49156
  229.1 10.4 %all-to-all-start.10 = ((bf16[8,2,2048]{2,1,0:T(2,128)(2,1)}), bf16[8,2,2048]{2,1,0:T(2,128)(2,1)S(1)}, u32[]{:S(2)}, u32[]{:S(2)}) async-start(bf16[8,2,2048]{2,1,0:T(2,128)(2,1)} %multiply_convert_fusion.1), calls=%async_computation.10 | async-start | bytes 131072 | tf_op jit(solution)/shard_map/all_to_all | solution.py:38
Sparse Core Ops, SparseCore 0:
  10.1 113.4 all-gather.2

commit v12 on v11

--- a/solution.py
+++ b/solution.py
@@ -138,12 +138,12 @@
     base = (got[4 * OWN : 4 * OWN + 4].astype(f32) + got[4 * OWN + 4 :].astype(f32)).reshape(2, TILE)
     base = base + own_state.astype(f32)
     own_grads = scale * own_grads
-    squared = jnp.broadcast_to(jnp.sum(own_grads * own_grads), (1, 128))
+    squared = jnp.sum(own_grads * own_grads, axis=0, keepdims=True)
     squared = jnp.sum(share(squared, DP, 64), axis=0)
     got = share(jnp.concatenate([got[: 4 * OWN], *high_low(squared)], axis=0), "z", 8).astype(f32)
     grads = scale * got[:, :OWN].reshape(TILE, 128)
     former = got[:, OWN : 4 * OWN]
-    squared = jnp.sum(got[:, 4 * OWN :], axis=(0, 1))[None]
+    squared = jnp.sum(got[:, 4 * OWN :])
 
     clip = jnp.minimum(f32(1.0), f32(1.0) / (jnp.sqrt(squared) + 1e-06))
     grads = clip * grads

time: 248 us -> 248 us (level)
  waiting for transfers between devices: 64.4 us -> 67.1 us
  starting transfers between devices: 65.3 us -> 62.8 us
    all_to_all x7, waiting for transfers between devices: 62.5 us -> 65.3 us  [swap(): return lax.all_to_all(chunks, axes, 0, 0, tiled=False)]
    all_to_all x7, starting transfers between devices: 50.3 us -> 47.8 us  [swap(): return lax.all_to_all(chunks, axes, 0, 0, tiled=False)]
  transfers between devices with their start and end apart: 11 -> 11, of which waited for: 8 -> 8; matrix products, arithmetic and copies ran while one was open for 9% -> 8% of each run, Pallas kernels for 0% -> 0%
where the time goes in v12:
time: 248 us; the launch traced here: 247 us
  waiting for transfers between devices  67.1 us (27%)
  starting transfers between devices  62.8 us (25%)
  blocking collectives  61.8 us (25%)
  matrix products  17.9 us (7%)
  between operations  17.4 us (7%)
  local copies, waits for them, and re-layouts  11.1 us (4%)
  other arithmetic  9.2 us (4%)
    all_to_all x7, waiting for transfers between devices, swap(): return lax.all_to_all(chunks, axes, 0, 0, tiled=False)  65.3 us
    all_to_all x4, blocking collectives, swap(): return lax.all_to_all(chunks, axes, 0, 0, tiled=False)  61.8 us
    all_to_all x7, starting transfers between devices, swap(): return lax.all_to_all(chunks, axes, 0, 0, tiled=False)  47.8 us
    dot_general x4, matrix products, columns(): return jnp.einsum('zsk,zkn->zsn', value, panel, preferred_element_type=f32)  14.5 us
    ppermute x2, starting transfers between devices, core_swap(): return lax.ppermute(value, 'core', [(0, 1), (1, 0)])  8.83 us
    ppermute x1, starting transfers between devices, body(): lax.ppermute(jnp.concatenate([own_grads.astype(bf16), old.astype(bf16), *...  6.15 us
  transfers between devices with their start and end apart: 11, of which 8 were waited for; matrix products, arithmetic and copies ran while one was open for 8% of the time, Pallas kernels for 0%

profile of v12, /device:TPU:1, one launch (start us, length us, event | category | flops | bytes accessed | tf_op | source)
XLA Modules:
  0.0 247.3 jit_solution(14813325436571074504)
XLA Ops:
  7.9 0.8 bitcast_convert_fusion
  9.5 10.5 %all-to-all-start = ((bf16[32,32,128]{2,1,0:T(8,128)(2,1)}), bf16[32,32,128]{2,1,0:T(8,128)(2,1)S(1)}, u32[]{:S(2)}, u32[]{:S(2)}) async-start(bf16[32,32,128]{2,1,0:T(8,128)(2,1)} %broadcast_in_dim.63), calls=%async_computation | async-start | bytes 524288 | tf_op jit(solution)/shard_map/all_to_all | solution.py:38
  20.0 0.8 fusion.67
  23.9 5.8 %all-to-all-done = bf16[32,32,128]{2,1,0:T(8,128)(2,1)S(1)} async-done(((bf16[32,32,128]{2,1,0:T(8,128)(2,1)}), bf16[32,32,128]{2,1,0:T(8,128)(2,1)S(1)}, u32[]{:S(2)}, u32[]{:S(2)}) %all-to-all-start) | async-done | bytes 262176 | tf_op jit(solution)/shard_map/all_to_all | solution.py:38
  29.7 5.6 %collective-permute-start = (bf16[32,32,128]{2,1,0:T(8,128)(2,1)S(1)}, bf16[32,32,128]{2,1,0:T(8,128)(2,1)S(1)}, u32[]{:S(2)}, u32[]{:S(2)}) collective-permute-start(bf16[32,32,128]{2,1,0:T(8,128)(2,1)S(1)} %all-to-all-done), channel_id=1, source_target_pairs={{0,8},{8,0},{1,9},{9,1},{2,10},{10,2},{3,11},{11,3},{4,12},{12,4},... | collective-permute-start | bytes 786440 | tf_op jit(solution)/shard_map/ppermute | solution.py:46
  35.3 1.2 multiply_convert_fusion
  37.8 0.8 broadcast_in_dim.67
  38.6 10.0 %all-to-all-start.1 = ((bf16[8,164,128]{2,1,0:T(8,128)(2,1)}), bf16[8,164,128]{2,1,0:T(8,128)(2,1)S(1)}, u32[]{:S(2)}, u32[]{:S(2)}) async-start(bf16[8,164,128]{2,1,0:T(8,128)(2,1)} %broadcast_in_dim.67), calls=%async_computation.1 | async-start | bytes 688128 | tf_op jit(solution)/shard_map/all_to_all | solution.py:38
  49.1 16.8 %all-to-all-done.1 = bf16[8,164,128]{2,1,0:T(8,128)(2,1)S(1)} async-done(((bf16[8,164,128]{2,1,0:T(8,128)(2,1)}), bf16[8,164,128]{2,1,0:T(8,128)(2,1)S(1)}, u32[]{:S(2)}, u32[]{:S(2)}) %all-to-all-start.1) | async-done | bytes 335904 | tf_op jit(solution)/shard_map/all_to_all | solution.py:38
  68.7 3.2 %collective-permute-start.1 = (bf16[32,40,128]{2,1,0:T(8,128)(2,1)S(1)}, bf16[32,40,128]{2,1,0:T(8,128)(2,1)S(1)}, u32[]{:S(2)}, u32[]{:S(2)}) collective-permute-start(bf16[32,40,128]{2,1,0:T(8,128)(2,1)S(1)} %pad_maximum_fusion), channel_id=1, source_target_pairs={{0,8},{8,0},{1,9},{9,1},{2,10},{10,2},{3,11},{11,3},{4,12},{12,4},... | collective-permute-start | bytes 983048 | tf_op jit(solution)/shard_map/ppermute | solution.py:46
  72.0 1.1 collective-permute-done.1
  73.4 0.8 pad_maximum_fusion.1
  74.2 4.1 %all-to-all-start.2 = ((bf16[32,40,128]{2,1,0:T(8,128)(2,1)}), bf16[32,40,128]{2,1,0:T(8,128)(2,1)S(1)}, u32[]{:S(2)}, u32[]{:S(2)}) async-start(bf16[32,40,128]{2,1,0:T(8,128)(2,1)} %pad_maximum_fusion.1), calls=%async_computation.2 | async-start | bytes 655360 | tf_op jit(solution)/shard_map/all_to_all | solution.py:38
  78.4 10.4 %all-to-all-done.2 = bf16[32,40,128]{2,1,0:T(8,128)(2,1)S(1)} async-done(((bf16[32,40,128]{2,1,0:T(8,128)(2,1)}), bf16[32,40,128]{2,1,0:T(8,128)(2,1)S(1)}, u32[]{:S(2)}, u32[]{:S(2)}) %all-to-all-start.2) | async-done | bytes 327712 | tf_op jit(solution)/shard_map/all_to_all | solution.py:38
  89.0 6.2 %collective-permute-start.2 = (bf16[136,128]{1,0:T(8,128)(2,1)S(1)}, bf16[136,128]{1,0:T(8,128)(2,1)S(1)}, u32[]{:S(2)}, u32[]{:S(2)}) collective-permute-start(bf16[136,128]{1,0:T(8,128)(2,1)S(1)} %concatenate.81), channel_id=1, source_target_pairs={{0,0},{1,64},{2,128},{3,192},{4,256},{5,320},{6,384},{7,448},{8,1}... | collective-permute-start | bytes 104456 | tf_op jit(solution)/shard_map/ppermute | solution.py:133
  95.8 7.9 %all-to-all-start.3 = ((f32[64,1,128]{2,1,0:T(1,128)}), f32[64,1,128]{2,1,0:T(1,128)S(1)}, u32[]{:S(2)}, u32[]{:S(2)}) async-start(f32[64,1,128]{2,1,0:T(1,128)} %broadcast_in_dim.68), calls=%async_computation.3 | async-start | bytes 65536 | tf_op jit(solution)/shard_map/all_to_all | solution.py:38
  104.3 8.5 %all-to-all-done.3 = f32[64,1,128]{2,1,0:T(1,128)S(1)} async-done(((f32[64,1,128]{2,1,0:T(1,128)}), f32[64,1,128]{2,1,0:T(1,128)S(1)}, u32[]{:S(2)}, u32[]{:S(2)}) %all-to-all-start.3) | async-done | bytes 32800 | tf_op jit(solution)/shard_map/all_to_all | solution.py:38
  112.9 0.8 broadcast_in_dim.69
  113.7 5.4 %all-to-all-start.4 = ((bf16[8,130,128]{2,1,0:T(8,128)(2,1)}), bf16[8,130,128]{2,1,0:T(8,128)(2,1)S(1)}, u32[]{:S(2)}, u32[]{:S(2)}) async-start(bf16[8,130,128]{2,1,0:T(8,128)(2,1)} %broadcast_in_dim.69), calls=%async_computation.4 | async-start | bytes 557056 | tf_op jit(solution)/shard_map/all_to_all | solution.py:38
  119.2 13.4 %all-to-all-done.4 = bf16[8,130,128]{2,1,0:T(8,128)(2,1)S(1)} async-done(((bf16[8,130,128]{2,1,0:T(8,128)(2,1)}), bf16[8,130,128]{2,1,0:T(8,128)(2,1)S(1)}, u32[]{:S(2)}, u32[]{:S(2)}) %all-to-all-start.4) | async-done | bytes 266272 | tf_op jit(solution)/shard_map/all_to_all | solution.py:38
  135.5 6.5 %all-to-all-start.5 = ((f32[64,1,128]{2,1,0:T(1,128)}), f32[64,1,128]{2,1,0:T(1,128)S(1)}, u32[]{:S(2)}, u32[]{:S(2)}) async-start(f32[64,1,128]{2,1,0:T(1,128)} %broadcast_in_dim.72), calls=%async_computation.5 | async-start | bytes 65536 | tf_op jit(solution)/shard_map/all_to_all | solution.py:38
  142.0 5.0 %fusion.16 = f32[8,66,2048]{2,1,0:T(8,128)S(1)} fusion(bf16[8,256,2048]{2,1,0:T(8,128)(2,1)} %bitcast.102, bf16[66,256]{1,0:T(8,128)(2,1)S(1)} %fusion.29), kind=kOutput, calls=%fused_computation.45 | convolution fusion | flops 553648128 | bytes 12747776 | tf_op jit(solution)/shard_map/zsk,zkn->zsn/dot_general | solution.py:175
  147.4 3.8 %all-to-all-done.5 = f32[64,1,128]{2,1,0:T(1,128)S(1)} async-done(((f32[64,1,128]{2,1,0:T(1,128)}), f32[64,1,128]{2,1,0:T(1,128)S(1)}, u32[]{:S(2)}, u32[]{:S(2)}) %all-to-all-start.5) | async-done | bytes 32800 | tf_op jit(solution)/shard_map/all_to_all | solution.py:38
  152.8 16.7 %all_to_all.55 = bf16[64,6,128]{2,1,0:T(8,128)(2,1)S(1)} all-to-all(bf16[64,6,128]{2,1,0:T(8,128)(2,1)S(1)} %pad_maximum_fusion.2), channel_id=1, replica_groups=mesh['x'=4,'ya'=2,'yb'=2,'yc'=2,'core'=2,'z'=8] {'x','ya','yb','yc','core'}, dimensions={0} | all-to-all | bytes 196608 | tf_op jit(solution)/shard_map/all_to_all | solution.py:38
  170.3 4.6 %convolution_convert_fusion.3 = bf16[8,2,2048]{2,1,0:T(2,128)(2,1)S(1)} fusion(bf16[8,256,2048]{2,1,0:T(8,128)(2,1)} %bitcast.103, bf16[2,256]{1,0:T(2,128)(2,1)S(1)} %get-tuple-element.33), kind=kOutput, calls=%fused_computation.5 | convolution fusion | flops 16809984 | bytes 8455168 | tf_op jit(solution)/shard_map/zsk,zkn->zsn/dot_general | solution.py:175
  175.6 15.0 %all_to_all.56 = bf16[64,6,128]{2,1,0:T(8,128)(2,1)S(1)} all-to-all(bf16[64,6,128]{2,1,0:T(8,128)(2,1)S(1)} %pad_maximum_fusion.3), channel_id=1, replica_groups=mesh['x'=4,'ya'=2,'yb'=2,'yc'=2,'core'=2,'z'=8] {'x','ya','yb','yc','core'}, dimensions={0} | all-to-all | bytes 196608 | tf_op jit(solution)/shard_map/all_to_all | solution.py:38
  191.5 4.6 %convolution_convert_fusion.2 = bf16[8,2,2048]{2,1,0:T(2,128)(2,1)S(1)} fusion(bf16[8,256,2048]{2,1,0:T(8,128)(2,1)} %bitcast.104, bf16[2,256]{1,0:T(2,128)(2,1)S(1)} %get-tuple-element.31), kind=kOutput, calls=%fused_computation.4 | convolution fusion | flops 16809984 | bytes 8455168 | tf_op jit(solution)/shard_map/zsk,zkn->zsn/dot_general | solution.py:175
  196.8 15.0 %all_to_all.57 = bf16[64,6,128]{2,1,0:T(8,128)(2,1)S(1)} all-to-all(bf16[64,6,128]{2,1,0:T(8,128)(2,1)S(1)} %pad_maximum_fusion.4), channel_id=1, replica_groups=mesh['x'=4,'ya'=2,'yb'=2,'yc'=2,'core'=2,'z'=8] {'x','ya','yb','yc','core'}, dimensions={0} | all-to-all | bytes 196608 | tf_op jit(solution)/shard_map/all_to_all | solution.py:38
  213.0 15.0 %all_to_all.58 = bf16[64,5,128]{2,1,0:T(8,128)(2,1)S(1)} all-to-all(bf16[64,5,128]{2,1,0:T(8,128)(2,1)S(1)} %broadcast_in_dim.88), channel_id=1, replica_groups=mesh['x'=4,'ya'=2,'yb'=2,'yc'=2,'core'=2,'z'=8] {'x','ya','yb','yc','core'}, dimensions={0} | all-to-all | bytes 163840 | tf_op jit(solution)/shard_map/all_to_all | solution.py:38
  228.6 0.8 multiply_convert_fusion.1
  229.4 3.4 %all-to-all-start.10 = ((bf16[8,2,2048]{2,1,0:T(2,128)(2,1)}), bf16[8,2,2048]{2,1,0:T(2,128)(2,1)S(1)}, u32[]{:S(2)}, u32[]{:S(2)}) async-start(bf16[8,2,2048]{2,1,0:T(2,128)(2,1)} %multiply_convert_fusion.1), calls=%async_computation.10 | async-start | bytes 131072 | tf_op jit(solution)/shard_map/all_to_all | solution.py:38
  233.4 6.4 %all-to-all-done.10 = bf16[8,2,2048]{2,1,0:T(2,128)(2,1)S(1)} async-done(((bf16[8,2,2048]{2,1,0:T(2,128)(2,1)}), bf16[8,2,2048]{2,1,0:T(2,128)(2,1)S(1)}, u32[]{:S(2)}, u32[]{:S(2)}) %all-to-all-start.10) | async-done | bytes 65568 | tf_op jit(solution)/shard_map/all_to_all | solution.py:38
  (167 shorter events, 18.9 us)
Async XLA Ops:
  7.2 30.0 %copy-start = (bf16[128,2048]{1,0:T(8,128)(2,1)S(1)}, bf16[128,2048]{1,0:T(8,128)(2,1)}, u32[]{:S(2)}) copy-start(bf16[128,2048]{1,0:T(8,128)(2,1)} %param.11) | copy-start | bytes 1572868
  7.2 41.4 %copy-start.1 = (bf16[256,2048]{1,0:T(8,128)(2,1)S(1)}, bf16[256,2048]{1,0:T(8,128)(2,1)}, u32[]{:S(2)}) copy-start(bf16[256,2048]{1,0:T(8,128)(2,1)} %param.19) | copy-start | bytes 3145732
  7.2 134.8 %all-gather.3.cloned.1.call-start = ((), (), s32[]{:S(2)}) async-start(), calls=%async_computation.11 | async-start | bytes 9437184 | tf_op jit(solution)/shard_map/all_gather | solution.py:76
  9.5 20.2 %all-to-all-start = ((bf16[32,32,128]{2,1,0:T(8,128)(2,1)}), bf16[32,32,128]{2,1,0:T(8,128)(2,1)S(1)}, u32[]{:S(2)}, u32[]{:S(2)}) async-start(bf16[32,32,128]{2,1,0:T(8,128)(2,1)} %broadcast_in_dim.63), calls=%async_computation | async-start | bytes 524288 | tf_op jit(solution)/shard_map/all_to_all | solution.py:38
  29.7 6.8 %collective-permute-start = (bf16[32,32,128]{2,1,0:T(8,128)(2,1)S(1)}, bf16[32,32,128]{2,1,0:T(8,128)(2,1)S(1)}, u32[]{:S(2)}, u32[]{:S(2)}) collective-permute-start(bf16[32,32,128]{2,1,0:T(8,128)(2,1)S(1)} %all-to-all-done), channel_id=1, source_target_pairs={{0,8},{8,0},{1,9},{9,1},{2,10},{10,2},{3,11},{11,3},{4,12},{12,4},... | collective-permute-start | bytes 786440 | tf_op jit(solution)/shard_map/ppermute | solution.py:46
  37.2 41.2 %copy-start.3 = (f32[1,32,128]{2,1,0:T(8,128)S(1)}, f32[1,32,128]{2,1,0:T(8,128)}, u32[]{:S(2)}) copy-start(f32[1,32,128]{2,1,0:T(8,128)} %param.18) | copy-start | bytes 49156
  37.2 41.1 %copy-start.4 = (f32[1,32,128]{2,1,0:T(8,128)S(1)}, f32[1,32,128]{2,1,0:T(8,128)}, u32[]{:S(2)}) copy-start(f32[1,32,128]{2,1,0:T(8,128)} %param.17) | copy-start | bytes 49156
  38.6 27.4 %all-to-all-start.1 = ((bf16[8,164,128]{2,1,0:T(8,128)(2,1)}), bf16[8,164,128]{2,1,0:T(8,128)(2,1)S(1)}, u32[]{:S(2)}, u32[]{:S(2)}) async-start(bf16[8,164,128]{2,1,0:T(8,128)(2,1)} %broadcast_in_dim.67), calls=%async_computation.1 | async-start | bytes 688128 | tf_op jit(solution)/shard_map/all_to_all | solution.py:38
  67.2 0.6 copy-start.2
  68.7 4.5 %collective-permute-start.1 = (bf16[32,40,128]{2,1,0:T(8,128)(2,1)S(1)}, bf16[32,40,128]{2,1,0:T(8,128)(2,1)S(1)}, u32[]{:S(2)}, u32[]{:S(2)}) collective-permute-start(bf16[32,40,128]{2,1,0:T(8,128)(2,1)S(1)} %pad_maximum_fusion), channel_id=1, source_target_pairs={{0,8},{8,0},{1,9},{9,1},{2,10},{10,2},{3,11},{11,3},{4,12},{12,4},... | collective-permute-start | bytes 983048 | tf_op jit(solution)/shard_map/ppermute | solution.py:46
  74.2 14.6 %all-to-all-start.2 = ((bf16[32,40,128]{2,1,0:T(8,128)(2,1)}), bf16[32,40,128]{2,1,0:T(8,128)(2,1)S(1)}, u32[]{:S(2)}, u32[]{:S(2)}) async-start(bf16[32,40,128]{2,1,0:T(8,128)(2,1)} %pad_maximum_fusion.1), calls=%async_computation.2 | async-start | bytes 655360 | tf_op jit(solution)/shard_map/all_to_all | solution.py:38
  89.0 15.4 %collective-permute-start.2 = (bf16[136,128]{1,0:T(8,128)(2,1)S(1)}, bf16[136,128]{1,0:T(8,128)(2,1)S(1)}, u32[]{:S(2)}, u32[]{:S(2)}) collective-permute-start(bf16[136,128]{1,0:T(8,128)(2,1)S(1)} %concatenate.81), channel_id=1, source_target_pairs={{0,0},{1,64},{2,128},{3,192},{4,256},{5,320},{6,384},{7,448},{8,1}... | collective-permute-start | bytes 104456 | tf_op jit(solution)/shard_map/ppermute | solution.py:133
  95.8 17.1 %all-to-all-start.3 = ((f32[64,1,128]{2,1,0:T(1,128)}), f32[64,1,128]{2,1,0:T(1,128)S(1)}, u32[]{:S(2)}, u32[]{:S(2)}) async-start(f32[64,1,128]{2,1,0:T(1,128)} %broadcast_in_dim.68), calls=%async_computation.3 | async-start | bytes 65536 | tf_op jit(solution)/shard_map/all_to_all | solution.py:38
  113.7 19.0 %all-to-all-start.4 = ((bf16[8,130,128]{2,1,0:T(8,128)(2,1)}), bf16[8,130,128]{2,1,0:T(8,128)(2,1)S(1)}, u32[]{:S(2)}, u32[]{:S(2)}) async-start(bf16[8,130,128]{2,1,0:T(8,128)(2,1)} %broadcast_in_dim.69), calls=%async_computation.4 | async-start | bytes 557056 | tf_op jit(solution)/shard_map/all_to_all | solution.py:38
  135.5 15.7 %all-to-all-start.5 = ((f32[64,1,128]{2,1,0:T(1,128)}), f32[64,1,128]{2,1,0:T(1,128)S(1)}, u32[]{:S(2)}, u32[]{:S(2)}) async-start(f32[64,1,128]{2,1,0:T(1,128)} %broadcast_in_dim.72), calls=%async_computation.5 | async-start | bytes 65536 | tf_op jit(solution)/shard_map/all_to_all | solution.py:38
  174.9 57.8 %copy-start.5 = (f32[1,32,128]{2,1,0:T(8,128)S(1)}, f32[1,32,128]{2,1,0:T(8,128)}, u32[]{:S(2)}) copy-start(f32[1,32,128]{2,1,0:T(8,128)} %param.16) | copy-start | bytes 49156
  229.4 10.4 %all-to-all-start.10 = ((bf16[8,2,2048]{2,1,0:T(2,128)(2,1)}), bf16[8,2,2048]{2,1,0:T(2,128)(2,1)S(1)}, u32[]{:S(2)}, u32[]{:S(2)}) async-start(bf16[8,2,2048]{2,1,0:T(2,128)(2,1)} %multiply_convert_fusion.1), calls=%async_computation.10 | async-start | bytes 131072 | tf_op jit(solution)/shard_map/all_to_all | solution.py:38
Sparse Core Ops, SparseCore 0:
  10.1 113.4 all-gather.2
